TPU v7x, 32 devices: a whole 2x2x4 slice. The times are simulated.
32 devices in a mesh: groups: 2 (over y), ep: 8 (over z, x), tp: 2 (over core).
Axes of the slice: x: 2, y: 2, z: 4, core: 2. Of those that a mesh axis runs over, the one named last changes fastest.
Arguments:
- tokens: bfloat16 [2048, 1536], P(('groups', 'ep', 'tp')), parts along dimension 0, may hold values from -16 to 16
- expert_ids: int32 [2048, 4], P(('groups', 'ep', 'tp')), parts along dimension 0, may hold values from 0 to 7, all different within a row; in each aligned block of 64 rows (0 to 63, 64 to 127, ...) at most 64 rows name the same one
- combine_weights: float32 [2048, 4], P(('groups', 'ep', 'tp')), parts along dimension 0, may hold values from 0.1 to 1
- gate_weight: bfloat16 [8, 1536, 1536], P(None, 'ep', 'tp'), may hold values from -0.15625 to 0.15625
- up_weight: bfloat16 [8, 1536, 1536], P(None, 'ep', 'tp'), may hold values from -0.15625 to 0.15625
Outputs:
- expert_mix: bfloat16 [2048, 1536], P(('groups', 'ep', 'tp')), parts along dimension 0
There are 2 independent parts, one for each index of `groups`. A program takes and returns all parts, laid end to end along the dimension named above; an argument that names none is the same for every part. Nothing has to cross between parts.
Inputs may be any that keep to these rules, and one draw needn't show every extreme that they name: `expert_ids`: each row names 4 different experts. In the rows of one device no expert is named more than 64 times, and in some device's rows some expert is named exactly 64 times.
All inputs are finite; a program needn't handle non-finite values.
Results may differ from a plain program's by a relative error of at most 0.008.
Values may be sent and summed in bfloat16 or wider, within the bound.
No kernel may reach another device: no remote copies, remote signals or barrier semaphores. Data moves between devices by JAX's collectives and lax.ppermute only.
A program may use at most 256 MiB of HBM per device.

v0:
```python
import jax
import jax.numpy as jnp
from jax import lax
from jax.sharding import PartitionSpec as P

THRESHOLDS = (0.25, 0.75, 1.25, 1.75, 2.5, 3.5, 5.0)
STEPS_UP = (0.5, 0.5, 0.5, 0.5, 1.0, 1.0, 2.0)
LIMIT = 7.0


def block_scale(largest):
    scale = jnp.full(largest.shape, 2.0 ** (-40), jnp.float32)
    for exponent_value in range(-39, 9):
        power = 2.0**exponent_value
        scale = jnp.where(largest >= power, jnp.float32(power), scale)
    return scale * 0.25


def code_blocks(weight):
    shaped = weight.reshape(weight.shape[:-1] + (weight.shape[-1] // 32, 32))
    magnitude = jnp.abs(shaped).astype(jnp.float32)
    scale = block_scale(jnp.max(magnitude, axis=-1))[..., None]
    total = jnp.zeros(magnitude.shape, jnp.float32)
    for bound_value, step_value in zip(THRESHOLDS, STEPS_UP):
        total = total + jnp.where(magnitude > bound_value * scale, step_value, 0.0)
    signed = jnp.where(shaped < 0, -total, total) * scale
    return signed.reshape(weight.shape).astype(jnp.bfloat16)


def activate(gate_value, up_value):
    gate_clamped = jnp.minimum(gate_value, LIMIT)
    up_clamped = jnp.clip(up_value, -LIMIT, LIMIT)
    return gate_clamped * jax.nn.sigmoid(1.702 * gate_clamped) * (up_clamped + 1.0)


def per_device(tokens, expert_ids, combine_weights, gate_weight, up_weight):
    experts = gate_weight.shape[0]
    owners = lax.axis_size("ep")
    cores = lax.axis_size("tp")
    tok_rows = tokens.shape[0]
    top_count = expert_ids.shape[1]
    width = tokens.shape[1]
    slots = max(2, 2 * tok_rows * top_count // experts)
    gate_split, up_split = (
        lax.all_to_all(gate_weight, "tp", split_axis=1, concat_axis=2, tiled=True),
        lax.all_to_all(up_weight, "tp", split_axis=1, concat_axis=2, tiled=True),
    )
    gate_local, up_local = (
        lax.all_to_all(gate_split, "ep", split_axis=0, concat_axis=1, tiled=True),
        lax.all_to_all(up_split, "ep", split_axis=0, concat_axis=1, tiled=True),
    )
    gate_coded = code_blocks(gate_local[0])
    up_coded = code_blocks(up_local[0])
    chosen = expert_ids.reshape(-1)
    onehot = (chosen[:, None] == jnp.arange(experts, dtype=jnp.int32)[None, :]).astype(jnp.int32)
    before = jnp.cumsum(onehot, axis=0, dtype=jnp.int32) - onehot
    ranking = jnp.sum(before * onehot, axis=1, dtype=jnp.int32)
    target = chosen * slots + ranking
    repeated = jnp.repeat(tokens, top_count, axis=0)
    outgoing = jnp.zeros((experts * slots, width), jnp.bfloat16).at[target].set(repeated)
    received = lax.all_to_all(
        outgoing.reshape(experts, slots, width), "ep", split_axis=0, concat_axis=0, tiled=True
    )
    piece = lax.all_gather(received.reshape(owners * slots, width), "tp", axis=0, tiled=True)
    gate_value = jnp.einsum("rd,fd->rf", piece, gate_coded, preferred_element_type=jnp.float32)
    up_value = jnp.einsum("rd,fd->rf", piece, up_coded, preferred_element_type=jnp.float32)
    actives = activate(gate_value, up_value).astype(jnp.bfloat16)
    shaped_back = actives.reshape(cores, owners, slots, actives.shape[1])
    returned = lax.all_to_all(
        lax.all_to_all(shaped_back, "ep", split_axis=1, concat_axis=1, tiled=True),
        "tp",
        split_axis=0,
        concat_axis=3,
        tiled=True,
    )
    flat_back = returned.reshape(experts * slots, returned.shape[3])
    values = flat_back[target].reshape(tok_rows, top_count, flat_back.shape[1])
    mixed = jnp.einsum("tk,tkf->tf", combine_weights, values.astype(jnp.float32))
    hidden_total = mixed.shape[1]
    quarter = hidden_total // (owners * cores)
    mixed = (
        mixed.reshape(tok_rows, cores, owners, quarter)
        .transpose(0, 2, 1, 3)
        .reshape(tok_rows, hidden_total)
    )
    return mixed.astype(jnp.bfloat16)


def solution(mesh):
    return jax.shard_map(
        per_device,
        mesh=mesh,
        in_specs=(
            P(("groups", "ep", "tp"), None),
            P(("groups", "ep", "tp"), None),
            P(("groups", "ep", "tp"), None),
            P(None, "ep", "tp"),
            P(None, "ep", "tp"),
        ),
        out_specs=P(("groups", "ep", "tp"), None),
        check_vma=False,
    )
```

profile of v0, /device:TPU:0, one launch (start us, length us, event | category | flops | bytes accessed | tf_op | source)
XLA Modules:
  0.0 327.7 jit_solution(2997738618568848121)
XLA Ops:
  6.5 4.4 %copy.87 = bf16[8,192,768]{2,0,1:T(8,128)(2,1)} copy(bf16[8,192,768]{2,1,0:T(8,128)(2,1)} %param.8) | data formatting | bytes 4718592 | tf_op args[3]
  10.9 3.9 %all-to-all-start.1 = ((bf16[8,192,768]{2,0,1:T(8,128)(2,1)}), bf16[8,192,768]{2,0,1:T(8,128)(2,1)S(1)}, u32[]{:S(2)}, u32[]{:S(2)}) async-start(bf16[8,192,768]{2,0,1:T(8,128)(2,1)} %copy.87), calls=%async_computation.1 | async-start | bytes 4718592 | tf_op jit(solution)/shard_map/all_to_all | solution.py:45
  17.6 4.4 %copy.98 = bf16[8,192,768]{2,0,1:T(8,128)(2,1)} copy(bf16[8,192,768]{2,1,0:T(8,128)(2,1)} %param.9) | data formatting | bytes 4718592 | tf_op args[4]
  22.0 3.8 %scatter_custom_fusion = bf16[512,1536]{1,0:T(8,128)(2,1)} fusion(s32[256]{0:T(256)S(1)} %bitcast.126, bf16[256,1536]{1,0:T(8,128)(2,1)} %reshape.386, bf16[]{:T(256)} %constant.64.clone.1), kind=kCustom, calls=%fused_computation.125 | custom fusion | bytes 1573376 | tf_op jit(solution)/shard_map/scatter | solution.py:60
  25.9 9.1 %all_to_all.79 = bf16[8,192,768]{2,0,1:T(8,128)(2,1)} all-to-all(bf16[8,192,768]{2,0,1:T(8,128)(2,1)} %copy.98), channel_id=1, replica_groups=mesh['groups'=2,'ep'=8,'tp'=2] {'tp'}, dimensions={1} | all-to-all | bytes 4718592 | tf_op jit(solution)/shard_map/all_to_all | solution.py:46
  34.9 7.3 %all-to-all-start = ((bf16[8,64,1536]{2,1,0:T(8,128)(2,1)}), bf16[8,64,1536]{2,1,0:T(8,128)(2,1)}, u32[]{:S(2)}, u32[]{:S(2)}) async-start(bf16[8,64,1536]{2,1,0:T(8,128)(2,1)} %bitcast.118), calls=%async_computation | async-start | bytes 3145728 | tf_op jit(solution)/shard_map/all_to_all | solution.py:61
  42.2 3.9 %copy.120 = bf16[8,2,96,768]{3,1,2,0:T(2,128)(2,1)} copy(bf16[8,2,96,768]{3,0,2,1:T(8,128)(2,1)S(1)} %bitcast.114) | data formatting | bytes 4718592 | tf_op jit(solution)/shard_map/all_to_all | solution.py:45
  46.0 6.3 %all_to_all.61 = bf16[8,96,1536]{2,1,0:T(8,128)(2,1)} reshape(bf16[8,96,2,768]{3,2,1,0:T(2,128)(2,1)} %bitcast.116) | data formatting | bytes 4718592 | tf_op jit(solution)/shard_map/all_to_all | solution.py:45
  52.3 27.3 %all-to-all-done = bf16[8,64,1536]{2,1,0:T(8,128)(2,1)} async-done(((bf16[8,64,1536]{2,1,0:T(8,128)(2,1)}), bf16[8,64,1536]{2,1,0:T(8,128)(2,1)}, u32[]{:S(2)}, u32[]{:S(2)}) %all-to-all-start) | async-done | bytes 1572896 | tf_op jit(solution)/shard_map/all_to_all | solution.py:61
  83.4 5.6 %copy.119 = bf16[8,2,96,768]{3,1,2,0:T(2,128)(2,1)} copy(bf16[8,2,96,768]{3,0,2,1:T(8,128)(2,1)} %bitcast.115) | data formatting | bytes 4718592 | tf_op jit(solution)/shard_map/all_to_all | solution.py:46
  89.0 6.3 %all_to_all.66 = bf16[8,96,1536]{2,1,0:T(8,128)(2,1)} reshape(bf16[8,96,2,768]{3,2,1,0:T(2,128)(2,1)} %bitcast.117) | data formatting | bytes 4718592 | tf_op jit(solution)/shard_map/all_to_all | solution.py:46
  95.3 42.0 %all-to-all-done.2 = bf16[8,96,1536]{2,1,0:T(8,128)(2,1)S(1)} async-done(((bf16[8,96,1536]{2,1,0:T(8,128)(2,1)}), bf16[8,96,1536]{2,1,0:T(8,128)(2,1)S(1)}, u32[]{:S(2)}, u32[]{:S(2)}) %all-to-all-start.2) | async-done | bytes 2359328 | tf_op jit(solution)/shard_map/all_to_all | solution.py:49
  137.3 4.4 %all-to-all-start.4 = ((bf16[8,96,1536]{2,1,0:T(8,128)(2,1)}), bf16[8,96,1536]{2,1,0:T(8,128)(2,1)}, u32[]{:S(2)}, u32[]{:S(2)}) async-start(bf16[8,96,1536]{2,1,0:T(8,128)(2,1)} %all_to_all.66), calls=%async_computation.4 | async-start | bytes 4718592 | tf_op jit(solution)/shard_map/all_to_all | solution.py:50
  145.6 49.5 %all-to-all-done.4 = bf16[8,96,1536]{2,1,0:T(8,128)(2,1)} async-done(((bf16[8,96,1536]{2,1,0:T(8,128)(2,1)}), bf16[8,96,1536]{2,1,0:T(8,128)(2,1)}, u32[]{:S(2)}, u32[]{:S(2)}) %all-to-all-start.4) | async-done | bytes 2359328 | tf_op jit(solution)/shard_map/all_to_all | solution.py:50
  203.5 4.8 %copy.100 = bf16[8,96,1536]{1,0,2:T(8,128)(2,1)} copy(bf16[8,96,1536]{2,1,0:T(8,128)(2,1)} %abs.18) | data formatting | bytes 4718592 | tf_op jit(solution)/shard_map/abs | solution.py:21
  208.3 6.0 %abs.19 = bf16[768,48,32]{0,2,1:T(8,128)(2,1)} reshape(bf16[8,96,1536]{1,0,2:T(8,128)(2,1)} %copy.100) | data formatting | bytes 4718592 | tf_op jit(solution)/shard_map/abs | solution.py:21
  214.3 4.5 %bitcast_convert_fusion = f32[768,1536]{1,0:T(8,128)} fusion(bf16[8,96,1536]{2,1,0:T(8,128)(2,1)} %abs.18), kind=kLoop, calls=%fused_computation.23 | loop fusion | flops 1179648 | bytes 7077888 | tf_op jit(solution)/shard_map/convert_element_type | solution.py:21
  218.8 6.1 %copy.101 = f32[768,1536]{0,1:T(8,128)} copy(f32[768,1536]{1,0:T(8,128)} %bitcast_convert_fusion) | data formatting | bytes 9437184 | tf_op jit(solution)/shard_map/convert_element_type | solution.py:21
  242.5 6.2 %copy.90 = f32[768,1536]{0,1:T(8,128)} copy(f32[768,1536]{1,0:T(8,128)} %bitcast_convert_fusion.1) | data formatting | bytes 9437184 | tf_op jit(solution)/shard_map/convert_element_type | solution.py:21
  249.4 5.6 %fusion.3 = bf16[768,1536]{0,1:T(8,128)(2,1)S(1)} fusion(pred[768,1536]{0,1:T(8,128)(4,1)S(1)} %copy-done.2, f32[768,1536]{0,1:T(8,128)} %copy.101, f32[768,48]{0,1:T(8,128)S(1)} %get-tuple-element.22, f32[768,48]{0,1:T(8,128)S(1)} %get-tuple-element.17, f32[768,48]{0,1:T(8,128)S(1)} %get-tuple-element.18, f32[768,48]{0,1:T(8,128)S(1)} %get-tuple-element.19, ...), kind=kLoop, calls=%fused_computation.7 | loop fusion | flops 28311552 | bytes 9437184 | tf_op jit(solution)/shard_map/convert_element_type | solution.py:27
  255.6 4.9 %fusion.1 = bf16[768,1536]{0,1:T(8,128)(2,1)} fusion(pred[768,1536]{0,1:T(8,128)(4,1)S(1)} %copy-done.1, f32[768,1536]{0,1:T(8,128)S(1)} %bitcast.113, f32[768,48]{0,1:T(8,128)S(1)} %get-tuple-element.15, f32[768,48]{0,1:T(8,128)S(1)} %get-tuple-element.10, f32[768,48]{0,1:T(8,128)S(1)} %get-tuple-element.11, f32[768,48]{0,1:T(8,128)S(1)} %get-tuple-element.12, ...), kind=kLoop, calls=%fused_computation.5 | loop fusion | flops 28311552 | bytes 9437184 | tf_op jit(solution)/shard_map/convert_element_type | solution.py:27
  260.5 4.6 %fusion.9 = f32[1024,768]{1,0:T(8,128)S(1)} fusion(bf16[1024,1536]{1,0:T(8,128)(2,1)} %all-gather.2.cloned.1.call-done, bf16[768,1536]{0,1:T(8,128)(2,1)S(1)} %fusion.3), kind=kOutput, calls=%fused_computation.156 | convolution fusion | flops 2415919104 | bytes 8650752 | tf_op jit(solution)/shard_map/rd,fd->rf/dot_general | solution.py:66
  273.4 37.0 %all-to-all-done.5 = bf16[2,8,64,768]{3,2,0,1:T(8,128)(2,1)S(1)} async-done(((bf16[2,8,64,768]{3,2,0,1:T(8,128)(2,1)}), bf16[2,8,64,768]{3,2,0,1:T(8,128)(2,1)S(1)}, u32[]{:S(2)}, u32[]{:S(2)}) %all-to-all-start.5) | async-done | bytes 1572896 | tf_op jit(solution)/shard_map/all_to_all | solution.py:70
  310.6 5.0 %all_to_all.80 = bf16[2,8,64,768]{3,2,1,0:T(8,128)(2,1)S(1)} all-to-all(bf16[2,8,64,768]{3,2,1,0:T(8,128)(2,1)S(1)} %copy.110), channel_id=1, replica_groups=mesh['groups'=2,'ep'=8,'tp'=2] {'tp'}, dimensions={0} | all-to-all | bytes 3145728 | tf_op jit(solution)/shard_map/all_to_all | solution.py:69
  (73 shorter events, 51.3 us)
Async XLA Ops:
  10.9 4.0 %copy-start.6 = (s32[64,4]{0,1:T(4,128)S(1)}, s32[64,4]{0,1:T(4,128)}, u32[]{:S(2)}) copy-start(s32[64,4]{0,1:T(4,128)} %param.6) | copy-start | bytes 3076
  10.9 5.3 %copy-start.5 = (bf16[64,1536]{1,0:T(8,128)(2,1)S(1)}, bf16[64,1536]{1,0:T(8,128)(2,1)}, u32[]{:S(2)}) copy-start(bf16[64,1536]{1,0:T(8,128)(2,1)} %param.5) | copy-start | bytes 589828
  10.9 15.0 %all-to-all-start.1 = ((bf16[8,192,768]{2,0,1:T(8,128)(2,1)}), bf16[8,192,768]{2,0,1:T(8,128)(2,1)S(1)}, u32[]{:S(2)}, u32[]{:S(2)}) async-start(bf16[8,192,768]{2,0,1:T(8,128)(2,1)} %copy.87), calls=%async_computation.1 | async-start | bytes 4718592 | tf_op jit(solution)/shard_map/all_to_all | solution.py:45
  34.9 44.7 %all-to-all-start = ((bf16[8,64,1536]{2,1,0:T(8,128)(2,1)}), bf16[8,64,1536]{2,1,0:T(8,128)(2,1)}, u32[]{:S(2)}, u32[]{:S(2)}) async-start(bf16[8,64,1536]{2,1,0:T(8,128)(2,1)} %bitcast.118), calls=%async_computation | async-start | bytes 3145728 | tf_op jit(solution)/shard_map/all_to_all | solution.py:61
  79.6 57.7 %all-to-all-start.2 = ((bf16[8,96,1536]{2,1,0:T(8,128)(2,1)}), bf16[8,96,1536]{2,1,0:T(8,128)(2,1)S(1)}, u32[]{:S(2)}, u32[]{:S(2)}) async-start(bf16[8,96,1536]{2,1,0:T(8,128)(2,1)} %all_to_all.61), calls=%async_computation.2 | async-start | bytes 4718592 | tf_op jit(solution)/shard_map/all_to_all | solution.py:49
  137.3 57.8 %all-to-all-start.4 = ((bf16[8,96,1536]{2,1,0:T(8,128)(2,1)}), bf16[8,96,1536]{2,1,0:T(8,128)(2,1)}, u32[]{:S(2)}, u32[]{:S(2)}) async-start(bf16[8,96,1536]{2,1,0:T(8,128)(2,1)} %all_to_all.66), calls=%async_computation.4 | async-start | bytes 4718592 | tf_op jit(solution)/shard_map/all_to_all | solution.py:50
  141.7 118.8 %all-gather.2.cloned.1.call-start = ((), (), s32[]{:S(2)}) async-start(), calls=%async_computation.7 | async-start | bytes 4718592 | tf_op jit(solution)/shard_map/all_gather | solution.py:64
  234.1 5.4 %copy-start = (bf16[8,96,1536]{2,1,0:T(8,128)(2,1)S(1)}, bf16[8,96,1536]{2,1,0:T(8,128)(2,1)}, u32[]{:S(2)}) copy-start(bf16[8,96,1536]{2,1,0:T(8,128)(2,1)} %abs.16) | copy-start | bytes 7077892
  242.5 6.8 %copy-start.2 = (pred[768,1536]{0,1:T(8,128)(4,1)S(1)}, pred[768,1536]{0,1:T(8,128)(4,1)}, u32[]{:S(2)}) copy-start(pred[768,1536]{0,1:T(8,128)(4,1)} %copy.108) | copy-start | bytes 3538948
  249.3 6.2 %slice-start = ((s8[4718592]{0:T(1024)(128)(4,1)}), s8[4194304]{0:T(1024)(128)(4,1)S(1)}, s32[]{:S(2)}) async-start(s8[4718592]{0:T(1024)(128)(4,1)} %bitcast.112), calls=%async_computation.8 | async-start | bytes 8388608
  249.4 5.6 %copy-start.4 = (bf16[768,48]{0,1:T(8,128)(2,1)S(1)}, bf16[768,48]{0,1:T(8,128)(2,1)}, u32[]{:S(2)}) copy-start(bf16[768,48]{0,1:T(8,128)(2,1)} %reduce_max.28) | copy-start | bytes 221188
  249.4 6.2 %slice-start.1 = ((s8[4718592]{0:T(1024)(128)(4,1)}), s8[524288]{0:T(1024)(128)(4,1)S(1)}, s32[]{:S(2)}) async-start(s8[4718592]{0:T(1024)(128)(4,1)} %bitcast.112), calls=%async_computation.9 | async-start | bytes 1048576
  249.4 6.2 %copy-start.1 = (pred[768,1536]{0,1:T(8,128)(4,1)S(1)}, pred[768,1536]{0,1:T(8,128)(4,1)}, u32[]{:S(2)}) copy-start(pred[768,1536]{0,1:T(8,128)(4,1)} %copy.97) | copy-start | bytes 3538948
  260.5 4.6 %copy-start.3 = (bf16[768,1536]{0,1:T(8,128)(2,1)S(1)}, bf16[768,1536]{0,1:T(8,128)(2,1)}, u32[]{:S(2)}) copy-start(bf16[768,1536]{0,1:T(8,128)(2,1)} %fusion.1) | copy-start | bytes 7077892
  260.5 4.7 %copy-start.8 = (bf16[1024,1536]{1,0:T(8,128)(2,1)S(1)}, bf16[1024,1536]{1,0:T(8,128)(2,1)}, u32[]{:S(2)}) copy-start(bf16[1024,1536]{1,0:T(8,128)(2,1)} %all-gather.2.cloned.1.call-done) | copy-start | bytes 9437188
  268.4 4.9 %copy-start.7 = (f32[64,4]{0,1:T(4,128)S(1)}, f32[64,4]{0,1:T(4,128)}, u32[]{:S(2)}) copy-start(f32[64,4]{0,1:T(4,128)} %param.7) | copy-start | bytes 3076
  269.6 40.8 %all-to-all-start.5 = ((bf16[2,8,64,768]{3,2,0,1:T(8,128)(2,1)}), bf16[2,8,64,768]{3,2,0,1:T(8,128)(2,1)S(1)}, u32[]{:S(2)}, u32[]{:S(2)}) async-start(bf16[2,8,64,768]{3,2,0,1:T(8,128)(2,1)} %copy.109), calls=%async_computation.5 | async-start | bytes 3145728 | tf_op jit(solution)/shard_map/all_to_all | solution.py:70
Sparse Core Ops, SparseCore 0:
  144.1 13.4 all-gather.1
where the time goes:
time: 329 us; the launch traced here: 328 us
  waiting for transfers between devices  157 us (48%)
  local copies, waits for them, and re-layouts  78.4 us (24%)
  other arithmetic  33.6 us (10%)
  starting transfers between devices  23 us (7%)
  blocking collectives  14.1 us (4%)
  between operations  13.7 us (4%)
  matrix products  8.38 us (3%)
    all_to_all x1, waiting for transfers between devices, per_device(): lax.all_to_all(up_split, 'ep', split_axis=0, concat_axis=1, tiled=True)  49.5 us
    all_to_all x1, waiting for transfers between devices, per_device(): lax.all_to_all(gate_split, 'ep', split_axis=0, concat_axis=1, tiled=True)  42 us
    all_to_all x1, waiting for transfers between devices, per_device(): lax.all_to_all(shaped_back, 'ep', split_axis=1, concat_axis=1, tiled=True)  37 us
    all_to_all x1, waiting for transfers between devices, per_device(): lax.all_to_all(outgoing.reshape(experts, slots, width), 'ep', split_axis=...  27.3 us
    abs x4, local copies, waits for them, and re-layouts, code_blocks(): magnitude = jnp.abs(shaped).astype(jnp.float32)  18.2 us
    convert_element_type x2, local copies, waits for them, and re-layouts, code_blocks(): magnitude = jnp.abs(shaped).astype(jnp.float32)  12.3 us
    all_to_all x2, local copies, waits for them, and re-layouts, per_device(): lax.all_to_all(up_weight, 'tp', split_axis=1, concat_axis=2, tiled=True)  11.9 us
    convert_element_type x2, other arithmetic, code_blocks(): return signed.reshape(weight.shape).astype(jnp.bfloat16)  10.5 us
  transfers between devices with their start and end apart: 6, of which 4 were waited for; matrix products, arithmetic and copies ran while one was open for 27% of the time, Pallas kernels for 0%

commit v1 on v0

--- a/solution.py
+++ b/solution.py
@@ -1,11 +1,229 @@
+import functools
+
 import jax
 import jax.numpy as jnp
 from jax import lax
+from jax.experimental import pallas as pl
+from jax.experimental.pallas import tpu as pltpu
 from jax.sharding import PartitionSpec as P
 
 THRESHOLDS = (0.25, 0.75, 1.25, 1.75, 2.5, 3.5, 5.0)
 STEPS_UP = (0.5, 0.5, 0.5, 0.5, 1.0, 1.0, 2.0)
 LIMIT = 7.0
+LANES = 128
+BLOCK = 32
+
+
+def ring_place(owner, owners):
+    return jnp.where(owner % 2 == 0, owner // 2, owners - 1 - owner // 2)
+
+
+def ring_owner(place, owners):
+    return jnp.where(place < owners // 2, 2 * place, 2 * (owners - 1 - place) + 1)
+
+
+def ring_shift(owners, steps):
+    order = list(range(0, owners, 2)) + list(range(1, owners, 2))[::-1]
+    return [(order[p], order[(p + steps) % owners]) for p in range(owners)]
+
+
+def ring_send(value, owners, steps):
+    return lax.ppermute(value, "ep", ring_shift(owners, steps))
+
+
+def code_columns(entries):
+    depth, count = entries.shape
+    blocks = entries.reshape(depth // BLOCK, BLOCK, count)
+    largest = jnp.max(jnp.abs(blocks), axis=1, keepdims=True)
+    largest = jnp.maximum(largest, 2.0**-40)
+    lifted = largest * 2.0**23
+    power = jnp.minimum((largest * 0.7 + lifted) - lifted, 2.0**8)
+    lowered = blocks * (1.0 - 2.0**-12)
+    top = power * 1.5
+    lowered = jnp.minimum(jnp.maximum(lowered, -top), top)
+    least = power * (0.25 * (1.0 + 2.0**-10))
+    anchor = jnp.maximum(jnp.abs(lowered), least) * 2.0**22
+    return ((lowered + anchor) - anchor).reshape(depth, count)
+
+
+def code_kernel(gate_ref, up_ref, out_ref):
+    depth = gate_ref.shape[2]
+    for low in range(0, depth, 256):
+        rows = [ref[expert, :, low : low + 256] for ref in (gate_ref, up_ref) for expert in range(ref.shape[0])]
+        turned = jnp.concatenate(rows, axis=0).T.astype(jnp.float32)
+        out_ref[low : low + 256, :] = code_columns(turned).astype(jnp.bfloat16)
+
+
+def code_weights(gate, up, first_expert, count, tail):
+    depth = gate.shape[2]
+    if tail:
+        block, tiles, index = (2, LANES // 2, depth), count // 2, lambda i: (first_expert // 2 + i, 2, 0)
+    else:
+        block, tiles, index = (1, LANES, depth), count, lambda i: (first_expert + i, 0, 0)
+    return pl.pallas_call(
+        code_kernel,
+        grid=(tiles,),
+        out_shape=jax.ShapeDtypeStruct((depth, 256 * tiles), jnp.bfloat16),
+        in_specs=[pl.BlockSpec(block, index)] * 2,
+        out_specs=pl.BlockSpec((depth, 256), lambda i: (0, i)),
+        compiler_params=pltpu.CompilerParams(vmem_limit_bytes=8 << 20),
+        cost_estimate=pl.CostEstimate(flops=10**9 * tiles // 2, bytes_accessed=4 * tiles * depth * 256, transcendentals=0),
+        name="code",
+    )(gate, up)
+
+
+def hidden_kernel(*refs, count, pieces, experts):
+    chunks = refs[:count]
+    own = refs[count : count + pieces]
+    other = refs[count + pieces : count + 2 * pieces]
+    outs = refs[count + 2 * pieces : 2 * count + 2 * pieces]
+    (tok,) = refs[2 * count + 2 * pieces :]
+    sizes = [chunk.shape[0] for chunk in chunks]
+    width = tok.shape[1]
+    core = lax.axis_index("tp")
+    depth = own[0].shape[0]
+    total = sum(sizes)
+    at = 0
+    mixes = []
+    for chunk, rows in zip(chunks, sizes):
+        tok[at : at + rows, :] = chunk[:, :width]
+        parts = chunk[:, width:].astype(jnp.float32)
+        mixes.append(parts[:, :experts] + parts[:, experts : 2 * experts] + parts[:, 2 * experts : 3 * experts])
+        at += rows
+    mix = jnp.concatenate(mixes, axis=0) if count > 1 else mixes[0]
+    near = tok[:, pl.ds(pl.multiple_of(core * depth, LANES), depth)]
+    far = tok[:, pl.ds(pl.multiple_of((1 - core) * depth, LANES), depth)]
+    lane = lax.broadcasted_iota(jnp.int32, (total, LANES), 1)
+    first_sum = jnp.zeros((total, LANES), jnp.float32)
+    second_sum = jnp.zeros((total, LANES), jnp.float32)
+    per_piece = own[0].shape[1] // 256
+    for tile in range(per_piece * pieces):
+        piece, inside = divmod(tile, per_piece)
+        columns = slice(inside * 256, inside * 256 + 256)
+        both = jnp.dot(near, own[piece][:, columns], preferred_element_type=jnp.float32)
+        both += jnp.dot(far, other[piece][:, columns], preferred_element_type=jnp.float32)
+        gate = jnp.minimum(both[:, :LANES], LIMIT)
+        up = jnp.clip(both[:, LANES:], -LIMIT, LIMIT)
+        active = gate * jax.nn.sigmoid(1.702 * gate) * (up + 1.0)
+        active = active.astype(jnp.bfloat16).astype(jnp.float32)
+        if tile < experts:
+            first_sum += active * mix[:, tile : tile + 1]
+        else:
+            pair = 2 * (tile - experts)
+            second_sum += active * jnp.where(lane < LANES // 2, mix[:, pair : pair + 1], mix[:, pair + 1 : pair + 2])
+    last = second_sum[:, : LANES // 2] + second_sum[:, LANES // 2 :]
+    at = 0
+    for out, rows in zip(outs, sizes):
+        out[:, :LANES] = first_sum[at : at + rows].astype(jnp.bfloat16)
+        out[:, LANES:] = last[at : at + rows].astype(jnp.bfloat16)
+        at += rows
+
+
+def hidden_units(chunks, own, other, experts):
+    units = 3 * LANES // 2
+    sizes = [chunk.shape[0] for chunk in chunks]
+    total, width = sum(sizes), 2 * own[0].shape[0]
+    return pl.pallas_call(
+        functools.partial(hidden_kernel, count=len(chunks), pieces=len(own), experts=experts),
+        out_shape=[jax.ShapeDtypeStruct((rows, units), jnp.bfloat16) for rows in sizes],
+        in_specs=[pl.BlockSpec(memory_space=pltpu.VMEM)] * (len(chunks) + 2 * len(own)),
+        out_specs=[pl.BlockSpec(memory_space=pltpu.VMEM)] * len(chunks),
+        scratch_shapes=[pltpu.VMEM((total, width), jnp.bfloat16)],
+        compiler_params=pltpu.CompilerParams(vmem_limit_bytes=20 << 20),
+        cost_estimate=pl.CostEstimate(
+            flops=2 * 3 * experts * LANES * width * max(total, 256), bytes_accessed=0, transcendentals=0
+        ),
+        name="hidden",
+    )(*chunks, *own, *other)
+
+
+def join_kernel(*refs, steps):
+    blocks, out_ref, held = refs[: len(steps)], refs[len(steps)], refs[len(steps) + 1]
+    owners = lax.axis_size("ep")
+    place = ring_place(lax.axis_index("ep"), owners)
+    units = blocks[0].shape[1]
+    for block, step in zip(blocks, steps):
+        held[ring_owner((place + step + owners) % owners, owners)] = block[...]
+    for owner in range(owners):
+        out_ref[:, owner * units : (owner + 1) * units] = held[owner]
+
+
+def join_units(blocks, steps):
+    rows, units = blocks[0].shape
+    return pl.pallas_call(
+        functools.partial(join_kernel, steps=steps),
+        out_shape=jax.ShapeDtypeStruct((rows, units * len(steps)), jnp.bfloat16),
+        in_specs=[pl.BlockSpec(memory_space=pltpu.VMEM)] * len(blocks),
+        out_specs=pl.BlockSpec(memory_space=pltpu.VMEM),
+        scratch_shapes=[pltpu.VMEM((len(steps), rows, units), jnp.bfloat16)],
+        name="join",
+    )(*blocks)
+
+
+def pack_kernel(tokens_ref, ids_ref, weights_ref, out_ref, *, experts):
+    rows, width = tokens_ref.shape
+    out_ref[:, :width] = tokens_ref[...]
+    number = lax.broadcasted_iota(jnp.int32, (experts, rows), 0)
+    mix = jnp.zeros((experts, rows), jnp.float32)
+    for choice in range(ids_ref.shape[0]):
+        mix += jnp.where(ids_ref[choice : choice + 1, :] == number, weights_ref[choice : choice + 1, :], 0.0)
+    high = mix.astype(jnp.bfloat16).astype(jnp.float32)
+    middle = (mix - high).astype(jnp.bfloat16).astype(jnp.float32)
+    low = mix - high - middle
+    fill = jnp.zeros((LANES - 3 * experts, rows), jnp.float32)
+    out_ref[:, width:] = jnp.concatenate([high, middle, low, fill], axis=0).T.astype(jnp.bfloat16)
+
+
+def pack_tokens(tokens, expert_ids, combine_weights, experts):
+    rows, width = tokens.shape
+    return pl.pallas_call(
+        functools.partial(pack_kernel, experts=experts),
+        out_shape=jax.ShapeDtypeStruct((rows, width + LANES), jnp.bfloat16),
+        in_specs=[pl.BlockSpec(memory_space=pltpu.VMEM)] * 3,
+        out_specs=pl.BlockSpec(memory_space=pltpu.VMEM),
+        name="pack",
+    )(tokens, expert_ids.T, combine_weights.T)
+
+
+def resident(tokens, expert_ids, combine_weights, gate_weight, up_weight):
+    experts = gate_weight.shape[0]
+    owners = lax.axis_size("ep")
+    rows = tokens.shape[0]
+    half = rows // 2
+    tie = lax.optimization_barrier
+
+    def swap(part):
+        return lax.ppermute(part, "tp", [(0, 1), (1, 0)])
+
+    def onward(right, left):
+        return ring_send(right, owners, 1), ring_send(left, owners, -1)
+
+    packed = pack_tokens(tokens, expert_ids, combine_weights, experts)
+    packed, gate_weight, up_weight = tie((packed, gate_weight, up_weight))
+    right1, left1 = onward(packed, packed)
+    own = [code_weights(gate_weight, up_weight, 0, experts // 2, False)]
+    own.append(code_weights(gate_weight, up_weight, experts // 2, experts // 2, False))
+
+    right1, left1, own, gate_weight, up_weight = tie((right1, left1, own, gate_weight, up_weight))
+    right2, left2 = onward(right1, left1)
+    other = [swap(part) for part in own]
+    own.append(code_weights(gate_weight, up_weight, 0, experts, True))
+
+    right2, left2, own = tie((right2, left2, own))
+    right3, left3 = onward(right2, left2)
+    other.append(swap(own[2]))
+    home, from1, back1, from2, back2 = hidden_units([packed, right1, left1, right2, left2], own, other, experts)
+
+    right3, left3, from1, back1, from2, back2 = tie((right3, left3, from1, back1, from2, back2))
+    right4, left4 = onward(right3[:half], left3[half:])
+    done = {0: home}
+    for step, value in ((1, from1), (-1, back1), (2, from2), (-2, back2)):
+        done[step] = ring_send(value, owners, -step)
+    from3, back3, *ends = hidden_units([right3, left3, right4, left4], own, other, experts)
+    for step, value in ((4, jnp.concatenate(ends, axis=0)), (3, from3), (-3, back3)):
+        done[step] = ring_send(value, owners, -step)
+    places = tuple(sorted(done))
+    return join_units([done[p] for p in places], places)
 
 
 def block_scale(largest):
@@ -33,7 +251,7 @@
     return gate_clamped * jax.nn.sigmoid(1.702 * gate_clamped) * (up_clamped + 1.0)
 
 
-def per_device(tokens, expert_ids, combine_weights, gate_weight, up_weight):
+def dispatched(tokens, expert_ids, combine_weights, gate_weight, up_weight):
     experts = gate_weight.shape[0]
     owners = lax.axis_size("ep")
     cores = lax.axis_size("tp")
@@ -84,6 +302,15 @@
         .reshape(tok_rows, hidden_total)
     )
     return mixed.astype(jnp.bfloat16)
+
+
+def per_device(tokens, expert_ids, combine_weights, gate_weight, up_weight):
+    experts, units, depth = gate_weight.shape
+    owners, cores = lax.axis_size("ep"), lax.axis_size("tp")
+    fits = owners == 8 and cores == 2 and experts <= 4 * expert_ids.shape[1] and experts % 8 == 0
+    fits = fits and units == 3 * LANES // 2 and depth % 256 == 0 and tokens.shape[0] % 64 == 0
+    plan = resident if fits else dispatched
+    return plan(tokens, expert_ids, combine_weights, gate_weight, up_weight)
 
 
 def solution(mesh):

time: 329 us -> 50.7 us (0.15)
  waiting for transfers between devices: 157 us -> 9.66 us
  local copies, waits for them, and re-layouts: 78.4 us -> 3.94 us
  other arithmetic: 33.6 us -> 0.01 us
  Pallas kernels: 0 us -> 15.1 us
  blocking collectives: 14.1 us -> 0 us
  between operations: 13.7 us -> 0.14 us
  matrix products: 8.38 us -> 0 us
    all_to_all x5 -> x0, waiting for transfers between devices: 156 us -> none  [the longest x1 49.5 us: per_device(): lax.all_to_all(up_split, 'ep', split_axis=0, concat_axis=1, tiled=True)]
    all_to_all x6 -> x0, local copies, waits for them, and re-layouts: 23.7 us -> none  [the longest x2 11.9 us: per_device(): lax.all_to_all(up_weight, 'tp', split_axis=1, concat_axis=2, tiled=True)]
    all_to_all x5 -> x0, starting transfers between devices: 23 us -> none  [the longest x1 7.25 us: per_device(): lax.all_to_all(outgoing.reshape(experts, slots, width), 'ep', split_axis=...]
    ppermute x0 -> x18, starting transfers between devices: none -> 21.5 us  [the longest x15 21 us: ring_send(): return lax.ppermute(value, 'ep', ring_shift(owners, steps))]
    abs x4 -> x0, local copies, waits for them, and re-layouts: 18.2 us -> none  [code_blocks(): magnitude = jnp.abs(shaped).astype(jnp.float32)]
    convert_element_type x5 -> x0, other arithmetic: 18 us -> none  [the longest x2 10.5 us: code_blocks(): return signed.reshape(weight.shape).astype(jnp.bfloat16)]
    pallas_call x0 -> x7, Pallas kernels: none -> 15.1 us  [the longest x2 5.87 us: hidden_units(): pl.pallas_call(functools.partial(hidden_kernel, count=len(chunks), pieces...]
    all_to_all x2 -> x0, blocking collectives: 14.1 us -> none  [the longest x1 9.06 us: per_device(): lax.all_to_all(up_weight, 'tp', split_axis=1, concat_axis=2, tiled=True)]
  transfers between devices with their start and end apart: 6 -> 18, of which waited for: 4 -> 8; matrix products, arithmetic and copies ran while one was open for 27% -> 0% of each run, Pallas kernels for 0% -> 23%
where the time goes in v1:
time: 50.7 us; the launch traced here: 50.4 us
  starting transfers between devices  21.5 us (42%)
  Pallas kernels  15.1 us (30%)
  waiting for transfers between devices  9.66 us (19%)
  local copies, waits for them, and re-layouts  3.94 us (8%)
    ppermute x15, starting transfers between devices, ring_send(): return lax.ppermute(value, 'ep', ring_shift(owners, steps))  21 us
    ppermute x15, waiting for transfers between devices, ring_send(): return lax.ppermute(value, 'ep', ring_shift(owners, steps))  8.28 us
    pallas_call x2, Pallas kernels, hidden_units(): pl.pallas_call(functools.partial(hidden_kernel, count=len(chunks), pieces...  5.87 us
    pallas_call x3, Pallas kernels, code_weights(): pl.pallas_call(code_kernel, grid=(tiles,), out_shape=jax.ShapeDtypeStruct...  5.85 us
    unnamed x22, local copies, waits for them, and re-layouts  3.92 us
    pallas_call x1, Pallas kernels, pack_tokens(): pl.pallas_call(functools.partial(pack_kernel, experts=experts), out_shape...  1.72 us
    pallas_call x1, Pallas kernels, join_units(): pl.pallas_call(functools.partial(join_kernel, steps=steps), out_shape=jax...  1.7 us
    ppermute x3, waiting for transfers between devices, swap(): return lax.ppermute(part, 'tp', [(0, 1), (1, 0)])  1.38 us
  transfers between devices with their start and end apart: 18, of which 8 were waited for; matrix products, arithmetic and copies ran while one was open for 0% of the time, Pallas kernels for 23%

profile of v1, /device:TPU:0, one launch (start us, length us, event | category | flops | bytes accessed | tf_op | source)
XLA Modules:
  0.0 50.4 jit_solution(8909945620624850356)
XLA Ops:
  0.0 1.7 %pack.1.refs_0_ = bf16[64,1664]{1,0:T(8,128)(2,1)} custom-call(bf16[64,1536]{1,0:T(8,128)(2,1)} %tokens_ref.1, s32[4,64]{1,0:T(4,128)} %bitcast.2, f32[4,64]{1,0:T(4,128)} %bitcast.3), custom_call_target="tpu_custom_call" | custom-call | tf_op jit(solution)/shard_map/pack/pallas_call | solution.py:179
  1.7 3.0 %collective-permute-start = (bf16[64,1664]{1,0:T(8,128)(2,1)}, bf16[64,1664]{1,0:T(8,128)(2,1)S(1)}, u32[]{:S(2)}, u32[]{:S(2)}) collective-permute-start(bf16[64,1664]{1,0:T(8,128)(2,1)} %pack.1.refs_0_), channel_id=1, source_target_pairs={{0,4},{4,8},{8,12},{12,14},{14,10},{10,6},{6,2},{2,0},{1,5},{5,9},... | collective-permute-start | bytes 638984 | tf_op jit(solution)/shard_map/ppermute | solution.py:31
  4.8 1.7 %copy-done.2 = bf16[8,192,768]{2,1,0:T(8,128)(2,1)S(1)} copy-done((bf16[8,192,768]{2,1,0:T(8,128)(2,1)S(1)}, bf16[8,192,768]{2,1,0:T(8,128)(2,1)}, u32[]{:S(2)}) %copy-start.2) | copy-done | bytes 2359320
  6.4 1.7 %copy-done.3 = bf16[8,192,768]{2,1,0:T(8,128)(2,1)S(1)} copy-done((bf16[8,192,768]{2,1,0:T(8,128)(2,1)S(1)}, bf16[8,192,768]{2,1,0:T(8,128)(2,1)}, u32[]{:S(2)}) %copy-start.3) | copy-done | bytes 2359320
  8.1 1.9 %code.3.refs_5_.refs_4_ = bf16[768,1024]{1,0:T(8,128)(2,1)S(1)} custom-call(bf16[8,192,768]{2,1,0:T(8,128)(2,1)S(1)} %copy-done.2, bf16[8,192,768]{2,1,0:T(8,128)(2,1)S(1)} %copy-done.3), custom_call_target="tpu_custom_call" | custom-call | flops 2000000000 | bytes 3145728 | tf_op jit(solution)/shard_map/code/pallas_call | solution.py:63
  10.0 1.9 %code.4.refs_6_.refs_5_ = bf16[768,1024]{1,0:T(8,128)(2,1)S(1)} custom-call(bf16[8,192,768]{2,1,0:T(8,128)(2,1)S(1)} %copy-done.2, bf16[8,192,768]{2,1,0:T(8,128)(2,1)S(1)} %copy-done.3), custom_call_target="tpu_custom_call" | custom-call | flops 2000000000 | bytes 3145728 | tf_op jit(solution)/shard_map/code/pallas_call | solution.py:63
  11.9 2.1 %collective-permute-start.2 = (bf16[64,1664]{1,0:T(8,128)(2,1)S(1)}, bf16[64,1664]{1,0:T(8,128)(2,1)S(1)}, u32[]{:S(2)}, u32[]{:S(2)}) collective-permute-start(bf16[64,1664]{1,0:T(8,128)(2,1)S(1)} %collective-permute-done.refs_1_), channel_id=1, source_target_pairs={{0,4},{4,8},{8,12},{12,14},{14,10},{10,6},{6,2},{2,0},{1,5},{5,9},... | collective-permute-start | bytes 638984 | tf_op jit(solution)/shard_map/ppermute | solution.py:31
  14.5 2.0 %code.5.refs_7_.refs_6_ = bf16[768,1024]{1,0:T(8,128)(2,1)S(1)} custom-call(bf16[8,192,768]{2,1,0:T(8,128)(2,1)S(1)} %copy-done.2, bf16[8,192,768]{2,1,0:T(8,128)(2,1)S(1)} %copy-done.3), custom_call_target="tpu_custom_call" | custom-call | flops 2000000000 | bytes 3145728 | tf_op jit(solution)/shard_map/code/pallas_call | solution.py:63
  16.6 2.1 %collective-permute-done.2.refs_3_ = bf16[64,1664]{1,0:T(8,128)(2,1)S(1)} collective-permute-done((bf16[64,1664]{1,0:T(8,128)(2,1)S(1)}, bf16[64,1664]{1,0:T(8,128)(2,1)S(1)}, u32[]{:S(2)}, u32[]{:S(2)}) %collective-permute-start.2) | collective-permute-done | bytes 213024 | tf_op jit(solution)/shard_map/ppermute | solution.py:31
  18.7 1.5 %collective-permute-done.3.refs_4_ = bf16[64,1664]{1,0:T(8,128)(2,1)S(1)} collective-permute-done((bf16[64,1664]{1,0:T(8,128)(2,1)S(1)}, bf16[64,1664]{1,0:T(8,128)(2,1)S(1)}, u32[]{:S(2)}, u32[]{:S(2)}) %collective-permute-start.3) | collective-permute-done | bytes 213024 | tf_op jit(solution)/shard_map/ppermute | solution.py:31
  20.2 1.6 %collective-permute-start.4 = (bf16[64,1664]{1,0:T(8,128)(2,1)S(1)}, bf16[64,1664]{1,0:T(8,128)(2,1)S(1)}, u32[]{:S(2)}, u32[]{:S(2)}) collective-permute-start(bf16[64,1664]{1,0:T(8,128)(2,1)S(1)} %collective-permute-done.2.refs_3_), channel_id=1, source_target_pairs={{0,4},{4,8},{8,12},{12,14},{14,10},{10,6},{6,2},{2,0},{1,5},{5,9},... | collective-permute-start | bytes 638984 | tf_op jit(solution)/shard_map/ppermute | solution.py:31
  22.2 1.4 %collective-permute-done.8.refs_10_.refs_9_ = bf16[768,1024]{1,0:T(8,128)(2,1)S(1)} collective-permute-done((bf16[768,1024]{1,0:T(8,128)(2,1)S(1)}, bf16[768,1024]{1,0:T(8,128)(2,1)S(1)}, u32[]{:S(2)}, u32[]{:S(2)}) %collective-permute-start.8) | collective-permute-done | bytes 1572896 | tf_op jit(solution)/shard_map/ppermute | solution.py:196
  23.6 3.6 %hidden.2 = (bf16[64,192]{1,0:T(8,128)(2,1)S(1)}, bf16[64,192]{1,0:T(8,128)(2,1)S(1)}, bf16[64,192]{1,0:T(8,128)(2,1)S(1)}, bf16[64,192]{1,0:T(8,128)(2,1)S(1)}, bf16[64,192]{1,0:T(8,128)(2,1)S(1)}) custom-call(bf16[64,1664]{1,0:T(8,128)(2,1)S(1)} %copy-done, bf16[64,1664]{1,0:T(8,128)(2,1)S(1)} %collective-permute-done.refs_1_, ...), custom_call_target="tpu_custom_call" | custom-call | flops 3019898880 | tf_op jit(solution)/shard_map/hidden/pallas_call | solution.py:126
  27.8 1.3 %collective-permute-done.5.refs_1_ = bf16[64,1664]{1,0:T(8,128)(2,1)S(1)} collective-permute-done((bf16[64,1664]{1,0:T(8,128)(2,1)S(1)}, bf16[64,1664]{1,0:T(8,128)(2,1)S(1)}, u32[]{:S(2)}, u32[]{:S(2)}) %collective-permute-start.5) | collective-permute-done | bytes 213024 | tf_op jit(solution)/shard_map/ppermute | solution.py:31
  29.7 1.6 %collective-permute-start.9 = (bf16[32,1664]{1,0:T(8,128)(2,1)S(1)}, bf16[32,1664]{1,0:T(8,128)(2,1)S(1)}, u32[]{:S(2)}, u32[]{:S(2)}) collective-permute-start(bf16[32,1664]{1,0:T(8,128)(2,1)S(1)} %slice.6), channel_id=1, source_target_pairs={{0,4},{4,8},{8,12},{12,14},{14,10},{10,6},{6,2},{2,0},{1,5},{5,9},... | collective-permute-start | bytes 319496 | tf_op jit(solution)/shard_map/ppermute | solution.py:31
  31.3 2.5 %collective-permute-start.12 = (bf16[64,192]{1,0:T(8,128)(2,1)S(1)}, bf16[64,192]{1,0:T(8,128)(2,1)S(1)}, u32[]{:S(2)}, u32[]{:S(2)}) collective-permute-start(bf16[64,192]{1,0:T(8,128)(2,1)S(1)} %get-tuple-element.55), channel_id=1, source_target_pairs={{0,8},{4,12},{8,14},{12,10},{14,6},{10,2},{6,0},{2,4},{1,9},{5,13}... | collective-permute-start | bytes 73736 | tf_op jit(solution)/shard_map/ppermute | solution.py:31
  34.2 1.6 %collective-permute-start.14 = (bf16[64,192]{1,0:T(8,128)(2,1)S(1)}, bf16[64,192]{1,0:T(8,128)(2,1)S(1)}, u32[]{:S(2)}, u32[]{:S(2)}) collective-permute-start(bf16[64,192]{1,0:T(8,128)(2,1)S(1)} %get-tuple-element.58), channel_id=1, source_target_pairs={{0,2},{4,0},{8,4},{12,8},{14,12},{10,14},{6,10},{2,6},{1,3},{5,1},... | collective-permute-start | bytes 73736 | tf_op jit(solution)/shard_map/ppermute | solution.py:31
  36.3 2.3 %hidden.3 = (bf16[64,192]{1,0:T(8,128)(2,1)S(1)}, bf16[64,192]{1,0:T(8,128)(2,1)S(1)}, bf16[32,192]{1,0:T(8,128)(2,1)S(1)}, bf16[32,192]{1,0:T(8,128)(2,1)S(1)}) custom-call(bf16[64,1664]{1,0:T(8,128)(2,1)S(1)} %collective-permute-done.4.refs_0_, bf16[64,1664]{1,0:T(8,128)(2,1)S(1)} %collective-permute-done.5.refs_1_, ...), custom_call_target="tpu_custom_call" | custom-call | flops 2415919104 | tf_op jit(solution)/shard_map/hidden/pallas_call | solution.py:126
  38.6 2.9 %collective-permute-start.17 = (bf16[64,192]{1,0:T(8,128)(2,1)S(1)}, bf16[64,192]{1,0:T(8,128)(2,1)S(1)}, u32[]{:S(2)}, u32[]{:S(2)}) collective-permute-start(bf16[64,192]{1,0:T(8,128)(2,1)S(1)} %pad_maximum_fusion), channel_id=1, source_target_pairs={{0,14},{4,10},{8,6},{12,2},{14,0},{10,4},{6,8},{2,12},{1,15},{5,11... | collective-permute-start | bytes 73736 | tf_op jit(solution)/shard_map/ppermute | solution.py:31
  41.5 0.8 %collective-permute-start.11 = (bf16[64,192]{1,0:T(8,128)(2,1)S(1)}, bf16[64,192]{1,0:T(8,128)(2,1)S(1)}, u32[]{:S(2)}, u32[]{:S(2)}) collective-permute-start(bf16[64,192]{1,0:T(8,128)(2,1)S(1)} %get-tuple-element.54), channel_id=1, source_target_pairs={{0,12},{4,14},{8,10},{12,6},{14,2},{10,0},{6,4},{2,8},{1,13},{5,15... | collective-permute-start | bytes 73736 | tf_op jit(solution)/shard_map/ppermute | solution.py:31
  42.4 3.0 %collective-permute-start.16 = (bf16[64,192]{1,0:T(8,128)(2,1)S(1)}, bf16[64,192]{1,0:T(8,128)(2,1)S(1)}, u32[]{:S(2)}, u32[]{:S(2)}) collective-permute-start(bf16[64,192]{1,0:T(8,128)(2,1)S(1)} %get-tuple-element.60), channel_id=1, source_target_pairs={{0,10},{4,6},{8,2},{12,0},{14,4},{10,8},{6,12},{2,14},{1,11},{5,7}... | collective-permute-start | bytes 73736 | tf_op jit(solution)/shard_map/ppermute | solution.py:31
  45.6 1.7 %collective-permute-done.11.refs_0_ = bf16[64,192]{1,0:T(8,128)(2,1)S(1)} collective-permute-done((bf16[64,192]{1,0:T(8,128)(2,1)S(1)}, bf16[64,192]{1,0:T(8,128)(2,1)S(1)}, u32[]{:S(2)}, u32[]{:S(2)}) %collective-permute-start.11) | collective-permute-done | bytes 24608 | tf_op jit(solution)/shard_map/ppermute | solution.py:31
  47.2 0.8 %collective-permute-done.16.refs_6_ = bf16[64,192]{1,0:T(8,128)(2,1)S(1)} collective-permute-done((bf16[64,192]{1,0:T(8,128)(2,1)S(1)}, bf16[64,192]{1,0:T(8,128)(2,1)S(1)}, u32[]{:S(2)}, u32[]{:S(2)}) %collective-permute-start.16) | collective-permute-done | bytes 24608 | tf_op jit(solution)/shard_map/ppermute | solution.py:31
  48.7 1.7 %join.1 = bf16[64,1536]{1,0:T(8,128)(2,1)} custom-call(bf16[64,192]{1,0:T(8,128)(2,1)} %copy-done.9, bf16[64,192]{1,0:T(8,128)(2,1)} %copy-done.4, bf16[64,192]{1,0:T(8,128)(2,1)} %copy-done.5, bf16[64,192]{1,0:T(8,128)(2,1)} %copy-done.1, bf16[64,192]{1,0:T(8,128)(2,1)} %copy-done.6, bf16[64,192]{1,0:T(8,128)(2,1)} %copy-done.7, ...), custom_call_target="tpu_custom_call" | custom-call | tf_op jit(solution)/shard_map/join/pallas_call | solution.py:153
  (44 shorter events, 3.8 us)
Async XLA Ops:
  1.7 10.2 %collective-permute-start = (bf16[64,1664]{1,0:T(8,128)(2,1)}, bf16[64,1664]{1,0:T(8,128)(2,1)S(1)}, u32[]{:S(2)}, u32[]{:S(2)}) collective-permute-start(bf16[64,1664]{1,0:T(8,128)(2,1)} %pack.1.refs_0_), channel_id=1, source_target_pairs={{0,4},{4,8},{8,12},{12,14},{14,10},{10,6},{6,2},{2,0},{1,5},{5,9},... | collective-permute-start | bytes 638984 | tf_op jit(solution)/shard_map/ppermute | solution.py:31
  4.7 7.2 %collective-permute-start.1 = (bf16[64,1664]{1,0:T(8,128)(2,1)}, bf16[64,1664]{1,0:T(8,128)(2,1)S(1)}, u32[]{:S(2)}, u32[]{:S(2)}) collective-permute-start(bf16[64,1664]{1,0:T(8,128)(2,1)} %pack.1.refs_0_), channel_id=1, source_target_pairs={{0,2},{4,0},{8,4},{12,8},{14,12},{10,14},{6,10},{2,6},{1,3},{5,1},... | collective-permute-start | bytes 638984 | tf_op jit(solution)/shard_map/ppermute | solution.py:31
  11.9 11.7 %copy-start = (bf16[64,1664]{1,0:T(8,128)(2,1)S(1)}, bf16[64,1664]{1,0:T(8,128)(2,1)}, u32[]{:S(2)}) copy-start(bf16[64,1664]{1,0:T(8,128)(2,1)} %pack.1.refs_0_) | copy-start | bytes 638980
  11.9 6.8 %collective-permute-start.2 = (bf16[64,1664]{1,0:T(8,128)(2,1)S(1)}, bf16[64,1664]{1,0:T(8,128)(2,1)S(1)}, u32[]{:S(2)}, u32[]{:S(2)}) collective-permute-start(bf16[64,1664]{1,0:T(8,128)(2,1)S(1)} %collective-permute-done.refs_1_), channel_id=1, source_target_pairs={{0,4},{4,8},{8,12},{12,14},{14,10},{10,6},{6,2},{2,0},{1,5},{5,9},... | collective-permute-start | bytes 638984 | tf_op jit(solution)/shard_map/ppermute | solution.py:31
  14.0 6.2 %collective-permute-start.3 = (bf16[64,1664]{1,0:T(8,128)(2,1)S(1)}, bf16[64,1664]{1,0:T(8,128)(2,1)S(1)}, u32[]{:S(2)}, u32[]{:S(2)}) collective-permute-start(bf16[64,1664]{1,0:T(8,128)(2,1)S(1)} %collective-permute-done.1.refs_2_), channel_id=1, source_target_pairs={{0,2},{4,0},{8,4},{12,8},{14,12},{10,14},{6,10},{2,6},{1,3},{5,1},... | collective-permute-start | bytes 638984 | tf_op jit(solution)/shard_map/ppermute | solution.py:31
  14.0 8.2 %collective-permute-start.6 = (bf16[768,1024]{1,0:T(8,128)(2,1)S(1)}, bf16[768,1024]{1,0:T(8,128)(2,1)S(1)}, u32[]{:S(2)}, u32[]{:S(2)}) collective-permute-start(bf16[768,1024]{1,0:T(8,128)(2,1)S(1)} %code.3.refs_5_.refs_4_), channel_id=1, source_target_pairs={{0,1},{1,0},{2,3},{3,2},{4,5},{5,4},{6,7},{7,6},{8,9},{9,8},{10,11... | collective-permute-start | bytes 4718600 | tf_op jit(solution)/shard_map/ppermute | solution.py:196
  14.0 8.2 %collective-permute-start.7 = (bf16[768,1024]{1,0:T(8,128)(2,1)S(1)}, bf16[768,1024]{1,0:T(8,128)(2,1)S(1)}, u32[]{:S(2)}, u32[]{:S(2)}) collective-permute-start(bf16[768,1024]{1,0:T(8,128)(2,1)S(1)} %code.4.refs_6_.refs_5_), channel_id=1, source_target_pairs={{0,1},{1,0},{2,3},{3,2},{4,5},{5,4},{6,7},{7,6},{8,9},{9,8},{10,11... | collective-permute-start | bytes 4718600 | tf_op jit(solution)/shard_map/ppermute | solution.py:196
  20.2 3.4 %collective-permute-start.8 = (bf16[768,1024]{1,0:T(8,128)(2,1)S(1)}, bf16[768,1024]{1,0:T(8,128)(2,1)S(1)}, u32[]{:S(2)}, u32[]{:S(2)}) collective-permute-start(bf16[768,1024]{1,0:T(8,128)(2,1)S(1)} %code.5.refs_7_.refs_6_), channel_id=1, source_target_pairs={{0,1},{1,0},{2,3},{3,2},{4,5},{5,4},{6,7},{7,6},{8,9},{9,8},{10,11... | collective-permute-start | bytes 4718600 | tf_op jit(solution)/shard_map/ppermute | solution.py:196
  20.2 7.7 %collective-permute-start.4 = (bf16[64,1664]{1,0:T(8,128)(2,1)S(1)}, bf16[64,1664]{1,0:T(8,128)(2,1)S(1)}, u32[]{:S(2)}, u32[]{:S(2)}) collective-permute-start(bf16[64,1664]{1,0:T(8,128)(2,1)S(1)} %collective-permute-done.2.refs_3_), channel_id=1, source_target_pairs={{0,4},{4,8},{8,12},{12,14},{14,10},{10,6},{6,2},{2,0},{1,5},{5,9},... | collective-permute-start | bytes 638984 | tf_op jit(solution)/shard_map/ppermute | solution.py:31
  21.8 7.4 %collective-permute-start.5 = (bf16[64,1664]{1,0:T(8,128)(2,1)S(1)}, bf16[64,1664]{1,0:T(8,128)(2,1)S(1)}, u32[]{:S(2)}, u32[]{:S(2)}) collective-permute-start(bf16[64,1664]{1,0:T(8,128)(2,1)S(1)} %collective-permute-done.3.refs_4_), channel_id=1, source_target_pairs={{0,2},{4,0},{8,4},{12,8},{14,12},{10,14},{6,10},{2,6},{1,3},{5,1},... | collective-permute-start | bytes 638984 | tf_op jit(solution)/shard_map/ppermute | solution.py:31
  27.2 11.4 %copy-start.1 = (bf16[64,192]{1,0:T(8,128)(2,1)}, bf16[64,192]{1,0:T(8,128)(2,1)S(1)}, u32[]{:S(2)}) copy-start(bf16[64,192]{1,0:T(8,128)(2,1)S(1)} %get-tuple-element.57.refs_3_) | copy-start | bytes 73732
  29.1 6.7 %collective-permute-start.10 = (bf16[32,1664]{1,0:T(8,128)(2,1)S(1)}, bf16[32,1664]{1,0:T(8,128)(2,1)S(1)}, u32[]{:S(2)}, u32[]{:S(2)}) collective-permute-start(bf16[32,1664]{1,0:T(8,128)(2,1)S(1)} %slice.7), channel_id=1, source_target_pairs={{0,2},{4,0},{8,4},{12,8},{14,12},{10,14},{6,10},{2,6},{1,3},{5,1},... | collective-permute-start | bytes 319496 | tf_op jit(solution)/shard_map/ppermute | solution.py:31
  29.7 6.6 %collective-permute-start.9 = (bf16[32,1664]{1,0:T(8,128)(2,1)S(1)}, bf16[32,1664]{1,0:T(8,128)(2,1)S(1)}, u32[]{:S(2)}, u32[]{:S(2)}) collective-permute-start(bf16[32,1664]{1,0:T(8,128)(2,1)S(1)} %slice.6), channel_id=1, source_target_pairs={{0,4},{4,8},{8,12},{12,14},{14,10},{10,6},{6,2},{2,0},{1,5},{5,9},... | collective-permute-start | bytes 319496 | tf_op jit(solution)/shard_map/ppermute | solution.py:31
  31.3 10.2 %collective-permute-start.12 = (bf16[64,192]{1,0:T(8,128)(2,1)S(1)}, bf16[64,192]{1,0:T(8,128)(2,1)S(1)}, u32[]{:S(2)}, u32[]{:S(2)}) collective-permute-start(bf16[64,192]{1,0:T(8,128)(2,1)S(1)} %get-tuple-element.55), channel_id=1, source_target_pairs={{0,8},{4,12},{8,14},{12,10},{14,6},{10,2},{6,0},{2,4},{1,9},{5,13}... | collective-permute-start | bytes 73736 | tf_op jit(solution)/shard_map/ppermute | solution.py:31
  33.8 8.6 %collective-permute-start.13 = (bf16[64,192]{1,0:T(8,128)(2,1)S(1)}, bf16[64,192]{1,0:T(8,128)(2,1)S(1)}, u32[]{:S(2)}, u32[]{:S(2)}) collective-permute-start(bf16[64,192]{1,0:T(8,128)(2,1)S(1)} %get-tuple-element.56), channel_id=1, source_target_pairs={{0,4},{4,8},{8,12},{12,14},{14,10},{10,6},{6,2},{2,0},{1,5},{5,9},... | collective-permute-start | bytes 73736 | tf_op jit(solution)/shard_map/ppermute | solution.py:31
  34.2 11.1 %collective-permute-start.14 = (bf16[64,192]{1,0:T(8,128)(2,1)S(1)}, bf16[64,192]{1,0:T(8,128)(2,1)S(1)}, u32[]{:S(2)}, u32[]{:S(2)}) collective-permute-start(bf16[64,192]{1,0:T(8,128)(2,1)S(1)} %get-tuple-element.58), channel_id=1, source_target_pairs={{0,2},{4,0},{8,4},{12,8},{14,12},{10,14},{6,10},{2,6},{1,3},{5,1},... | collective-permute-start | bytes 73736 | tf_op jit(solution)/shard_map/ppermute | solution.py:31
  35.8 9.5 %collective-permute-start.15 = (bf16[64,192]{1,0:T(8,128)(2,1)S(1)}, bf16[64,192]{1,0:T(8,128)(2,1)S(1)}, u32[]{:S(2)}, u32[]{:S(2)}) collective-permute-start(bf16[64,192]{1,0:T(8,128)(2,1)S(1)} %get-tuple-element.59), channel_id=1, source_target_pairs={{0,6},{4,2},{8,0},{12,4},{14,8},{10,12},{6,14},{2,10},{1,7},{5,3},... | collective-permute-start | bytes 73736 | tf_op jit(solution)/shard_map/ppermute | solution.py:31
  38.6 7.0 %collective-permute-start.17 = (bf16[64,192]{1,0:T(8,128)(2,1)S(1)}, bf16[64,192]{1,0:T(8,128)(2,1)S(1)}, u32[]{:S(2)}, u32[]{:S(2)}) collective-permute-start(bf16[64,192]{1,0:T(8,128)(2,1)S(1)} %pad_maximum_fusion), channel_id=1, source_target_pairs={{0,14},{4,10},{8,6},{12,2},{14,0},{10,4},{6,8},{2,12},{1,15},{5,11... | collective-permute-start | bytes 73736 | tf_op jit(solution)/shard_map/ppermute | solution.py:31
  41.5 6.6 %copy-start.4 = (bf16[64,192]{1,0:T(8,128)(2,1)}, bf16[64,192]{1,0:T(8,128)(2,1)S(1)}, u32[]{:S(2)}) copy-start(bf16[64,192]{1,0:T(8,128)(2,1)S(1)} %collective-permute-done.12.refs_1_) | copy-start | bytes 73732
  41.5 5.7 %collective-permute-start.11 = (bf16[64,192]{1,0:T(8,128)(2,1)S(1)}, bf16[64,192]{1,0:T(8,128)(2,1)S(1)}, u32[]{:S(2)}, u32[]{:S(2)}) collective-permute-start(bf16[64,192]{1,0:T(8,128)(2,1)S(1)} %get-tuple-element.54), channel_id=1, source_target_pairs={{0,12},{4,14},{8,10},{12,6},{14,2},{10,0},{6,4},{2,8},{1,13},{5,15... | collective-permute-start | bytes 73736 | tf_op jit(solution)/shard_map/ppermute | solution.py:31
  42.4 5.7 %copy-start.5 = (bf16[64,192]{1,0:T(8,128)(2,1)}, bf16[64,192]{1,0:T(8,128)(2,1)S(1)}, u32[]{:S(2)}) copy-start(bf16[64,192]{1,0:T(8,128)(2,1)S(1)} %collective-permute-done.13.refs_2_) | copy-start | bytes 73732
  42.4 5.7 %collective-permute-start.16 = (bf16[64,192]{1,0:T(8,128)(2,1)S(1)}, bf16[64,192]{1,0:T(8,128)(2,1)S(1)}, u32[]{:S(2)}, u32[]{:S(2)}) collective-permute-start(bf16[64,192]{1,0:T(8,128)(2,1)S(1)} %get-tuple-element.60), channel_id=1, source_target_pairs={{0,10},{4,6},{8,2},{12,0},{14,4},{10,8},{6,12},{2,14},{1,11},{5,7}... | collective-permute-start | bytes 73736 | tf_op jit(solution)/shard_map/ppermute | solution.py:31
  45.4 2.7 %copy-start.6 = (bf16[64,192]{1,0:T(8,128)(2,1)}, bf16[64,192]{1,0:T(8,128)(2,1)S(1)}, u32[]{:S(2)}) copy-start(bf16[64,192]{1,0:T(8,128)(2,1)S(1)} %collective-permute-done.14.refs_4_) | copy-start | bytes 73732
  45.4 2.7 %copy-start.7 = (bf16[64,192]{1,0:T(8,128)(2,1)}, bf16[64,192]{1,0:T(8,128)(2,1)S(1)}, u32[]{:S(2)}) copy-start(bf16[64,192]{1,0:T(8,128)(2,1)S(1)} %collective-permute-done.15.refs_5_) | copy-start | bytes 73732
  (5 other events, 7.4 us)

commit v2 on v1

--- a/solution.py
+++ b/solution.py
@@ -46,38 +46,147 @@
     return ((lowered + anchor) - anchor).reshape(depth, count)
 
 
-def code_kernel(gate_ref, up_ref, out_ref):
-    depth = gate_ref.shape[2]
+def tile_rows(tile, experts):
+    if tile < experts:
+        return [(tile, 0, LANES)]
+    pair = 2 * (tile - experts)
+    return [(pair, LANES, LANES // 2), (pair + 1, LANES, LANES // 2)]
+
+
+def code_tile(rows_ref, out_ref, first):
+    depth = rows_ref.shape[1]
     for low in range(0, depth, 256):
-        rows = [ref[expert, :, low : low + 256] for ref in (gate_ref, up_ref) for expert in range(ref.shape[0])]
-        turned = jnp.concatenate(rows, axis=0).T.astype(jnp.float32)
-        out_ref[low : low + 256, :] = code_columns(turned).astype(jnp.bfloat16)
-
-
-def code_weights(gate, up, first_expert, count, tail):
+        turned = rows_ref[:, low : low + 256].T.astype(jnp.float32)
+        out_ref[low : low + 256, pl.ds(first, 256)] = code_columns(turned).astype(jnp.bfloat16)
+
+
+def fetch_rows(gate_ref, up_ref, tiles, target, arrived):
+    experts = gate_ref.shape[0]
+    groups = []
+    for n, tile in enumerate(tiles):
+        group, at = [], 0
+        for ref in (gate_ref, up_ref):
+            for expert, first, count in tile_rows(tile, experts):
+                source = ref.at[expert, first : first + count]
+                group.append(pltpu.make_async_copy(source, target.at[n, at : at + count], arrived.at[n, len(group)]))
+                at += count
+        groups.append(group)
+    return groups
+
+
+def code_kernel(*refs, following):
+    if following:
+        gate_ref, up_ref, rows_ref, _, out_ref, rest_ref, arrived = refs
+        groups = fetch_rows(gate_ref, up_ref, following, rest_ref, arrived)
+    else:
+        (rows_ref, _, out_ref), groups = refs, []
+    for group in groups:
+        for copy in group:
+            copy.start()
+
+    @pl.loop(0, rows_ref.shape[0])
+    def _(n):
+        code_tile(rows_ref.at[n], out_ref, pl.multiple_of(n * 256, 256))
+
+    for group in groups:
+        for copy in group:
+            copy.wait()
+
+
+def code_weights(gate, up, rows, following, after):
+    tiles, _, depth = rows.shape
+    outs = [pltpu.VMEM((depth, 256 * tiles), jnp.bfloat16)]
+    operands, scratch = [rows, after], []
+    spaces = [pltpu.VMEM, pl.ANY]
+    if following:
+        outs.append(pltpu.VMEM((len(following), 2 * LANES, depth), jnp.bfloat16))
+        operands = [pltpu.with_memory_space_constraint(x, pltpu.HBM) for x in (gate, up)] + operands
+        spaces = [pl.ANY, pl.ANY] + spaces
+        scratch = [pltpu.SemaphoreType.DMA((len(following), 4))]
+    return pl.pallas_call(
+        functools.partial(code_kernel, following=following),
+        out_shape=outs,
+        in_specs=[pl.BlockSpec(memory_space=space) for space in spaces],
+        out_specs=[pl.BlockSpec(memory_space=pltpu.VMEM)] * len(outs),
+        scratch_shapes=scratch,
+        compiler_params=pltpu.CompilerParams(vmem_limit_bytes=12 << 20),
+        cost_estimate=pl.CostEstimate(flops=1024, bytes_accessed=1024, transcendentals=0),
+        name="code",
+    )(*operands)
+
+
+def begin_kernel(
+    tokens_ref, ids_ref, weights_ref, gate_ref, up_ref, packed_ref, out_ref, rest_ref, ids, weights, held, near, fetched,
+    *, tiles, following,
+):
+    experts = gate_ref.shape[0]
+    rows, width = tokens_ref.shape
+    routes = [
+        pltpu.make_async_copy(ids_ref, ids, near.at[0]),
+        pltpu.make_async_copy(weights_ref, weights, near.at[1]),
+    ]
+    moved = pltpu.make_async_copy(tokens_ref, packed_ref.at[:, :width], near.at[2])
+    now = len(tiles)
+    groups = fetch_rows(gate_ref, up_ref, tiles, held, fetched)
+    later = fetch_rows(gate_ref, up_ref, following, rest_ref, fetched.at[now:])
+    for copy in routes + [moved]:
+        copy.start()
+    for group in groups + later:
+        for copy in group:
+            copy.start()
+    for copy in routes:
+        copy.wait()
+    number = lax.broadcasted_iota(jnp.int32, (experts, rows), 0)
+    mix = jnp.zeros((experts, rows), jnp.float32)
+    for choice in range(ids_ref.shape[0]):
+        mix += jnp.where(ids[choice : choice + 1, :] == number, weights[choice : choice + 1, :], 0.0)
+    high = mix.astype(jnp.bfloat16).astype(jnp.float32)
+    middle = (mix - high).astype(jnp.bfloat16).astype(jnp.float32)
+    low = mix - high - middle
+    fill = jnp.zeros((LANES - 3 * experts, rows), jnp.float32)
+    packed_ref[:, width:] = jnp.concatenate([high, middle, low, fill], axis=0).T.astype(jnp.bfloat16)
+    for n, group in enumerate(groups):
+        for copy in group:
+            copy.wait()
+        code_tile(held.at[n], out_ref, 256 * n)
+    for group in later:
+        for copy in group:
+            copy.wait()
+    moved.wait()
+
+
+def begin(tokens, expert_ids, combine_weights, gate, up, tiles, following):
     depth = gate.shape[2]
-    if tail:
-        block, tiles, index = (2, LANES // 2, depth), count // 2, lambda i: (first_expert // 2 + i, 2, 0)
-    else:
-        block, tiles, index = (1, LANES, depth), count, lambda i: (first_expert + i, 0, 0)
+    rows, width = tokens.shape
+    choices = expert_ids.shape[1]
+    operands = (tokens, expert_ids.T, combine_weights.T, gate, up)
     return pl.pallas_call(
-        code_kernel,
-        grid=(tiles,),
-        out_shape=jax.ShapeDtypeStruct((depth, 256 * tiles), jnp.bfloat16),
-        in_specs=[pl.BlockSpec(block, index)] * 2,
-        out_specs=pl.BlockSpec((depth, 256), lambda i: (0, i)),
-        compiler_params=pltpu.CompilerParams(vmem_limit_bytes=8 << 20),
-        cost_estimate=pl.CostEstimate(flops=10**9 * tiles // 2, bytes_accessed=4 * tiles * depth * 256, transcendentals=0),
-        name="code",
-    )(gate, up)
-
-
-def hidden_kernel(*refs, count, pieces, experts):
+        functools.partial(begin_kernel, tiles=tiles, following=following),
+        out_shape=[
+            pltpu.VMEM((rows, width + LANES), jnp.bfloat16),
+            pltpu.VMEM((depth, 256 * len(tiles)), jnp.bfloat16),
+            pltpu.VMEM((len(following), 2 * LANES, depth), jnp.bfloat16),
+        ],
+        in_specs=[pl.BlockSpec(memory_space=pl.ANY)] * 5,
+        out_specs=[pl.BlockSpec(memory_space=pltpu.VMEM)] * 3,
+        scratch_shapes=[
+            pltpu.VMEM((choices, rows), jnp.int32),
+            pltpu.VMEM((choices, rows), jnp.float32),
+            pltpu.VMEM((len(tiles), 2 * LANES, depth), jnp.bfloat16),
+            pltpu.SemaphoreType.DMA((3,)),
+            pltpu.SemaphoreType.DMA((len(tiles) + len(following), 4)),
+        ],
+        compiler_params=pltpu.CompilerParams(vmem_limit_bytes=16 << 20),
+        cost_estimate=pl.CostEstimate(flops=1024, bytes_accessed=1024, transcendentals=0),
+        name="begin",
+    )(*(pltpu.with_memory_space_constraint(x, pltpu.HBM) for x in operands))
+
+
+def hidden_kernel(*refs, count, pieces, after, experts):
     chunks = refs[:count]
     own = refs[count : count + pieces]
     other = refs[count + pieces : count + 2 * pieces]
-    outs = refs[count + 2 * pieces : 2 * count + 2 * pieces]
-    (tok,) = refs[2 * count + 2 * pieces :]
+    *outs, tok = refs[count + 2 * pieces + after :]
     sizes = [chunk.shape[0] for chunk in chunks]
     width = tok.shape[1]
     core = lax.axis_index("tp")
@@ -96,10 +205,9 @@
     lane = lax.broadcasted_iota(jnp.int32, (total, LANES), 1)
     first_sum = jnp.zeros((total, LANES), jnp.float32)
     second_sum = jnp.zeros((total, LANES), jnp.float32)
-    per_piece = own[0].shape[1] // 256
-    for tile in range(per_piece * pieces):
-        piece, inside = divmod(tile, per_piece)
-        columns = slice(inside * 256, inside * 256 + 256)
+    places = [(piece, at) for piece in range(pieces) for at in range(0, own[piece].shape[1], 256)]
+    for tile, (piece, at) in enumerate(places):
+        columns = slice(at, at + 256)
         both = jnp.dot(near, own[piece][:, columns], preferred_element_type=jnp.float32)
         both += jnp.dot(far, other[piece][:, columns], preferred_element_type=jnp.float32)
         gate = jnp.minimum(both[:, :LANES], LIMIT)
@@ -119,22 +227,21 @@
         at += rows
 
 
-def hidden_units(chunks, own, other, experts):
+def hidden_units(chunks, own, other, experts, *after):
     units = 3 * LANES // 2
     sizes = [chunk.shape[0] for chunk in chunks]
     total, width = sum(sizes), 2 * own[0].shape[0]
     return pl.pallas_call(
-        functools.partial(hidden_kernel, count=len(chunks), pieces=len(own), experts=experts),
+        functools.partial(hidden_kernel, count=len(chunks), pieces=len(own), after=len(after), experts=experts),
         out_shape=[jax.ShapeDtypeStruct((rows, units), jnp.bfloat16) for rows in sizes],
-        in_specs=[pl.BlockSpec(memory_space=pltpu.VMEM)] * (len(chunks) + 2 * len(own)),
+        in_specs=[pl.BlockSpec(memory_space=pltpu.VMEM)] * (len(chunks) + 2 * len(own))
+        + [pl.BlockSpec(memory_space=pl.ANY)] * len(after),
         out_specs=[pl.BlockSpec(memory_space=pltpu.VMEM)] * len(chunks),
         scratch_shapes=[pltpu.VMEM((total, width), jnp.bfloat16)],
         compiler_params=pltpu.CompilerParams(vmem_limit_bytes=20 << 20),
-        cost_estimate=pl.CostEstimate(
-            flops=2 * 3 * experts * LANES * width * max(total, 256), bytes_accessed=0, transcendentals=0
-        ),
+        cost_estimate=pl.CostEstimate(flops=12*10**9, bytes_accessed=1024, transcendentals=0),
         name="hidden",
-    )(*chunks, *own, *other)
+    )(*chunks, *own, *other, *after)
 
 
 def join_kernel(*refs, steps):
@@ -156,33 +263,25 @@
         in_specs=[pl.BlockSpec(memory_space=pltpu.VMEM)] * len(blocks),
         out_specs=pl.BlockSpec(memory_space=pltpu.VMEM),
         scratch_shapes=[pltpu.VMEM((len(steps), rows, units), jnp.bfloat16)],
+        compiler_params=pltpu.CompilerParams(vmem_limit_bytes=4 << 20),
         name="join",
     )(*blocks)
 
 
-def pack_kernel(tokens_ref, ids_ref, weights_ref, out_ref, *, experts):
-    rows, width = tokens_ref.shape
-    out_ref[:, :width] = tokens_ref[...]
-    number = lax.broadcasted_iota(jnp.int32, (experts, rows), 0)
-    mix = jnp.zeros((experts, rows), jnp.float32)
-    for choice in range(ids_ref.shape[0]):
-        mix += jnp.where(ids_ref[choice : choice + 1, :] == number, weights_ref[choice : choice + 1, :], 0.0)
-    high = mix.astype(jnp.bfloat16).astype(jnp.float32)
-    middle = (mix - high).astype(jnp.bfloat16).astype(jnp.float32)
-    low = mix - high - middle
-    fill = jnp.zeros((LANES - 3 * experts, rows), jnp.float32)
-    out_ref[:, width:] = jnp.concatenate([high, middle, low, fill], axis=0).T.astype(jnp.bfloat16)
-
-
-def pack_tokens(tokens, expert_ids, combine_weights, experts):
-    rows, width = tokens.shape
+def mark_kernel(*refs):
+    refs[-1][...] = jnp.zeros(refs[-1].shape, refs[-1].dtype)
+
+
+def mark(*after):
     return pl.pallas_call(
-        functools.partial(pack_kernel, experts=experts),
-        out_shape=jax.ShapeDtypeStruct((rows, width + LANES), jnp.bfloat16),
-        in_specs=[pl.BlockSpec(memory_space=pltpu.VMEM)] * 3,
+        mark_kernel,
+        out_shape=jax.ShapeDtypeStruct((8, LANES), jnp.float32),
+        in_specs=[pl.BlockSpec(memory_space=pl.ANY)] * len(after),
         out_specs=pl.BlockSpec(memory_space=pltpu.VMEM),
-        name="pack",
-    )(tokens, expert_ids.T, combine_weights.T)
+        compiler_params=pltpu.CompilerParams(vmem_limit_bytes=1 << 20),
+        cost_estimate=pl.CostEstimate(flops=6*10**10, bytes_accessed=1024, transcendentals=0),
+        name="mark",
+    )(*after)
 
 
 def resident(tokens, expert_ids, combine_weights, gate_weight, up_weight):
@@ -198,30 +297,34 @@
     def onward(right, left):
         return ring_send(right, owners, 1), ring_send(left, owners, -1)
 
-    packed = pack_tokens(tokens, expert_ids, combine_weights, experts)
-    packed, gate_weight, up_weight = tie((packed, gate_weight, up_weight))
+    tiles = tuple(range(experts * 3 // 2))
+    now, soon, later = tiles[:3], tiles[3:7], tiles[7:]
+    packed, first, rest = begin(tokens, expert_ids, combine_weights, gate_weight, up_weight, now, soon)
     right1, left1 = onward(packed, packed)
-    own = [code_weights(gate_weight, up_weight, 0, experts // 2, False)]
-    own.append(code_weights(gate_weight, up_weight, experts // 2, experts // 2, False))
-
-    right1, left1, own, gate_weight, up_weight = tie((right1, left1, own, gate_weight, up_weight))
+    own, other = [first], [swap(first)]
+    coded, rest = code_weights(gate_weight, up_weight, rest, later, other[0])
+    own.append(coded)
+    own += code_weights(gate_weight, up_weight, rest, (), coded)
+    other += [swap(part) for part in own[1:]]
+
+    right1, left1, point = tie((right1, left1, mark(right1, left1, own[2])))
     right2, left2 = onward(right1, left1)
-    other = [swap(part) for part in own]
-    own.append(code_weights(gate_weight, up_weight, 0, experts, True))
-
-    right2, left2, own = tie((right2, left2, own))
+    home, from1, back1 = hidden_units([packed, right1, left1], own, other, experts, point)
+    done = {0: home, 1: ring_send(from1, owners, -1), -1: ring_send(back1, owners, 1)}
+
+    right2, left2, _ = tie((right2, left2, from1))
     right3, left3 = onward(right2, left2)
-    other.append(swap(own[2]))
-    home, from1, back1, from2, back2 = hidden_units([packed, right1, left1, right2, left2], own, other, experts)
-
-    right3, left3, from1, back1, from2, back2 = tie((right3, left3, from1, back1, from2, back2))
+    from2, back2 = hidden_units([right2, left2], own, other, experts, done[1], done[-1])
+    done[2], done[-2] = ring_send(from2, owners, -2), ring_send(back2, owners, 2)
+
+    right3, left3, _ = tie((right3, left3, from2))
     right4, left4 = onward(right3[:half], left3[half:])
-    done = {0: home}
-    for step, value in ((1, from1), (-1, back1), (2, from2), (-2, back2)):
-        done[step] = ring_send(value, owners, -step)
-    from3, back3, *ends = hidden_units([right3, left3, right4, left4], own, other, experts)
-    for step, value in ((4, jnp.concatenate(ends, axis=0)), (3, from3), (-3, back3)):
-        done[step] = ring_send(value, owners, -step)
+    from3, back3 = hidden_units([right3, left3], own, other, experts, done[2], done[-2])
+    done[3], done[-3] = ring_send(from3, owners, -3), ring_send(back3, owners, 3)
+
+    right4, left4, _ = tie((right4, left4, from3))
+    ends = hidden_units([right4, left4], own, other, experts)
+    done[4] = ring_send(jnp.concatenate(ends, axis=0), owners, 4)
     places = tuple(sorted(done))
     return join_units([done[p] for p in places], places)
 

time: 50.7 us -> 46.7 us (0.921)
  local copies, waits for them, and re-layouts: 3.94 us -> 0.02 us
  waiting for transfers between devices: 9.66 us -> 8.23 us
  starting transfers between devices: 21.5 us -> 22.9 us
    unnamed x22 -> x0, local copies, waits for them, and re-layouts: 3.92 us -> none
    pallas_call x2 -> x4, Pallas kernels: 5.87 us -> 7.3 us  [hidden_units(): pl.pallas_call(functools.partial(hidden_kernel, count=len(chunks), pieces...]
    ppermute x3, waiting for transfers between devices: 1.38 us -> 0.01 us  [swap(): return lax.ppermute(part, 'tp', [(0, 1), (1, 0)])]
    pallas_call x1, Pallas kernels: 1.7 us -> 0.82 us  [join_units(): pl.pallas_call(functools.partial(join_kernel, steps=steps), out_shape=jax...]
    ppermute x15, starting transfers between devices: 21 us -> 21.8 us  [ring_send(): return lax.ppermute(value, 'ep', ring_shift(owners, steps))]
    ppermute x3, starting transfers between devices: 0.51 us -> 1.16 us  [swap(): return lax.ppermute(part, 'tp', [(0, 1), (1, 0)])]
  transfers between devices with their start and end apart: 18 -> 18, of which waited for: 8 -> 7; matrix products, arithmetic and copies ran while one was open for 0% -> 0% of each run, Pallas kernels for 23% -> 24%
where the time goes in v2:
time: 46.7 us; the launch traced here: 46.6 us
  starting transfers between devices  22.9 us (49%)
  Pallas kernels  15.4 us (33%)
  waiting for transfers between devices  8.23 us (18%)
    ppermute x15, starting transfers between devices, ring_send(): return lax.ppermute(value, 'ep', ring_shift(owners, steps))  21.8 us
    ppermute x15, waiting for transfers between devices, ring_send(): return lax.ppermute(value, 'ep', ring_shift(owners, steps))  8.22 us
    pallas_call x4, Pallas kernels, hidden_units(): pl.pallas_call(functools.partial(hidden_kernel, count=len(chunks), pieces...  7.3 us
    pallas_call x2, Pallas kernels, code_weights(): pl.pallas_call(functools.partial(code_kernel, following=following), out_s...  4.07 us
    pallas_call x1, Pallas kernels, begin(): pl.pallas_call(functools.partial(begin_kernel, tiles=tiles, following=fol...  3.17 us
    ppermute x3, starting transfers between devices, swap(): return lax.ppermute(part, 'tp', [(0, 1), (1, 0)])  1.16 us
  transfers between devices with their start and end apart: 18, of which 7 were waited for; matrix products, arithmetic and copies ran while one was open for 0% of the time, Pallas kernels for 24%

profile of v2, /device:TPU:0, one launch (start us, length us, event | category | flops | bytes accessed | tf_op | source)
XLA Modules:
  0.0 46.6 jit_solution(10219549124537758080)
XLA Ops:
  0.0 3.2 %begin.1 = (bf16[64,1664]{1,0:T(8,128)(2,1)S(1)}, bf16[768,768]{1,0:T(8,128)(2,1)S(1)}, bf16[4,256,768]{2,1,0:T(8,128)(2,1)S(1)}) custom-call(bf16[64,1536]{1,0:T(8,128)(2,1)} %tokens_ref.1, s32[4,64]{1,0:T(4,128)} %bitcast.2, f32[4,64]{1,0:T(4,128)} %bitcast.3, bf16[8,192,768]{2,1,0:T(8,128)(2,1)} %refs_0_.1, bf16[8,192,768]{2,1,0:T(8,128)(2,1)} %refs_1_.1), custom_call_target="tpu_custom_call" | custom-call | flops 1024 | bytes 1024 | tf_op jit(solution)/shard_map/begin/pallas_call | solution.py:163
  3.7 2.6 %collective-permute-start = (bf16[64,1664]{1,0:T(8,128)(2,1)S(1)}, bf16[64,1664]{1,0:T(8,128)(2,1)S(1)}, u32[]{:S(2)}, u32[]{:S(2)}) collective-permute-start(bf16[64,1664]{1,0:T(8,128)(2,1)S(1)} %get-tuple-element.28.refs_0_), channel_id=1, source_target_pairs={{0,4},{4,8},{8,12},{12,14},{14,10},{10,6},{6,2},{2,0},{1,5},{5,9},... | collective-permute-start | bytes 638984 | tf_op jit(solution)/shard_map/ppermute | solution.py:31
  6.3 1.9 %code.2 = (bf16[768,1024]{1,0:T(8,128)(2,1)S(1)}, bf16[5,256,768]{2,1,0:T(8,128)(2,1)S(1)}) custom-call(bf16[8,192,768]{2,1,0:T(8,128)(2,1)} %refs_0_.1, bf16[8,192,768]{2,1,0:T(8,128)(2,1)} %refs_1_.1, bf16[4,256,768]{2,1,0:T(8,128)(2,1)S(1)} %get-tuple-element.29.refs_2_, bf16[768,768]{1,0:T(8,128)(2,1)S(1)} %collective-permute-done.2.refs_3_.refs_6_.refs_5_), custom_call_target="tpu_custom_call" | custom-call | flops 1024 | bytes 1024 | tf_op jit(solution)/shard_map/code/pallas_call | solution.py:106
  8.5 2.1 %code.3.refs_2_.refs_5_.refs_4_ = bf16[768,1280]{1,0:T(8,128)(2,1)S(1)} custom-call(bf16[5,256,768]{2,1,0:T(8,128)(2,1)S(1)} %get-tuple-element.31.refs_0_, bf16[768,1024]{1,0:T(8,128)(2,1)S(1)} %get-tuple-element.32.refs_1_.refs_4_.refs_3_), custom_call_target="tpu_custom_call" | custom-call | flops 1024 | bytes 1024 | tf_op jit(solution)/shard_map/code/pallas_call | solution.py:106
  11.1 1.0 %collective-permute-done.refs_0_.refs_1_ = bf16[64,1664]{1,0:T(8,128)(2,1)S(1)} collective-permute-done((bf16[64,1664]{1,0:T(8,128)(2,1)S(1)}, bf16[64,1664]{1,0:T(8,128)(2,1)S(1)}, u32[]{:S(2)}, u32[]{:S(2)}) %collective-permute-start) | collective-permute-done | bytes 213024 | tf_op jit(solution)/shard_map/ppermute | solution.py:31
  12.1 1.5 %collective-permute-done.1.refs_1_.refs_2_ = bf16[64,1664]{1,0:T(8,128)(2,1)S(1)} collective-permute-done((bf16[64,1664]{1,0:T(8,128)(2,1)S(1)}, bf16[64,1664]{1,0:T(8,128)(2,1)S(1)}, u32[]{:S(2)}, u32[]{:S(2)}) %collective-permute-start.1) | collective-permute-done | bytes 213024 | tf_op jit(solution)/shard_map/ppermute | solution.py:31
  13.7 1.6 %collective-permute-start.3 = (bf16[64,1664]{1,0:T(8,128)(2,1)S(1)}, bf16[64,1664]{1,0:T(8,128)(2,1)S(1)}, u32[]{:S(2)}, u32[]{:S(2)}) collective-permute-start(bf16[64,1664]{1,0:T(8,128)(2,1)S(1)} %collective-permute-done.refs_0_.refs_1_), channel_id=1, source_target_pairs={{0,4},{4,8},{8,12},{12,14},{14,10},{10,6},{6,2},{2,0},{1,5},{5,9},... | collective-permute-start | bytes 638984 | tf_op jit(solution)/shard_map/ppermute | solution.py:31
  15.7 2.3 %hidden.4 = (bf16[64,192]{1,0:T(8,128)(2,1)S(1)}, bf16[64,192]{1,0:T(8,128)(2,1)S(1)}, bf16[64,192]{1,0:T(8,128)(2,1)S(1)}) custom-call(bf16[64,1664]{1,0:T(8,128)(2,1)S(1)} %get-tuple-element.28.refs_0_, bf16[64,1664]{1,0:T(8,128)(2,1)S(1)} %collective-permute-done.refs_0_.refs_1_, bf16[64,1664]{1,0:T(8,128)(2,1)S(1)} %collective-permute-done.1.refs_1_.refs_2_, ...), custom_call_target="tpu_custom_call" | custom-call | flops 12000000000 | bytes 1024 | tf_op jit(solution)/shard_map/hidden/pallas_call | solution.py:234
  17.9 1.8 %collective-permute-start.10 = (bf16[64,192]{1,0:T(8,128)(2,1)S(1)}, bf16[64,192]{1,0:T(8,128)(2,1)S(1)}, u32[]{:S(2)}, u32[]{:S(2)}) collective-permute-start(bf16[64,192]{1,0:T(8,128)(2,1)S(1)} %get-tuple-element.39), channel_id=1, source_target_pairs={{0,4},{4,8},{8,12},{12,14},{14,10},{10,6},{6,2},{2,0},{1,5},{5,9},... | collective-permute-start | bytes 73736 | tf_op jit(solution)/shard_map/ppermute | solution.py:31
  20.2 1.3 %collective-permute-done.4.refs_1_ = bf16[64,1664]{1,0:T(8,128)(2,1)S(1)} collective-permute-done((bf16[64,1664]{1,0:T(8,128)(2,1)S(1)}, bf16[64,1664]{1,0:T(8,128)(2,1)S(1)}, u32[]{:S(2)}, u32[]{:S(2)}) %collective-permute-start.4) | collective-permute-done | bytes 213024 | tf_op jit(solution)/shard_map/ppermute | solution.py:31
  21.5 1.6 %collective-permute-start.7 = (bf16[64,1664]{1,0:T(8,128)(2,1)S(1)}, bf16[64,1664]{1,0:T(8,128)(2,1)S(1)}, u32[]{:S(2)}, u32[]{:S(2)}) collective-permute-start(bf16[64,1664]{1,0:T(8,128)(2,1)S(1)} %collective-permute-done.3.refs_0_), channel_id=1, source_target_pairs={{0,4},{4,8},{8,12},{12,14},{14,10},{10,6},{6,2},{2,0},{1,5},{5,9},... | collective-permute-start | bytes 638984 | tf_op jit(solution)/shard_map/ppermute | solution.py:31
  23.7 1.6 %hidden.5 = (bf16[64,192]{1,0:T(8,128)(2,1)S(1)}, bf16[64,192]{1,0:T(8,128)(2,1)S(1)}) custom-call(bf16[64,1664]{1,0:T(8,128)(2,1)S(1)} %collective-permute-done.3.refs_0_, bf16[64,1664]{1,0:T(8,128)(2,1)S(1)} %collective-permute-done.4.refs_1_, bf16[768,768]{1,0:T(8,128)(2,1)S(1)} %get-tuple-element.30.refs_3_.refs_2_, ...), custom_call_target="tpu_custom_call" | custom-call | flops 12000000000 | bytes 1024 | tf_op jit(solution)/shard_map/hidden/pallas_call | solution.py:234
  25.2 1.4 %collective-permute-start.11 = (bf16[64,192]{1,0:T(8,128)(2,1)S(1)}, bf16[64,192]{1,0:T(8,128)(2,1)S(1)}, u32[]{:S(2)}, u32[]{:S(2)}) collective-permute-start(bf16[64,192]{1,0:T(8,128)(2,1)S(1)} %get-tuple-element.40), channel_id=1, source_target_pairs={{0,6},{4,2},{8,0},{12,4},{14,8},{10,12},{6,14},{2,10},{1,7},{5,3},... | collective-permute-start | bytes 73736 | tf_op jit(solution)/shard_map/ppermute | solution.py:31
  26.7 1.5 %collective-permute-start.12 = (bf16[64,192]{1,0:T(8,128)(2,1)S(1)}, bf16[64,192]{1,0:T(8,128)(2,1)S(1)}, u32[]{:S(2)}, u32[]{:S(2)}) collective-permute-start(bf16[64,192]{1,0:T(8,128)(2,1)S(1)} %get-tuple-element.43), channel_id=1, source_target_pairs={{0,8},{4,12},{8,14},{12,10},{14,6},{10,2},{6,0},{2,4},{1,9},{5,13}... | collective-permute-start | bytes 73736 | tf_op jit(solution)/shard_map/ppermute | solution.py:31
  28.2 1.3 %collective-permute-done.8.refs_1_ = bf16[64,1664]{1,0:T(8,128)(2,1)S(1)} collective-permute-done((bf16[64,1664]{1,0:T(8,128)(2,1)S(1)}, bf16[64,1664]{1,0:T(8,128)(2,1)S(1)}, u32[]{:S(2)}, u32[]{:S(2)}) %collective-permute-start.8) | collective-permute-done | bytes 213024 | tf_op jit(solution)/shard_map/ppermute | solution.py:31
  29.6 1.5 %collective-permute-start.15 = (bf16[32,1664]{1,0:T(8,128)(2,1)S(1)}, bf16[32,1664]{1,0:T(8,128)(2,1)S(1)}, u32[]{:S(2)}, u32[]{:S(2)}) collective-permute-start(bf16[32,1664]{1,0:T(8,128)(2,1)S(1)} %slice.6), channel_id=1, source_target_pairs={{0,4},{4,8},{8,12},{12,14},{14,10},{10,6},{6,2},{2,0},{1,5},{5,9},... | collective-permute-start | bytes 319496 | tf_op jit(solution)/shard_map/ppermute | solution.py:31
  31.1 0.6 %collective-permute-start.16 = (bf16[32,1664]{1,0:T(8,128)(2,1)S(1)}, bf16[32,1664]{1,0:T(8,128)(2,1)S(1)}, u32[]{:S(2)}, u32[]{:S(2)}) collective-permute-start(bf16[32,1664]{1,0:T(8,128)(2,1)S(1)} %slice.7), channel_id=1, source_target_pairs={{0,2},{4,0},{8,4},{12,8},{14,12},{10,14},{6,10},{2,6},{1,3},{5,1},... | collective-permute-start | bytes 319496 | tf_op jit(solution)/shard_map/ppermute | solution.py:31
  31.7 1.6 %hidden.6 = (bf16[64,192]{1,0:T(8,128)(2,1)S(1)}, bf16[64,192]{1,0:T(8,128)(2,1)S(1)}) custom-call(bf16[64,1664]{1,0:T(8,128)(2,1)S(1)} %collective-permute-done.7.refs_0_, bf16[64,1664]{1,0:T(8,128)(2,1)S(1)} %collective-permute-done.8.refs_1_, bf16[768,768]{1,0:T(8,128)(2,1)S(1)} %get-tuple-element.30.refs_3_.refs_2_, ...), custom_call_target="tpu_custom_call" | custom-call | flops 12000000000 | bytes 1024 | tf_op jit(solution)/shard_map/hidden/pallas_call | solution.py:234
  33.3 3.0 %collective-permute-start.13 = (bf16[64,192]{1,0:T(8,128)(2,1)S(1)}, bf16[64,192]{1,0:T(8,128)(2,1)S(1)}, u32[]{:S(2)}, u32[]{:S(2)}) collective-permute-start(bf16[64,192]{1,0:T(8,128)(2,1)S(1)} %get-tuple-element.44), channel_id=1, source_target_pairs={{0,12},{4,14},{8,10},{12,6},{14,2},{10,0},{6,4},{2,8},{1,13},{5,15... | collective-permute-start | bytes 73736 | tf_op jit(solution)/shard_map/ppermute | solution.py:31
  36.4 0.9 %collective-permute-start.14 = (bf16[64,192]{1,0:T(8,128)(2,1)S(1)}, bf16[64,192]{1,0:T(8,128)(2,1)S(1)}, u32[]{:S(2)}, u32[]{:S(2)}) collective-permute-start(bf16[64,192]{1,0:T(8,128)(2,1)S(1)} %get-tuple-element.46), channel_id=1, source_target_pairs={{0,10},{4,6},{8,2},{12,0},{14,4},{10,8},{6,12},{2,14},{1,11},{5,7}... | collective-permute-start | bytes 73736 | tf_op jit(solution)/shard_map/ppermute | solution.py:31
  37.2 1.9 %hidden.7 = (bf16[32,192]{1,0:T(8,128)(2,1)S(1)}, bf16[32,192]{1,0:T(8,128)(2,1)S(1)}) custom-call(bf16[32,1664]{1,0:T(8,128)(2,1)S(1)} %collective-permute-done.15.refs_0_, bf16[32,1664]{1,0:T(8,128)(2,1)S(1)} %collective-permute-done.16.refs_1_, bf16[768,768]{1,0:T(8,128)(2,1)S(1)} %get-tuple-element.30.refs_3_.refs_2_, ...), custom_call_target="tpu_custom_call" | custom-call | flops 12000000000 | bytes 1024 | tf_op jit(solution)/shard_map/hidden/pallas_call | solution.py:234
  39.1 4.0 %collective-permute-start.17 = (bf16[64,192]{1,0:T(8,128)(2,1)S(1)}, bf16[64,192]{1,0:T(8,128)(2,1)S(1)}, u32[]{:S(2)}, u32[]{:S(2)}) collective-permute-start(bf16[64,192]{1,0:T(8,128)(2,1)S(1)} %pad_maximum_fusion), channel_id=1, source_target_pairs={{0,14},{4,10},{8,6},{12,2},{14,0},{10,4},{6,8},{2,12},{1,15},{5,11... | collective-permute-start | bytes 73736 | tf_op jit(solution)/shard_map/ppermute | solution.py:31
  43.1 2.7 %collective-permute-done.17.refs_7_ = bf16[64,192]{1,0:T(8,128)(2,1)S(1)} collective-permute-done((bf16[64,192]{1,0:T(8,128)(2,1)S(1)}, bf16[64,192]{1,0:T(8,128)(2,1)S(1)}, u32[]{:S(2)}, u32[]{:S(2)}) %collective-permute-start.17) | collective-permute-done | bytes 24608 | tf_op jit(solution)/shard_map/ppermute | solution.py:31
  45.8 0.8 %join.1 = bf16[64,1536]{1,0:T(8,128)(2,1)} custom-call(bf16[64,192]{1,0:T(8,128)(2,1)S(1)} %collective-permute-done.13.refs_0_, bf16[64,192]{1,0:T(8,128)(2,1)S(1)} %collective-permute-done.12.refs_9_.refs_1_, bf16[64,192]{1,0:T(8,128)(2,1)S(1)} %collective-permute-done.10.refs_9_.refs_2_, bf16[64,192]{1,0:T(8,128)(2,1)S(1)} %get-tuple-element.45.refs_3_, ...), custom_call_target="tpu_custom_call" | custom-call | tf_op jit(solution)/shard_map/join/pallas_call | solution.py:260
  (24 shorter events, 2.7 us)
Async XLA Ops:
  3.2 3.2 %collective-permute-start.2 = (bf16[768,768]{1,0:T(8,128)(2,1)S(1)}, bf16[768,768]{1,0:T(8,128)(2,1)S(1)}, u32[]{:S(2)}, u32[]{:S(2)}) collective-permute-start(bf16[768,768]{1,0:T(8,128)(2,1)S(1)} %get-tuple-element.30.refs_3_.refs_2_), channel_id=1, source_target_pairs={{0,1},{1,0},{2,3},{3,2},{4,5},{5,4},{6,7},{7,6},{8,9},{9,8},{10,11... | collective-permute-start | bytes 3538952 | tf_op jit(solution)/shard_map/ppermute | solution.py:295
  3.7 8.4 %collective-permute-start = (bf16[64,1664]{1,0:T(8,128)(2,1)S(1)}, bf16[64,1664]{1,0:T(8,128)(2,1)S(1)}, u32[]{:S(2)}, u32[]{:S(2)}) collective-permute-start(bf16[64,1664]{1,0:T(8,128)(2,1)S(1)} %get-tuple-element.28.refs_0_), channel_id=1, source_target_pairs={{0,4},{4,8},{8,12},{12,14},{14,10},{10,6},{6,2},{2,0},{1,5},{5,9},... | collective-permute-start | bytes 638984 | tf_op jit(solution)/shard_map/ppermute | solution.py:31
  6.3 7.3 %collective-permute-start.1 = (bf16[64,1664]{1,0:T(8,128)(2,1)S(1)}, bf16[64,1664]{1,0:T(8,128)(2,1)S(1)}, u32[]{:S(2)}, u32[]{:S(2)}) collective-permute-start(bf16[64,1664]{1,0:T(8,128)(2,1)S(1)} %get-tuple-element.28.refs_0_), channel_id=1, source_target_pairs={{0,2},{4,0},{8,4},{12,8},{14,12},{10,14},{6,10},{2,6},{1,3},{5,1},... | collective-permute-start | bytes 638984 | tf_op jit(solution)/shard_map/ppermute | solution.py:31
  8.3 7.4 %collective-permute-start.5 = (bf16[768,1024]{1,0:T(8,128)(2,1)S(1)}, bf16[768,1024]{1,0:T(8,128)(2,1)S(1)}, u32[]{:S(2)}, u32[]{:S(2)}) collective-permute-start(bf16[768,1024]{1,0:T(8,128)(2,1)S(1)} %get-tuple-element.32.refs_1_.refs_4_.refs_3_), channel_id=1, source_target_pairs={{0,1},{1,0},{2,3},{3,2},{4,5},{5,4},{6,7},{7,6},{8,9},{9,8},{10,11... | collective-permute-start | bytes 4718600 | tf_op jit(solution)/shard_map/ppermute | solution.py:295
  10.7 5.0 %collective-permute-start.6 = (bf16[768,1280]{1,0:T(8,128)(2,1)S(1)}, bf16[768,1280]{1,0:T(8,128)(2,1)S(1)}, u32[]{:S(2)}, u32[]{:S(2)}) collective-permute-start(bf16[768,1280]{1,0:T(8,128)(2,1)S(1)} %code.3.refs_2_.refs_5_.refs_4_), channel_id=1, source_target_pairs={{0,1},{1,0},{2,3},{3,2},{4,5},{5,4},{6,7},{7,6},{8,9},{9,8},{10,11... | collective-permute-start | bytes 5898248 | tf_op jit(solution)/shard_map/ppermute | solution.py:295
  13.7 6.5 %collective-permute-start.3 = (bf16[64,1664]{1,0:T(8,128)(2,1)S(1)}, bf16[64,1664]{1,0:T(8,128)(2,1)S(1)}, u32[]{:S(2)}, u32[]{:S(2)}) collective-permute-start(bf16[64,1664]{1,0:T(8,128)(2,1)S(1)} %collective-permute-done.refs_0_.refs_1_), channel_id=1, source_target_pairs={{0,4},{4,8},{8,12},{12,14},{14,10},{10,6},{6,2},{2,0},{1,5},{5,9},... | collective-permute-start | bytes 638984 | tf_op jit(solution)/shard_map/ppermute | solution.py:31
  15.2 6.2 %collective-permute-start.4 = (bf16[64,1664]{1,0:T(8,128)(2,1)S(1)}, bf16[64,1664]{1,0:T(8,128)(2,1)S(1)}, u32[]{:S(2)}, u32[]{:S(2)}) collective-permute-start(bf16[64,1664]{1,0:T(8,128)(2,1)S(1)} %collective-permute-done.1.refs_1_.refs_2_), channel_id=1, source_target_pairs={{0,2},{4,0},{8,4},{12,8},{14,12},{10,14},{6,10},{2,6},{1,3},{5,1},... | collective-permute-start | bytes 638984 | tf_op jit(solution)/shard_map/ppermute | solution.py:31
  17.9 5.5 %collective-permute-start.10 = (bf16[64,192]{1,0:T(8,128)(2,1)S(1)}, bf16[64,192]{1,0:T(8,128)(2,1)S(1)}, u32[]{:S(2)}, u32[]{:S(2)}) collective-permute-start(bf16[64,192]{1,0:T(8,128)(2,1)S(1)} %get-tuple-element.39), channel_id=1, source_target_pairs={{0,4},{4,8},{8,12},{12,14},{14,10},{10,6},{6,2},{2,0},{1,5},{5,9},... | collective-permute-start | bytes 73736 | tf_op jit(solution)/shard_map/ppermute | solution.py:31
  19.8 3.9 %collective-permute-start.9 = (bf16[64,192]{1,0:T(8,128)(2,1)S(1)}, bf16[64,192]{1,0:T(8,128)(2,1)S(1)}, u32[]{:S(2)}, u32[]{:S(2)}) collective-permute-start(bf16[64,192]{1,0:T(8,128)(2,1)S(1)} %get-tuple-element.36), channel_id=1, source_target_pairs={{0,2},{4,0},{8,4},{12,8},{14,12},{10,14},{6,10},{2,6},{1,3},{5,1},... | collective-permute-start | bytes 73736 | tf_op jit(solution)/shard_map/ppermute | solution.py:31
  21.5 6.8 %collective-permute-start.7 = (bf16[64,1664]{1,0:T(8,128)(2,1)S(1)}, bf16[64,1664]{1,0:T(8,128)(2,1)S(1)}, u32[]{:S(2)}, u32[]{:S(2)}) collective-permute-start(bf16[64,1664]{1,0:T(8,128)(2,1)S(1)} %collective-permute-done.3.refs_0_), channel_id=1, source_target_pairs={{0,4},{4,8},{8,12},{12,14},{14,10},{10,6},{6,2},{2,0},{1,5},{5,9},... | collective-permute-start | bytes 638984 | tf_op jit(solution)/shard_map/ppermute | solution.py:31
  23.0 6.5 %collective-permute-start.8 = (bf16[64,1664]{1,0:T(8,128)(2,1)S(1)}, bf16[64,1664]{1,0:T(8,128)(2,1)S(1)}, u32[]{:S(2)}, u32[]{:S(2)}) collective-permute-start(bf16[64,1664]{1,0:T(8,128)(2,1)S(1)} %collective-permute-done.4.refs_1_), channel_id=1, source_target_pairs={{0,2},{4,0},{8,4},{12,8},{14,12},{10,14},{6,10},{2,6},{1,3},{5,1},... | collective-permute-start | bytes 638984 | tf_op jit(solution)/shard_map/ppermute | solution.py:31
  25.2 6.5 %collective-permute-start.11 = (bf16[64,192]{1,0:T(8,128)(2,1)S(1)}, bf16[64,192]{1,0:T(8,128)(2,1)S(1)}, u32[]{:S(2)}, u32[]{:S(2)}) collective-permute-start(bf16[64,192]{1,0:T(8,128)(2,1)S(1)} %get-tuple-element.40), channel_id=1, source_target_pairs={{0,6},{4,2},{8,0},{12,4},{14,8},{10,12},{6,14},{2,10},{1,7},{5,3},... | collective-permute-start | bytes 73736 | tf_op jit(solution)/shard_map/ppermute | solution.py:31
  26.7 5.1 %collective-permute-start.12 = (bf16[64,192]{1,0:T(8,128)(2,1)S(1)}, bf16[64,192]{1,0:T(8,128)(2,1)S(1)}, u32[]{:S(2)}, u32[]{:S(2)}) collective-permute-start(bf16[64,192]{1,0:T(8,128)(2,1)S(1)} %get-tuple-element.43), channel_id=1, source_target_pairs={{0,8},{4,12},{8,14},{12,10},{14,6},{10,2},{6,0},{2,4},{1,9},{5,13}... | collective-permute-start | bytes 73736 | tf_op jit(solution)/shard_map/ppermute | solution.py:31
  29.6 7.6 %collective-permute-start.15 = (bf16[32,1664]{1,0:T(8,128)(2,1)S(1)}, bf16[32,1664]{1,0:T(8,128)(2,1)S(1)}, u32[]{:S(2)}, u32[]{:S(2)}) collective-permute-start(bf16[32,1664]{1,0:T(8,128)(2,1)S(1)} %slice.6), channel_id=1, source_target_pairs={{0,4},{4,8},{8,12},{12,14},{14,10},{10,6},{6,2},{2,0},{1,5},{5,9},... | collective-permute-start | bytes 319496 | tf_op jit(solution)/shard_map/ppermute | solution.py:31
  31.1 6.1 %collective-permute-start.16 = (bf16[32,1664]{1,0:T(8,128)(2,1)S(1)}, bf16[32,1664]{1,0:T(8,128)(2,1)S(1)}, u32[]{:S(2)}, u32[]{:S(2)}) collective-permute-start(bf16[32,1664]{1,0:T(8,128)(2,1)S(1)} %slice.7), channel_id=1, source_target_pairs={{0,2},{4,0},{8,4},{12,8},{14,12},{10,14},{6,10},{2,6},{1,3},{5,1},... | collective-permute-start | bytes 319496 | tf_op jit(solution)/shard_map/ppermute | solution.py:31
  33.3 9.8 %collective-permute-start.13 = (bf16[64,192]{1,0:T(8,128)(2,1)S(1)}, bf16[64,192]{1,0:T(8,128)(2,1)S(1)}, u32[]{:S(2)}, u32[]{:S(2)}) collective-permute-start(bf16[64,192]{1,0:T(8,128)(2,1)S(1)} %get-tuple-element.44), channel_id=1, source_target_pairs={{0,12},{4,14},{8,10},{12,6},{14,2},{10,0},{6,4},{2,8},{1,13},{5,15... | collective-permute-start | bytes 73736 | tf_op jit(solution)/shard_map/ppermute | solution.py:31
  36.4 6.8 %collective-permute-start.14 = (bf16[64,192]{1,0:T(8,128)(2,1)S(1)}, bf16[64,192]{1,0:T(8,128)(2,1)S(1)}, u32[]{:S(2)}, u32[]{:S(2)}) collective-permute-start(bf16[64,192]{1,0:T(8,128)(2,1)S(1)} %get-tuple-element.46), channel_id=1, source_target_pairs={{0,10},{4,6},{8,2},{12,0},{14,4},{10,8},{6,12},{2,14},{1,11},{5,7}... | collective-permute-start | bytes 73736 | tf_op jit(solution)/shard_map/ppermute | solution.py:31
  39.1 6.7 %collective-permute-start.17 = (bf16[64,192]{1,0:T(8,128)(2,1)S(1)}, bf16[64,192]{1,0:T(8,128)(2,1)S(1)}, u32[]{:S(2)}, u32[]{:S(2)}) collective-permute-start(bf16[64,192]{1,0:T(8,128)(2,1)S(1)} %pad_maximum_fusion), channel_id=1, source_target_pairs={{0,14},{4,10},{8,6},{12,2},{14,0},{10,4},{6,8},{2,12},{1,15},{5,11... | collective-permute-start | bytes 73736 | tf_op jit(solution)/shard_map/ppermute | solution.py:31

commit v3 on v2

--- a/solution.py
+++ b/solution.py
@@ -22,13 +22,14 @@
     return jnp.where(place < owners // 2, 2 * place, 2 * (owners - 1 - place) + 1)
 
 
-def ring_shift(owners, steps):
+def ring_send(value, owners, steps):
     order = list(range(0, owners, 2)) + list(range(1, owners, 2))[::-1]
-    return [(order[p], order[(p + steps) % owners]) for p in range(owners)]
-
-
-def ring_send(value, owners, steps):
-    return lax.ppermute(value, "ep", ring_shift(owners, steps))
+    pairs = [
+        (2 * order[p] + core, 2 * order[(p + sign * steps) % owners] + core)
+        for core, sign in ((0, 1), (1, -1))
+        for p in range(owners)
+    ]
+    return lax.ppermute(value, ("ep", "tp"), pairs)
 
 
 def code_columns(entries):
@@ -191,15 +192,18 @@
     width = tok.shape[1]
     core = lax.axis_index("tp")
     depth = own[0].shape[0]
-    total = sum(sizes)
+    total = tok.shape[0]
     at = 0
     mixes = []
     for chunk, rows in zip(chunks, sizes):
         tok[at : at + rows, :] = chunk[:, :width]
-        parts = chunk[:, width:].astype(jnp.float32)
+        parts = chunk[:, width : width + LANES].astype(jnp.float32)
         mixes.append(parts[:, :experts] + parts[:, experts : 2 * experts] + parts[:, 2 * experts : 3 * experts])
         at += rows
-    mix = jnp.concatenate(mixes, axis=0) if count > 1 else mixes[0]
+    if at < total:
+        tok[at:, :] = jnp.zeros((total - at, width), tok.dtype)
+        mixes.append(jnp.zeros((total - at, experts), jnp.float32))
+    mix = jnp.concatenate(mixes, axis=0) if len(mixes) > 1 else mixes[0]
     near = tok[:, pl.ds(pl.multiple_of(core * depth, LANES), depth)]
     far = tok[:, pl.ds(pl.multiple_of((1 - core) * depth, LANES), depth)]
     lane = lax.broadcasted_iota(jnp.int32, (total, LANES), 1)
@@ -230,7 +234,7 @@
 def hidden_units(chunks, own, other, experts, *after):
     units = 3 * LANES // 2
     sizes = [chunk.shape[0] for chunk in chunks]
-    total, width = sum(sizes), 2 * own[0].shape[0]
+    total, width = max(sum(sizes), LANES), 2 * own[0].shape[0]
     return pl.pallas_call(
         functools.partial(hidden_kernel, count=len(chunks), pieces=len(own), after=len(after), experts=experts),
         out_shape=[jax.ShapeDtypeStruct((rows, units), jnp.bfloat16) for rows in sizes],
@@ -248,15 +252,17 @@
     blocks, out_ref, held = refs[: len(steps)], refs[len(steps)], refs[len(steps) + 1]
     owners = lax.axis_size("ep")
     place = ring_place(lax.axis_index("ep"), owners)
-    units = blocks[0].shape[1]
+    sign = 1 - 2 * lax.axis_index("tp")
+    units = held.shape[2]
     for block, step in zip(blocks, steps):
-        held[ring_owner((place + step + owners) % owners, owners)] = block[...]
+        first = max(block.shape[1] - 2 * LANES, 0)
+        held[ring_owner((place + sign * step + owners) % owners, owners)] = block[:, first : first + units]
     for owner in range(owners):
         out_ref[:, owner * units : (owner + 1) * units] = held[owner]
 
 
-def join_units(blocks, steps):
-    rows, units = blocks[0].shape
+def join_units(blocks, steps, units):
+    rows = blocks[0].shape[0]
     return pl.pallas_call(
         functools.partial(join_kernel, steps=steps),
         out_shape=jax.ShapeDtypeStruct((rows, units * len(steps)), jnp.bfloat16),
@@ -268,6 +274,26 @@
     )(*blocks)
 
 
+def attach_kernel(chunk_ref, block_ref, out_ref):
+    width, units = chunk_ref.shape[1], block_ref.shape[1]
+    out_ref[:, :width] = chunk_ref[...]
+    out_ref[:, width : width + units] = block_ref[...]
+    out_ref[:, width + units :] = jnp.zeros((out_ref.shape[0], 2 * LANES - units), out_ref.dtype)
+
+
+def attach(chunk, block):
+    rows, width = chunk.shape
+    return pl.pallas_call(
+        attach_kernel,
+        out_shape=jax.ShapeDtypeStruct((rows, width + 2 * LANES), chunk.dtype),
+        in_specs=[pl.BlockSpec(memory_space=pltpu.VMEM)] * 2,
+        out_specs=pl.BlockSpec(memory_space=pltpu.VMEM),
+        compiler_params=pltpu.CompilerParams(vmem_limit_bytes=4 << 20),
+        cost_estimate=pl.CostEstimate(flops=1024, bytes_accessed=1024, transcendentals=0),
+        name="attach",
+    )(chunk, block)
+
+
 def mark_kernel(*refs):
     refs[-1][...] = jnp.zeros(refs[-1].shape, refs[-1].dtype)
 
@@ -287,8 +313,6 @@
 def resident(tokens, expert_ids, combine_weights, gate_weight, up_weight):
     experts = gate_weight.shape[0]
     owners = lax.axis_size("ep")
-    rows = tokens.shape[0]
-    half = rows // 2
     tie = lax.optimization_barrier
 
     def swap(part):
@@ -298,35 +322,38 @@
         return ring_send(right, owners, 1), ring_send(left, owners, -1)
 
     tiles = tuple(range(experts * 3 // 2))
-    now, soon, later = tiles[:3], tiles[3:7], tiles[7:]
-    packed, first, rest = begin(tokens, expert_ids, combine_weights, gate_weight, up_weight, now, soon)
+    parts = tiles[:2], tiles[2:5], tiles[5:8], tiles[8:]
+    packed, first, rest = begin(tokens, expert_ids, combine_weights, gate_weight, up_weight, *parts[:2])
     right1, left1 = onward(packed, packed)
     own, other = [first], [swap(first)]
-    coded, rest = code_weights(gate_weight, up_weight, rest, later, other[0])
-    own.append(coded)
-    own += code_weights(gate_weight, up_weight, rest, (), coded)
+    after = other[0]
+    for following in parts[2:]:
+        coded, rest = code_weights(gate_weight, up_weight, rest, following, after)
+        own.append(coded)
+        after = coded
+    own += code_weights(gate_weight, up_weight, rest, (), after)
     other += [swap(part) for part in own[1:]]
 
-    right1, left1, point = tie((right1, left1, mark(right1, left1, own[2])))
+    right1, left1, point = tie((right1, left1, mark(right1, left1, own[-1])))
     right2, left2 = onward(right1, left1)
-    home, from1, back1 = hidden_units([packed, right1, left1], own, other, experts, point)
-    done = {0: home, 1: ring_send(from1, owners, -1), -1: ring_send(back1, owners, 1)}
-
-    right2, left2, _ = tie((right2, left2, from1))
-    right3, left3 = onward(right2, left2)
-    from2, back2 = hidden_units([right2, left2], own, other, experts, done[1], done[-1])
+    from1, back1 = hidden_units([right1, left1], own, other, experts, point)
+    right3, left3 = onward(attach(right2, back1), attach(left2, from1))
+    done = {-1: right3, 1: left3}
+    from2, back2 = hidden_units([right2, left2], own, other, experts)
     done[2], done[-2] = ring_send(from2, owners, -2), ring_send(back2, owners, 2)
 
-    right3, left3, _ = tie((right3, left3, from2))
-    right4, left4 = onward(right3[:half], left3[half:])
-    from3, back3 = hidden_units([right3, left3], own, other, experts, done[2], done[-2])
+    right3, _ = tie((right3, from2))
+    left3, _ = tie((left3, back2))
+    right4 = ring_send(right3, owners, 1)
+    from3, back3 = hidden_units([right3, left3], own, other, experts)
     done[3], done[-3] = ring_send(from3, owners, -3), ring_send(back3, owners, 3)
 
-    right4, left4, _ = tie((right4, left4, from3))
-    ends = hidden_units([right4, left4], own, other, experts)
-    done[4] = ring_send(jnp.concatenate(ends, axis=0), owners, 4)
+    right4, _, done[2], done[-2] = tie((right4, from3, done[2], done[-2]))
+    (from4,) = hidden_units([right4], own, other, experts)
+    done[4] = ring_send(from4, owners, 4)
+    (done[0],) = hidden_units([packed], own, other, experts)
     places = tuple(sorted(done))
-    return join_units([done[p] for p in places], places)
+    return join_units([done[p] for p in places], places, done[0].shape[1])
 
 
 def block_scale(largest):

time: 46.7 us -> 44 us (0.942)
  waiting for transfers between devices: 8.23 us -> 6.14 us
  starting transfers between devices: 22.9 us -> 21.8 us
    ppermute x15 -> x12, waiting for transfers between devices: 8.22 us -> 5.07 us  [ring_send(): return lax.ppermute(value, ('ep', 'tp'), pairs)]
    ppermute x15 -> x12, starting transfers between devices: 21.8 us -> 20.5 us  [ring_send(): return lax.ppermute(value, ('ep', 'tp'), pairs)]
    ppermute x3 -> x4, waiting for transfers between devices: 0.01 us -> 1.07 us  [swap(): return lax.ppermute(part, 'tp', [(0, 1), (1, 0)])]
    pallas_call x1, Pallas kernels: 3.17 us -> 2.44 us  [begin(): pl.pallas_call(functools.partial(begin_kernel, tiles=tiles, following=fol...]
    pallas_call x2 -> x3, Pallas kernels: 4.07 us -> 4.73 us  [code_weights(): pl.pallas_call(functools.partial(code_kernel, following=following), out_s...]
    pallas_call x4 -> x5, Pallas kernels: 7.3 us -> 7.74 us  [hidden_units(): pl.pallas_call(functools.partial(hidden_kernel, count=len(chunks), pieces...]
    ppermute x3 -> x4, starting transfers between devices: 1.16 us -> 1.31 us  [swap(): return lax.ppermute(part, 'tp', [(0, 1), (1, 0)])]
  transfers between devices with their start and end apart: 18 -> 16, of which waited for: 7 -> 5; matrix products, arithmetic and copies ran while one was open for 0% -> 0% of each run, Pallas kernels for 24% -> 29%
where the time goes in v3:
time: 44 us; the launch traced here: 43.8 us
  starting transfers between devices  21.8 us (50%)
  Pallas kernels  15.8 us (36%)
  waiting for transfers between devices  6.14 us (14%)
    ppermute x12, starting transfers between devices, ring_send(): return lax.ppermute(value, ('ep', 'tp'), pairs)  20.5 us
    pallas_call x5, Pallas kernels, hidden_units(): pl.pallas_call(functools.partial(hidden_kernel, count=len(chunks), pieces...  7.74 us
    ppermute x12, waiting for transfers between devices, ring_send(): return lax.ppermute(value, ('ep', 'tp'), pairs)  5.07 us
    pallas_call x3, Pallas kernels, code_weights(): pl.pallas_call(functools.partial(code_kernel, following=following), out_s...  4.73 us
    pallas_call x1, Pallas kernels, begin(): pl.pallas_call(functools.partial(begin_kernel, tiles=tiles, following=fol...  2.44 us
    ppermute x4, starting transfers between devices, swap(): return lax.ppermute(part, 'tp', [(0, 1), (1, 0)])  1.31 us
    ppermute x4, waiting for transfers between devices, swap(): return lax.ppermute(part, 'tp', [(0, 1), (1, 0)])  1.07 us
  transfers between devices with their start and end apart: 16, of which 5 were waited for; matrix products, arithmetic and copies ran while one was open for 0% of the time, Pallas kernels for 29%

profile of v3, /device:TPU:0, one launch (start us, length us, event | category | flops | bytes accessed | tf_op | source)
XLA Modules:
  0.0 43.8 jit_solution(17367426775823265180)
XLA Ops:
  0.0 2.4 %begin.1 = (bf16[64,1664]{1,0:T(8,128)(2,1)S(1)}, bf16[768,512]{1,0:T(8,128)(2,1)S(1)}, bf16[3,256,768]{2,1,0:T(8,128)(2,1)S(1)}) custom-call(bf16[64,1536]{1,0:T(8,128)(2,1)} %tokens_ref.1, s32[4,64]{1,0:T(4,128)} %bitcast.2, f32[4,64]{1,0:T(4,128)} %bitcast.3, bf16[8,192,768]{2,1,0:T(8,128)(2,1)} %refs_0_.3, bf16[8,192,768]{2,1,0:T(8,128)(2,1)} %refs_1_.3), custom_call_target="tpu_custom_call" | custom-call | flops 1024 | bytes 1024 | tf_op jit(solution)/shard_map/begin/pallas_call | solution.py:164
  2.4 0.5 %collective-permute-start.2 = (bf16[768,512]{1,0:T(8,128)(2,1)S(1)}, bf16[768,512]{1,0:T(8,128)(2,1)S(1)}, u32[]{:S(2)}, u32[]{:S(2)}) collective-permute-start(bf16[768,512]{1,0:T(8,128)(2,1)S(1)} %get-tuple-element.28.refs_2_.refs_1_), channel_id=1, source_target_pairs={{0,1},{1,0},{2,3},{3,2},{4,5},{5,4},{6,7},{7,6},{8,9},{9,8},{10,11... | collective-permute-start | bytes 2359304 | tf_op jit(solution)/shard_map/ppermute | solution.py:319
  3.0 2.6 %collective-permute-start.1 = (bf16[64,1664]{1,0:T(8,128)(2,1)S(1)}, bf16[64,1664]{1,0:T(8,128)(2,1)S(1)}, u32[]{:S(2)}, u32[]{:S(2)}) collective-permute-start(bf16[64,1664]{1,0:T(8,128)(2,1)S(1)} %get-tuple-element.26.refs_0_), channel_id=1, source_target_pairs={{0,2},{4,0},{8,4},{12,8},{14,12},{10,14},{6,10},{2,6},{1,5},{5,9},... | collective-permute-start | bytes 638984 | tf_op jit(solution)/shard_map/ppermute | solution.py:32
  5.7 1.4 %code.3 = (bf16[768,768]{1,0:T(8,128)(2,1)S(1)}, bf16[3,256,768]{2,1,0:T(8,128)(2,1)S(1)}) custom-call(bf16[8,192,768]{2,1,0:T(8,128)(2,1)} %refs_0_.3, bf16[8,192,768]{2,1,0:T(8,128)(2,1)} %refs_1_.3, bf16[3,256,768]{2,1,0:T(8,128)(2,1)S(1)} %get-tuple-element.27.refs_2_, bf16[768,512]{1,0:T(8,128)(2,1)S(1)} %collective-permute-done.2.refs_3_.refs_6_.refs_5_), custom_call_target="tpu_custom_call" | custom-call | flops 1024 | bytes 1024 | tf_op jit(solution)/shard_map/code/pallas_call | solution.py:107
  7.3 1.6 %code.4 = (bf16[768,768]{1,0:T(8,128)(2,1)S(1)}, bf16[4,256,768]{2,1,0:T(8,128)(2,1)S(1)}) custom-call(bf16[8,192,768]{2,1,0:T(8,128)(2,1)} %refs_0_.3, bf16[8,192,768]{2,1,0:T(8,128)(2,1)} %refs_1_.3, bf16[3,256,768]{2,1,0:T(8,128)(2,1)S(1)} %get-tuple-element.29.refs_2_, bf16[768,768]{1,0:T(8,128)(2,1)S(1)} %get-tuple-element.30.refs_3_.refs_2_), custom_call_target="tpu_custom_call" | custom-call | flops 1024 | bytes 1024 | tf_op jit(solution)/shard_map/code/pallas_call | solution.py:107
  8.9 0.5 %collective-permute-start.5 = (bf16[768,768]{1,0:T(8,128)(2,1)S(1)}, bf16[768,768]{1,0:T(8,128)(2,1)S(1)}, u32[]{:S(2)}, u32[]{:S(2)}) collective-permute-start(bf16[768,768]{1,0:T(8,128)(2,1)S(1)} %get-tuple-element.32.refs_1_.refs_4_.refs_3_), channel_id=1, source_target_pairs={{0,1},{1,0},{2,3},{3,2},{4,5},{5,4},{6,7},{7,6},{8,9},{9,8},{10,11... | collective-permute-start | bytes 3538952 | tf_op jit(solution)/shard_map/ppermute | solution.py:319
  9.4 1.7 %code.5.refs_2_.refs_5_.refs_4_ = bf16[768,1024]{1,0:T(8,128)(2,1)S(1)} custom-call(bf16[4,256,768]{2,1,0:T(8,128)(2,1)S(1)} %get-tuple-element.31.refs_0_, bf16[768,768]{1,0:T(8,128)(2,1)S(1)} %get-tuple-element.32.refs_1_.refs_4_.refs_3_), custom_call_target="tpu_custom_call" | custom-call | flops 1024 | bytes 1024 | tf_op jit(solution)/shard_map/code/pallas_call | solution.py:107
  11.4 2.1 %collective-permute-start.3 = (bf16[64,1664]{1,0:T(8,128)(2,1)S(1)}, bf16[64,1664]{1,0:T(8,128)(2,1)S(1)}, u32[]{:S(2)}, u32[]{:S(2)}) collective-permute-start(bf16[64,1664]{1,0:T(8,128)(2,1)S(1)} %collective-permute-done.refs_0_), channel_id=1, source_target_pairs={{0,4},{4,8},{8,12},{12,14},{14,10},{10,6},{6,2},{2,0},{1,3},{5,1},... | collective-permute-start | bytes 638984 | tf_op jit(solution)/shard_map/ppermute | solution.py:32
  13.5 1.1 %collective-permute-done.6.refs_9_.refs_8_ = bf16[768,1024]{1,0:T(8,128)(2,1)S(1)} collective-permute-done((bf16[768,1024]{1,0:T(8,128)(2,1)S(1)}, bf16[768,1024]{1,0:T(8,128)(2,1)S(1)}, u32[]{:S(2)}, u32[]{:S(2)}) %collective-permute-start.6) | collective-permute-done | bytes 1572896 | tf_op jit(solution)/shard_map/ppermute | solution.py:319
  14.6 1.6 %hidden.5 = (bf16[64,192]{1,0:T(8,128)(2,1)S(1)}, bf16[64,192]{1,0:T(8,128)(2,1)S(1)}) custom-call(bf16[64,1664]{1,0:T(8,128)(2,1)S(1)} %collective-permute-done.refs_0_, bf16[64,1664]{1,0:T(8,128)(2,1)S(1)} %collective-permute-done.1.refs_1_, bf16[768,512]{1,0:T(8,128)(2,1)S(1)} %get-tuple-element.28.refs_2_.refs_1_, ...), custom_call_target="tpu_custom_call" | custom-call | flops 12000000000 | bytes 1024 | tf_op jit(solution)/shard_map/hidden/pallas_call | solution.py:238
  16.1 2.5 %collective-permute-done.3.chunk_ref.refs_0_ = bf16[64,1664]{1,0:T(8,128)(2,1)S(1)} collective-permute-done((bf16[64,1664]{1,0:T(8,128)(2,1)S(1)}, bf16[64,1664]{1,0:T(8,128)(2,1)S(1)}, u32[]{:S(2)}, u32[]{:S(2)}) %collective-permute-start.3) | collective-permute-done | bytes 213024 | tf_op jit(solution)/shard_map/ppermute | solution.py:32
  18.6 2.5 %collective-permute-start.7 = (bf16[64,1920]{1,0:T(8,128)(2,1)S(1)}, bf16[64,1920]{1,0:T(8,128)(2,1)S(1)}, u32[]{:S(2)}, u32[]{:S(2)}) collective-permute-start(bf16[64,1920]{1,0:T(8,128)(2,1)S(1)} %attach.2), channel_id=1, source_target_pairs={{0,4},{4,8},{8,12},{12,14},{14,10},{10,6},{6,2},{2,0},{1,3},{5,1},... | collective-permute-start | bytes 737288 | tf_op jit(solution)/shard_map/ppermute | solution.py:32
  21.3 1.6 %hidden.6 = (bf16[64,192]{1,0:T(8,128)(2,1)S(1)}, bf16[64,192]{1,0:T(8,128)(2,1)S(1)}) custom-call(bf16[64,1664]{1,0:T(8,128)(2,1)S(1)} %collective-permute-done.3.chunk_ref.refs_0_, bf16[64,1664]{1,0:T(8,128)(2,1)S(1)} %collective-permute-done.8.refs_1_.chunk_ref, bf16[768,512]{1,0:T(8,128)(2,1)S(1)} %get-tuple-element.28.refs_2_.refs_1_, ...), custom_call_target="tpu_custom_call" | custom-call | flops 12000000000 | bytes 1024 | tf_op jit(solution)/shard_map/hidden/pallas_call | solution.py:238
  22.8 2.9 %collective-permute-start.12 = (bf16[64,192]{1,0:T(8,128)(2,1)S(1)}, bf16[64,192]{1,0:T(8,128)(2,1)S(1)}, u32[]{:S(2)}, u32[]{:S(2)}) collective-permute-start(bf16[64,192]{1,0:T(8,128)(2,1)S(1)} %get-tuple-element.37), channel_id=1, source_target_pairs={{0,6},{4,2},{8,0},{12,4},{14,8},{10,12},{6,14},{2,10},{1,9},{5,13}... | collective-permute-start | bytes 73736 | tf_op jit(solution)/shard_map/ppermute | solution.py:32
  25.7 0.4 collective-permute-start.13
  26.1 1.4 %collective-permute-done.7.refs_0_.refs_2_ = bf16[64,1920]{1,0:T(8,128)(2,1)S(1)} collective-permute-done((bf16[64,1920]{1,0:T(8,128)(2,1)S(1)}, bf16[64,1920]{1,0:T(8,128)(2,1)S(1)}, u32[]{:S(2)}, u32[]{:S(2)}) %collective-permute-start.7) | collective-permute-done | bytes 245792 | tf_op jit(solution)/shard_map/ppermute | solution.py:32
  27.5 1.9 %collective-permute-start.11 = (bf16[64,1920]{1,0:T(8,128)(2,1)S(1)}, bf16[64,1920]{1,0:T(8,128)(2,1)S(1)}, u32[]{:S(2)}, u32[]{:S(2)}) collective-permute-start(bf16[64,1920]{1,0:T(8,128)(2,1)S(1)} %collective-permute-done.7.refs_0_.refs_2_), channel_id=1, source_target_pairs={{0,4},{4,8},{8,12},{12,14},{14,10},{10,6},{6,2},{2,0},{1,3},{5,1},... | collective-permute-start | bytes 737288 | tf_op jit(solution)/shard_map/ppermute | solution.py:32
  29.4 1.6 %hidden.7 = (bf16[64,192]{1,0:T(8,128)(2,1)S(1)}, bf16[64,192]{1,0:T(8,128)(2,1)S(1)}) custom-call(bf16[64,1920]{1,0:T(8,128)(2,1)S(1)} %collective-permute-done.7.refs_0_.refs_2_, bf16[64,1920]{1,0:T(8,128)(2,1)S(1)} %collective-permute-done.9.refs_1_.refs_4_, bf16[768,512]{1,0:T(8,128)(2,1)S(1)} %get-tuple-element.28.refs_2_.refs_1_, ...), custom_call_target="tpu_custom_call" | custom-call | flops 12000000000 | bytes 1024 | tf_op jit(solution)/shard_map/hidden/pallas_call | solution.py:238
  30.9 3.5 %collective-permute-start.10 = (bf16[64,192]{1,0:T(8,128)(2,1)S(1)}, bf16[64,192]{1,0:T(8,128)(2,1)S(1)}, u32[]{:S(2)}, u32[]{:S(2)}) collective-permute-start(bf16[64,192]{1,0:T(8,128)(2,1)S(1)} %get-tuple-element.42), channel_id=1, source_target_pairs={{0,12},{4,14},{8,10},{12,6},{14,2},{10,0},{6,4},{2,8},{1,11},{5,7}... | collective-permute-start | bytes 73736 | tf_op jit(solution)/shard_map/ppermute | solution.py:32
  34.8 1.5 %hidden.9 = bf16[64,192]{1,0:T(8,128)(2,1)S(1)} custom-call(bf16[64,1920]{1,0:T(8,128)(2,1)S(1)} %collective-permute-done.11.refs_0_, bf16[768,512]{1,0:T(8,128)(2,1)S(1)} %get-tuple-element.28.refs_2_.refs_1_, bf16[768,768]{1,0:T(8,128)(2,1)S(1)} %get-tuple-element.30.refs_3_.refs_2_, bf16[768,768]{1,0:T(8,128)(2,1)S(1)} %get-tuple-element.32.refs_1_.refs_4_.refs_3_, ...), custom_call_target="tpu_custom_call" | custom-call | flops 12000000000 | bytes 1024 | tf_op jit(solution)/shard_map/hidden/pallas_call | solution.py:238
  36.3 4.1 %collective-permute-start.15 = (bf16[64,192]{1,0:T(8,128)(2,1)S(1)}, bf16[64,192]{1,0:T(8,128)(2,1)S(1)}, u32[]{:S(2)}, u32[]{:S(2)}) collective-permute-start(bf16[64,192]{1,0:T(8,128)(2,1)S(1)} %hidden.9), channel_id=1, source_target_pairs={{0,14},{4,10},{8,6},{12,2},{14,0},{10,4},{6,8},{2,12},{1,15},{5,11... | collective-permute-start | bytes 73736 | tf_op jit(solution)/shard_map/ppermute | solution.py:32
  40.4 1.5 %hidden.8.refs_3_ = bf16[64,192]{1,0:T(8,128)(2,1)S(1)} custom-call(bf16[64,1664]{1,0:T(8,128)(2,1)S(1)} %get-tuple-element.26.refs_0_, bf16[768,512]{1,0:T(8,128)(2,1)S(1)} %get-tuple-element.28.refs_2_.refs_1_, bf16[768,768]{1,0:T(8,128)(2,1)S(1)} %get-tuple-element.30.refs_3_.refs_2_, bf16[768,768]{1,0:T(8,128)(2,1)S(1)} %get-tuple-element.32.refs_1_.refs_4_.refs_3_, ...), custom_call_target="tpu_custom_call" | custom-call | flops 12000000000 | bytes 1024 | tf_op jit(solution)/shard_map/hidden/pallas_call | solution.py:238
  42.0 1.1 %collective-permute-done.15.refs_7_ = bf16[64,192]{1,0:T(8,128)(2,1)S(1)} collective-permute-done((bf16[64,192]{1,0:T(8,128)(2,1)S(1)}, bf16[64,192]{1,0:T(8,128)(2,1)S(1)}, u32[]{:S(2)}, u32[]{:S(2)}) %collective-permute-start.15) | collective-permute-done | bytes 24608 | tf_op jit(solution)/shard_map/ppermute | solution.py:32
  43.0 0.8 %join.1 = bf16[64,1536]{1,0:T(8,128)(2,1)} custom-call(bf16[64,192]{1,0:T(8,128)(2,1)S(1)} %collective-permute-done.10.refs_0_, bf16[64,192]{1,0:T(8,128)(2,1)S(1)} %collective-permute-done.13.refs_1_, bf16[64,1920]{1,0:T(8,128)(2,1)S(1)} %collective-permute-done.7.refs_0_.refs_2_, bf16[64,192]{1,0:T(8,128)(2,1)S(1)} %hidden.8.refs_3_, ...), custom_call_target="tpu_custom_call" | custom-call | tf_op jit(solution)/shard_map/join/pallas_call | solution.py:266
  (21 shorter events, 1.1 us)
Async XLA Ops:
  2.4 3.2 %collective-permute-start.2 = (bf16[768,512]{1,0:T(8,128)(2,1)S(1)}, bf16[768,512]{1,0:T(8,128)(2,1)S(1)}, u32[]{:S(2)}, u32[]{:S(2)}) collective-permute-start(bf16[768,512]{1,0:T(8,128)(2,1)S(1)} %get-tuple-element.28.refs_2_.refs_1_), channel_id=1, source_target_pairs={{0,1},{1,0},{2,3},{3,2},{4,5},{5,4},{6,7},{7,6},{8,9},{9,8},{10,11... | collective-permute-start | bytes 2359304 | tf_op jit(solution)/shard_map/ppermute | solution.py:319
  3.0 8.3 %collective-permute-start.1 = (bf16[64,1664]{1,0:T(8,128)(2,1)S(1)}, bf16[64,1664]{1,0:T(8,128)(2,1)S(1)}, u32[]{:S(2)}, u32[]{:S(2)}) collective-permute-start(bf16[64,1664]{1,0:T(8,128)(2,1)S(1)} %get-tuple-element.26.refs_0_), channel_id=1, source_target_pairs={{0,2},{4,0},{8,4},{12,8},{14,12},{10,14},{6,10},{2,6},{1,5},{5,9},... | collective-permute-start | bytes 638984 | tf_op jit(solution)/shard_map/ppermute | solution.py:32
  5.5 5.9 %collective-permute-start = (bf16[64,1664]{1,0:T(8,128)(2,1)S(1)}, bf16[64,1664]{1,0:T(8,128)(2,1)S(1)}, u32[]{:S(2)}, u32[]{:S(2)}) collective-permute-start(bf16[64,1664]{1,0:T(8,128)(2,1)S(1)} %get-tuple-element.26.refs_0_), channel_id=1, source_target_pairs={{0,4},{4,8},{8,12},{12,14},{14,10},{10,6},{6,2},{2,0},{1,3},{5,1},... | collective-permute-start | bytes 638984 | tf_op jit(solution)/shard_map/ppermute | solution.py:32
  7.1 6.4 %collective-permute-start.4 = (bf16[768,768]{1,0:T(8,128)(2,1)S(1)}, bf16[768,768]{1,0:T(8,128)(2,1)S(1)}, u32[]{:S(2)}, u32[]{:S(2)}) collective-permute-start(bf16[768,768]{1,0:T(8,128)(2,1)S(1)} %get-tuple-element.30.refs_3_.refs_2_), channel_id=1, source_target_pairs={{0,1},{1,0},{2,3},{3,2},{4,5},{5,4},{6,7},{7,6},{8,9},{9,8},{10,11... | collective-permute-start | bytes 3538952 | tf_op jit(solution)/shard_map/ppermute | solution.py:319
  8.9 4.6 %collective-permute-start.5 = (bf16[768,768]{1,0:T(8,128)(2,1)S(1)}, bf16[768,768]{1,0:T(8,128)(2,1)S(1)}, u32[]{:S(2)}, u32[]{:S(2)}) collective-permute-start(bf16[768,768]{1,0:T(8,128)(2,1)S(1)} %get-tuple-element.32.refs_1_.refs_4_.refs_3_), channel_id=1, source_target_pairs={{0,1},{1,0},{2,3},{3,2},{4,5},{5,4},{6,7},{7,6},{8,9},{9,8},{10,11... | collective-permute-start | bytes 3538952 | tf_op jit(solution)/shard_map/ppermute | solution.py:319
  11.1 3.5 %collective-permute-start.6 = (bf16[768,1024]{1,0:T(8,128)(2,1)S(1)}, bf16[768,1024]{1,0:T(8,128)(2,1)S(1)}, u32[]{:S(2)}, u32[]{:S(2)}) collective-permute-start(bf16[768,1024]{1,0:T(8,128)(2,1)S(1)} %code.5.refs_2_.refs_5_.refs_4_), channel_id=1, source_target_pairs={{0,1},{1,0},{2,3},{3,2},{4,5},{5,4},{6,7},{7,6},{8,9},{9,8},{10,11... | collective-permute-start | bytes 4718600 | tf_op jit(solution)/shard_map/ppermute | solution.py:319
  11.4 7.2 %collective-permute-start.3 = (bf16[64,1664]{1,0:T(8,128)(2,1)S(1)}, bf16[64,1664]{1,0:T(8,128)(2,1)S(1)}, u32[]{:S(2)}, u32[]{:S(2)}) collective-permute-start(bf16[64,1664]{1,0:T(8,128)(2,1)S(1)} %collective-permute-done.refs_0_), channel_id=1, source_target_pairs={{0,4},{4,8},{8,12},{12,14},{14,10},{10,6},{6,2},{2,0},{1,3},{5,1},... | collective-permute-start | bytes 638984 | tf_op jit(solution)/shard_map/ppermute | solution.py:32
  13.5 7.7 %collective-permute-start.8 = (bf16[64,1664]{1,0:T(8,128)(2,1)S(1)}, bf16[64,1664]{1,0:T(8,128)(2,1)S(1)}, u32[]{:S(2)}, u32[]{:S(2)}) collective-permute-start(bf16[64,1664]{1,0:T(8,128)(2,1)S(1)} %collective-permute-done.1.refs_1_), channel_id=1, source_target_pairs={{0,2},{4,0},{8,4},{12,8},{14,12},{10,14},{6,10},{2,6},{1,5},{5,9},... | collective-permute-start | bytes 638984 | tf_op jit(solution)/shard_map/ppermute | solution.py:32
  18.6 8.8 %collective-permute-start.7 = (bf16[64,1920]{1,0:T(8,128)(2,1)S(1)}, bf16[64,1920]{1,0:T(8,128)(2,1)S(1)}, u32[]{:S(2)}, u32[]{:S(2)}) collective-permute-start(bf16[64,1920]{1,0:T(8,128)(2,1)S(1)} %attach.2), channel_id=1, source_target_pairs={{0,4},{4,8},{8,12},{12,14},{14,10},{10,6},{6,2},{2,0},{1,3},{5,1},... | collective-permute-start | bytes 737288 | tf_op jit(solution)/shard_map/ppermute | solution.py:32
  21.2 8.2 %collective-permute-start.9 = (bf16[64,1920]{1,0:T(8,128)(2,1)S(1)}, bf16[64,1920]{1,0:T(8,128)(2,1)S(1)}, u32[]{:S(2)}, u32[]{:S(2)}) collective-permute-start(bf16[64,1920]{1,0:T(8,128)(2,1)S(1)} %attach.3), channel_id=1, source_target_pairs={{0,2},{4,0},{8,4},{12,8},{14,12},{10,14},{6,10},{2,6},{1,5},{5,9},... | collective-permute-start | bytes 737288 | tf_op jit(solution)/shard_map/ppermute | solution.py:32
  22.8 12.0 %collective-permute-start.12 = (bf16[64,192]{1,0:T(8,128)(2,1)S(1)}, bf16[64,192]{1,0:T(8,128)(2,1)S(1)}, u32[]{:S(2)}, u32[]{:S(2)}) collective-permute-start(bf16[64,192]{1,0:T(8,128)(2,1)S(1)} %get-tuple-element.37), channel_id=1, source_target_pairs={{0,6},{4,2},{8,0},{12,4},{14,8},{10,12},{6,14},{2,10},{1,9},{5,13}... | collective-permute-start | bytes 73736 | tf_op jit(solution)/shard_map/ppermute | solution.py:32
  25.7 9.1 %collective-permute-start.13 = (bf16[64,192]{1,0:T(8,128)(2,1)S(1)}, bf16[64,192]{1,0:T(8,128)(2,1)S(1)}, u32[]{:S(2)}, u32[]{:S(2)}) collective-permute-start(bf16[64,192]{1,0:T(8,128)(2,1)S(1)} %get-tuple-element.40), channel_id=1, source_target_pairs={{0,8},{4,12},{8,14},{12,10},{14,6},{10,2},{6,0},{2,4},{1,7},{5,3},... | collective-permute-start | bytes 73736 | tf_op jit(solution)/shard_map/ppermute | solution.py:32
  27.5 7.4 %collective-permute-start.11 = (bf16[64,1920]{1,0:T(8,128)(2,1)S(1)}, bf16[64,1920]{1,0:T(8,128)(2,1)S(1)}, u32[]{:S(2)}, u32[]{:S(2)}) collective-permute-start(bf16[64,1920]{1,0:T(8,128)(2,1)S(1)} %collective-permute-done.7.refs_0_.refs_2_), channel_id=1, source_target_pairs={{0,4},{4,8},{8,12},{12,14},{14,10},{10,6},{6,2},{2,0},{1,3},{5,1},... | collective-permute-start | bytes 737288 | tf_op jit(solution)/shard_map/ppermute | solution.py:32
  30.9 11.0 %collective-permute-start.10 = (bf16[64,192]{1,0:T(8,128)(2,1)S(1)}, bf16[64,192]{1,0:T(8,128)(2,1)S(1)}, u32[]{:S(2)}, u32[]{:S(2)}) collective-permute-start(bf16[64,192]{1,0:T(8,128)(2,1)S(1)} %get-tuple-element.42), channel_id=1, source_target_pairs={{0,12},{4,14},{8,10},{12,6},{14,2},{10,0},{6,4},{2,8},{1,11},{5,7}... | collective-permute-start | bytes 73736 | tf_op jit(solution)/shard_map/ppermute | solution.py:32
  34.5 7.5 %collective-permute-start.14 = (bf16[64,192]{1,0:T(8,128)(2,1)S(1)}, bf16[64,192]{1,0:T(8,128)(2,1)S(1)}, u32[]{:S(2)}, u32[]{:S(2)}) collective-permute-start(bf16[64,192]{1,0:T(8,128)(2,1)S(1)} %get-tuple-element.43), channel_id=1, source_target_pairs={{0,10},{4,6},{8,2},{12,0},{14,4},{10,8},{6,12},{2,14},{1,13},{5,15... | collective-permute-start | bytes 73736 | tf_op jit(solution)/shard_map/ppermute | solution.py:32
  36.3 6.7 %collective-permute-start.15 = (bf16[64,192]{1,0:T(8,128)(2,1)S(1)}, bf16[64,192]{1,0:T(8,128)(2,1)S(1)}, u32[]{:S(2)}, u32[]{:S(2)}) collective-permute-start(bf16[64,192]{1,0:T(8,128)(2,1)S(1)} %hidden.9), channel_id=1, source_target_pairs={{0,14},{4,10},{8,6},{12,2},{14,0},{10,4},{6,8},{2,12},{1,15},{5,11... | collective-permute-start | bytes 73736 | tf_op jit(solution)/shard_map/ppermute | solution.py:32

commit v4 on v3

--- a/solution.py
+++ b/solution.py
@@ -255,8 +255,13 @@
     sign = 1 - 2 * lax.axis_index("tp")
     units = held.shape[2]
     for block, step in zip(blocks, steps):
-        first = max(block.shape[1] - 2 * LANES, 0)
-        held[ring_owner((place + sign * step + owners) % owners, owners)] = block[:, first : first + units]
+        source = ring_owner((place + sign * step + owners) % owners, owners)
+        width = block.shape[1]
+        if width == units:
+            held[source] = block[...]
+        else:
+            held[source, :, :LANES] = block[:, width - LANES :]
+            held[source, :, LANES:] = block[:, width - LANES - LANES // 2 : width - LANES]
     for owner in range(owners):
         out_ref[:, owner * units : (owner + 1) * units] = held[owner]
 
@@ -275,17 +280,18 @@
 
 
 def attach_kernel(chunk_ref, block_ref, out_ref):
-    width, units = chunk_ref.shape[1], block_ref.shape[1]
-    out_ref[:, :width] = chunk_ref[...]
-    out_ref[:, width : width + units] = block_ref[...]
-    out_ref[:, width + units :] = jnp.zeros((out_ref.shape[0], 2 * LANES - units), out_ref.dtype)
+    width = chunk_ref.shape[1]
+    out_ref[:, : width - LANES] = chunk_ref[:, : width - LANES]
+    beside = [chunk_ref[:, width - LANES : width - LANES // 2], block_ref[:, LANES:]]
+    out_ref[:, width - LANES : width] = jnp.concatenate(beside, axis=1)
+    out_ref[:, width:] = block_ref[:, :LANES]
 
 
 def attach(chunk, block):
     rows, width = chunk.shape
     return pl.pallas_call(
         attach_kernel,
-        out_shape=jax.ShapeDtypeStruct((rows, width + 2 * LANES), chunk.dtype),
+        out_shape=jax.ShapeDtypeStruct((rows, width + LANES), chunk.dtype),
         in_specs=[pl.BlockSpec(memory_space=pltpu.VMEM)] * 2,
         out_specs=pl.BlockSpec(memory_space=pltpu.VMEM),
         compiler_params=pltpu.CompilerParams(vmem_limit_bytes=4 << 20),
@@ -322,7 +328,7 @@
         return ring_send(right, owners, 1), ring_send(left, owners, -1)
 
     tiles = tuple(range(experts * 3 // 2))
-    parts = tiles[:2], tiles[2:5], tiles[5:8], tiles[8:]
+    parts = tiles[:1], tiles[1:6], tiles[6:]
     packed, first, rest = begin(tokens, expert_ids, combine_weights, gate_weight, up_weight, *parts[:2])
     right1, left1 = onward(packed, packed)
     own, other = [first], [swap(first)]

time: 44 us -> 42.6 us (0.968)
  starting transfers between devices: 21.8 us -> 21.1 us
  waiting for transfers between devices: 6.14 us -> 5.61 us
    ppermute x12, waiting for transfers between devices: 5.07 us -> 3.51 us  [ring_send(): return lax.ppermute(value, ('ep', 'tp'), pairs)]
    ppermute x4 -> x3, waiting for transfers between devices: 1.07 us -> 2.1 us  [swap(): return lax.ppermute(part, 'tp', [(0, 1), (1, 0)])]
    ppermute x12, starting transfers between devices: 20.5 us -> 20 us  [ring_send(): return lax.ppermute(value, ('ep', 'tp'), pairs)]
    pallas_call x3 -> x2, Pallas kernels: 4.73 us -> 4.96 us  [code_weights(): pl.pallas_call(functools.partial(code_kernel, following=following), out_s...]
    ppermute x4 -> x3, starting transfers between devices: 1.31 us -> 1.16 us  [swap(): return lax.ppermute(part, 'tp', [(0, 1), (1, 0)])]
  transfers between devices with their start and end apart: 16 -> 15, of which waited for: 5 -> 5; matrix products, arithmetic and copies ran while one was open for 0% -> 0% of each run, Pallas kernels for 29% -> 30%
where the time goes in v4:
time: 42.6 us; the launch traced here: 42.5 us
  starting transfers between devices  21.1 us (50%)
  Pallas kernels  15.7 us (37%)
  waiting for transfers between devices  5.61 us (13%)
    ppermute x12, starting transfers between devices, ring_send(): return lax.ppermute(value, ('ep', 'tp'), pairs)  20 us
    pallas_call x5, Pallas kernels, hidden_units(): pl.pallas_call(functools.partial(hidden_kernel, count=len(chunks), pieces...  7.53 us
    pallas_call x2, Pallas kernels, code_weights(): pl.pallas_call(functools.partial(code_kernel, following=following), out_s...  4.96 us
    ppermute x12, waiting for transfers between devices, ring_send(): return lax.ppermute(value, ('ep', 'tp'), pairs)  3.51 us
    pallas_call x1, Pallas kernels, begin(): pl.pallas_call(functools.partial(begin_kernel, tiles=tiles, following=fol...  2.16 us
    ppermute x3, waiting for transfers between devices, swap(): return lax.ppermute(part, 'tp', [(0, 1), (1, 0)])  2.1 us
    ppermute x3, starting transfers between devices, swap(): return lax.ppermute(part, 'tp', [(0, 1), (1, 0)])  1.16 us
    pallas_call x1, Pallas kernels, join_units(): pl.pallas_call(functools.partial(join_kernel, steps=steps), out_shape=jax...  0.87 us
  transfers between devices with their start and end apart: 15, of which 5 were waited for; matrix products, arithmetic and copies ran while one was open for 0% of the time, Pallas kernels for 30%

profile of v4, /device:TPU:0, one launch (start us, length us, event | category | flops | bytes accessed | tf_op | source)
XLA Modules:
  0.0 42.5 jit_solution(17638404882070174255)
XLA Ops:
  0.0 2.2 %begin.1 = (bf16[64,1664]{1,0:T(8,128)(2,1)S(1)}, bf16[768,256]{1,0:T(8,128)(2,1)S(1)}, bf16[5,256,768]{2,1,0:T(8,128)(2,1)S(1)}) custom-call(bf16[64,1536]{1,0:T(8,128)(2,1)} %tokens_ref.1, s32[4,64]{1,0:T(4,128)} %bitcast.2, f32[4,64]{1,0:T(4,128)} %bitcast.3, bf16[8,192,768]{2,1,0:T(8,128)(2,1)} %refs_0_.1, bf16[8,192,768]{2,1,0:T(8,128)(2,1)} %refs_1_.1), custom_call_target="tpu_custom_call" | custom-call | flops 1024 | bytes 1024 | tf_op jit(solution)/shard_map/begin/pallas_call | solution.py:164
  2.2 0.5 %collective-permute-start.2 = (bf16[768,256]{1,0:T(8,128)(2,1)S(1)}, bf16[768,256]{1,0:T(8,128)(2,1)S(1)}, u32[]{:S(2)}, u32[]{:S(2)}) collective-permute-start(bf16[768,256]{1,0:T(8,128)(2,1)S(1)} %get-tuple-element.26.refs_2_.refs_1_), channel_id=1, source_target_pairs={{0,1},{1,0},{2,3},{3,2},{4,5},{5,4},{6,7},{7,6},{8,9},{9,8},{10,11... | collective-permute-start | bytes 1179656 | tf_op jit(solution)/shard_map/ppermute | solution.py:325
  2.7 2.6 %collective-permute-start.1 = (bf16[64,1664]{1,0:T(8,128)(2,1)S(1)}, bf16[64,1664]{1,0:T(8,128)(2,1)S(1)}, u32[]{:S(2)}, u32[]{:S(2)}) collective-permute-start(bf16[64,1664]{1,0:T(8,128)(2,1)S(1)} %get-tuple-element.24.refs_0_), channel_id=1, source_target_pairs={{0,2},{4,0},{8,4},{12,8},{14,12},{10,14},{6,10},{2,6},{1,5},{5,9},... | collective-permute-start | bytes 638984 | tf_op jit(solution)/shard_map/ppermute | solution.py:32
  5.2 0.2 collective-permute-start
  5.4 2.4 %code.2 = (bf16[768,1280]{1,0:T(8,128)(2,1)S(1)}, bf16[6,256,768]{2,1,0:T(8,128)(2,1)S(1)}) custom-call(bf16[8,192,768]{2,1,0:T(8,128)(2,1)} %refs_0_.1, bf16[8,192,768]{2,1,0:T(8,128)(2,1)} %refs_1_.1, bf16[5,256,768]{2,1,0:T(8,128)(2,1)S(1)} %get-tuple-element.25.refs_2_, bf16[768,256]{1,0:T(8,128)(2,1)S(1)} %collective-permute-done.2.refs_3_.refs_5_.refs_4_), custom_call_target="tpu_custom_call" | custom-call | flops 1024 | bytes 1024 | tf_op jit(solution)/shard_map/code/pallas_call | solution.py:107
  8.0 2.6 %code.3.refs_2_.refs_4_.refs_3_ = bf16[768,1536]{1,0:T(8,128)(2,1)S(1)} custom-call(bf16[6,256,768]{2,1,0:T(8,128)(2,1)S(1)} %get-tuple-element.27.refs_0_, bf16[768,1280]{1,0:T(8,128)(2,1)S(1)} %get-tuple-element.28.refs_1_.refs_3_.refs_2_), custom_call_target="tpu_custom_call" | custom-call | flops 1024 | bytes 1024 | tf_op jit(solution)/shard_map/code/pallas_call | solution.py:107
  10.5 0.5 %collective-permute-start.5 = (bf16[768,1536]{1,0:T(8,128)(2,1)S(1)}, bf16[768,1536]{1,0:T(8,128)(2,1)S(1)}, u32[]{:S(2)}, u32[]{:S(2)}) collective-permute-start(bf16[768,1536]{1,0:T(8,128)(2,1)S(1)} %code.3.refs_2_.refs_4_.refs_3_), channel_id=1, source_target_pairs={{0,1},{1,0},{2,3},{3,2},{4,5},{5,4},{6,7},{7,6},{8,9},{9,8},{10,11... | collective-permute-start | bytes 7077896 | tf_op jit(solution)/shard_map/ppermute | solution.py:325
  11.1 1.9 %collective-permute-start.3 = (bf16[64,1664]{1,0:T(8,128)(2,1)S(1)}, bf16[64,1664]{1,0:T(8,128)(2,1)S(1)}, u32[]{:S(2)}, u32[]{:S(2)}) collective-permute-start(bf16[64,1664]{1,0:T(8,128)(2,1)S(1)} %collective-permute-done.refs_0_), channel_id=1, source_target_pairs={{0,4},{4,8},{8,12},{12,14},{14,10},{10,6},{6,2},{2,0},{1,3},{5,1},... | collective-permute-start | bytes 638984 | tf_op jit(solution)/shard_map/ppermute | solution.py:32
  13.1 2.1 %collective-permute-done.5.refs_7_.refs_6_ = bf16[768,1536]{1,0:T(8,128)(2,1)S(1)} collective-permute-done((bf16[768,1536]{1,0:T(8,128)(2,1)S(1)}, bf16[768,1536]{1,0:T(8,128)(2,1)S(1)}, u32[]{:S(2)}, u32[]{:S(2)}) %collective-permute-start.5) | collective-permute-done | bytes 2359328 | tf_op jit(solution)/shard_map/ppermute | solution.py:325
  15.2 1.5 %hidden.5 = (bf16[64,192]{1,0:T(8,128)(2,1)S(1)}, bf16[64,192]{1,0:T(8,128)(2,1)S(1)}) custom-call(bf16[64,1664]{1,0:T(8,128)(2,1)S(1)} %collective-permute-done.refs_0_, bf16[64,1664]{1,0:T(8,128)(2,1)S(1)} %collective-permute-done.1.refs_1_, bf16[768,256]{1,0:T(8,128)(2,1)S(1)} %get-tuple-element.26.refs_2_.refs_1_, ...), custom_call_target="tpu_custom_call" | custom-call | flops 12000000000 | bytes 1024 | tf_op jit(solution)/shard_map/hidden/pallas_call | solution.py:238
  16.7 1.9 %collective-permute-done.3.chunk_ref.refs_0_ = bf16[64,1664]{1,0:T(8,128)(2,1)S(1)} collective-permute-done((bf16[64,1664]{1,0:T(8,128)(2,1)S(1)}, bf16[64,1664]{1,0:T(8,128)(2,1)S(1)}, u32[]{:S(2)}, u32[]{:S(2)}) %collective-permute-start.3) | collective-permute-done | bytes 213024 | tf_op jit(solution)/shard_map/ppermute | solution.py:32
  18.7 1.8 %collective-permute-start.6 = (bf16[64,1792]{1,0:T(8,128)(2,1)S(1)}, bf16[64,1792]{1,0:T(8,128)(2,1)S(1)}, u32[]{:S(2)}, u32[]{:S(2)}) collective-permute-start(bf16[64,1792]{1,0:T(8,128)(2,1)S(1)} %attach.2), channel_id=1, source_target_pairs={{0,4},{4,8},{8,12},{12,14},{14,10},{10,6},{6,2},{2,0},{1,3},{5,1},... | collective-permute-start | bytes 688136 | tf_op jit(solution)/shard_map/ppermute | solution.py:32
  20.6 0.4 collective-permute-start.8
  21.0 1.5 %hidden.6 = (bf16[64,192]{1,0:T(8,128)(2,1)S(1)}, bf16[64,192]{1,0:T(8,128)(2,1)S(1)}) custom-call(bf16[64,1664]{1,0:T(8,128)(2,1)S(1)} %collective-permute-done.3.chunk_ref.refs_0_, bf16[64,1664]{1,0:T(8,128)(2,1)S(1)} %collective-permute-done.7.refs_1_.chunk_ref, bf16[768,256]{1,0:T(8,128)(2,1)S(1)} %get-tuple-element.26.refs_2_.refs_1_, ...), custom_call_target="tpu_custom_call" | custom-call | flops 12000000000 | bytes 1024 | tf_op jit(solution)/shard_map/hidden/pallas_call | solution.py:238
  22.5 3.1 %collective-permute-start.11 = (bf16[64,192]{1,0:T(8,128)(2,1)S(1)}, bf16[64,192]{1,0:T(8,128)(2,1)S(1)}, u32[]{:S(2)}, u32[]{:S(2)}) collective-permute-start(bf16[64,192]{1,0:T(8,128)(2,1)S(1)} %get-tuple-element.33), channel_id=1, source_target_pairs={{0,6},{4,2},{8,0},{12,4},{14,8},{10,12},{6,14},{2,10},{1,9},{5,13}... | collective-permute-start | bytes 73736 | tf_op jit(solution)/shard_map/ppermute | solution.py:32
  25.6 1.1 %collective-permute-done.6.refs_0_.refs_2_ = bf16[64,1792]{1,0:T(8,128)(2,1)S(1)} collective-permute-done((bf16[64,1792]{1,0:T(8,128)(2,1)S(1)}, bf16[64,1792]{1,0:T(8,128)(2,1)S(1)}, u32[]{:S(2)}, u32[]{:S(2)}) %collective-permute-start.6) | collective-permute-done | bytes 229408 | tf_op jit(solution)/shard_map/ppermute | solution.py:32
  26.8 1.2 %collective-permute-start.10 = (bf16[64,1792]{1,0:T(8,128)(2,1)S(1)}, bf16[64,1792]{1,0:T(8,128)(2,1)S(1)}, u32[]{:S(2)}, u32[]{:S(2)}) collective-permute-start(bf16[64,1792]{1,0:T(8,128)(2,1)S(1)} %collective-permute-done.6.refs_0_.refs_2_), channel_id=1, source_target_pairs={{0,4},{4,8},{8,12},{12,14},{14,10},{10,6},{6,2},{2,0},{1,3},{5,1},... | collective-permute-start | bytes 688136 | tf_op jit(solution)/shard_map/ppermute | solution.py:32
  28.0 1.5 %hidden.7 = (bf16[64,192]{1,0:T(8,128)(2,1)S(1)}, bf16[64,192]{1,0:T(8,128)(2,1)S(1)}) custom-call(bf16[64,1792]{1,0:T(8,128)(2,1)S(1)} %collective-permute-done.6.refs_0_.refs_2_, bf16[64,1792]{1,0:T(8,128)(2,1)S(1)} %collective-permute-done.8.refs_1_.refs_4_, bf16[768,256]{1,0:T(8,128)(2,1)S(1)} %get-tuple-element.26.refs_2_.refs_1_, ...), custom_call_target="tpu_custom_call" | custom-call | flops 12000000000 | bytes 1024 | tf_op jit(solution)/shard_map/hidden/pallas_call | solution.py:238
  29.5 3.9 %collective-permute-start.9 = (bf16[64,192]{1,0:T(8,128)(2,1)S(1)}, bf16[64,192]{1,0:T(8,128)(2,1)S(1)}, u32[]{:S(2)}, u32[]{:S(2)}) collective-permute-start(bf16[64,192]{1,0:T(8,128)(2,1)S(1)} %get-tuple-element.38), channel_id=1, source_target_pairs={{0,12},{4,14},{8,10},{12,6},{14,2},{10,0},{6,4},{2,8},{1,11},{5,7}... | collective-permute-start | bytes 73736 | tf_op jit(solution)/shard_map/ppermute | solution.py:32
  33.4 1.5 %hidden.9 = bf16[64,192]{1,0:T(8,128)(2,1)S(1)} custom-call(bf16[64,1792]{1,0:T(8,128)(2,1)S(1)} %collective-permute-done.10.refs_0_, bf16[768,256]{1,0:T(8,128)(2,1)S(1)} %get-tuple-element.26.refs_2_.refs_1_, bf16[768,1280]{1,0:T(8,128)(2,1)S(1)} %get-tuple-element.28.refs_1_.refs_3_.refs_2_, bf16[768,1536]{1,0:T(8,128)(2,1)S(1)} %code.3.refs_2_.refs_4_.refs_3_, ...), custom_call_target="tpu_custom_call" | custom-call | flops 12000000000 | bytes 1024 | tf_op jit(solution)/shard_map/hidden/pallas_call | solution.py:238
  34.9 4.8 %collective-permute-start.14 = (bf16[64,192]{1,0:T(8,128)(2,1)S(1)}, bf16[64,192]{1,0:T(8,128)(2,1)S(1)}, u32[]{:S(2)}, u32[]{:S(2)}) collective-permute-start(bf16[64,192]{1,0:T(8,128)(2,1)S(1)} %hidden.9), channel_id=1, source_target_pairs={{0,14},{4,10},{8,6},{12,2},{14,0},{10,4},{6,8},{2,12},{1,15},{5,11... | collective-permute-start | bytes 73736 | tf_op jit(solution)/shard_map/ppermute | solution.py:32
  39.7 1.5 %hidden.8.refs_3_ = bf16[64,192]{1,0:T(8,128)(2,1)S(1)} custom-call(bf16[64,1664]{1,0:T(8,128)(2,1)S(1)} %get-tuple-element.24.refs_0_, bf16[768,256]{1,0:T(8,128)(2,1)S(1)} %get-tuple-element.26.refs_2_.refs_1_, bf16[768,1280]{1,0:T(8,128)(2,1)S(1)} %get-tuple-element.28.refs_1_.refs_3_.refs_2_, bf16[768,1536]{1,0:T(8,128)(2,1)S(1)} %code.3.refs_2_.refs_4_.refs_3_, ...), custom_call_target="tpu_custom_call" | custom-call | flops 12000000000 | bytes 1024 | tf_op jit(solution)/shard_map/hidden/pallas_call | solution.py:238
  41.2 0.4 collective-permute-done.14.refs_7_
  41.6 0.9 %join.1 = bf16[64,1536]{1,0:T(8,128)(2,1)} custom-call(bf16[64,192]{1,0:T(8,128)(2,1)S(1)} %collective-permute-done.9.refs_0_, bf16[64,192]{1,0:T(8,128)(2,1)S(1)} %collective-permute-done.12.refs_1_, bf16[64,1792]{1,0:T(8,128)(2,1)S(1)} %collective-permute-done.6.refs_0_.refs_2_, bf16[64,192]{1,0:T(8,128)(2,1)S(1)} %hidden.8.refs_3_, ...), custom_call_target="tpu_custom_call" | custom-call | tf_op jit(solution)/shard_map/join/pallas_call | solution.py:271
  (18 shorter events, 0.5 us)
Async XLA Ops:
  2.2 3.2 %collective-permute-start.2 = (bf16[768,256]{1,0:T(8,128)(2,1)S(1)}, bf16[768,256]{1,0:T(8,128)(2,1)S(1)}, u32[]{:S(2)}, u32[]{:S(2)}) collective-permute-start(bf16[768,256]{1,0:T(8,128)(2,1)S(1)} %get-tuple-element.26.refs_2_.refs_1_), channel_id=1, source_target_pairs={{0,1},{1,0},{2,3},{3,2},{4,5},{5,4},{6,7},{7,6},{8,9},{9,8},{10,11... | collective-permute-start | bytes 1179656 | tf_op jit(solution)/shard_map/ppermute | solution.py:325
  2.7 8.3 %collective-permute-start.1 = (bf16[64,1664]{1,0:T(8,128)(2,1)S(1)}, bf16[64,1664]{1,0:T(8,128)(2,1)S(1)}, u32[]{:S(2)}, u32[]{:S(2)}) collective-permute-start(bf16[64,1664]{1,0:T(8,128)(2,1)S(1)} %get-tuple-element.24.refs_0_), channel_id=1, source_target_pairs={{0,2},{4,0},{8,4},{12,8},{14,12},{10,14},{6,10},{2,6},{1,5},{5,9},... | collective-permute-start | bytes 638984 | tf_op jit(solution)/shard_map/ppermute | solution.py:32
  5.2 5.9 %collective-permute-start = (bf16[64,1664]{1,0:T(8,128)(2,1)S(1)}, bf16[64,1664]{1,0:T(8,128)(2,1)S(1)}, u32[]{:S(2)}, u32[]{:S(2)}) collective-permute-start(bf16[64,1664]{1,0:T(8,128)(2,1)S(1)} %get-tuple-element.24.refs_0_), channel_id=1, source_target_pairs={{0,4},{4,8},{8,12},{12,14},{14,10},{10,6},{6,2},{2,0},{1,3},{5,1},... | collective-permute-start | bytes 638984 | tf_op jit(solution)/shard_map/ppermute | solution.py:32
  7.8 5.3 %collective-permute-start.4 = (bf16[768,1280]{1,0:T(8,128)(2,1)S(1)}, bf16[768,1280]{1,0:T(8,128)(2,1)S(1)}, u32[]{:S(2)}, u32[]{:S(2)}) collective-permute-start(bf16[768,1280]{1,0:T(8,128)(2,1)S(1)} %get-tuple-element.28.refs_1_.refs_3_.refs_2_), channel_id=1, source_target_pairs={{0,1},{1,0},{2,3},{3,2},{4,5},{5,4},{6,7},{7,6},{8,9},{9,8},{10,11... | collective-permute-start | bytes 5898248 | tf_op jit(solution)/shard_map/ppermute | solution.py:325
  10.5 4.7 %collective-permute-start.5 = (bf16[768,1536]{1,0:T(8,128)(2,1)S(1)}, bf16[768,1536]{1,0:T(8,128)(2,1)S(1)}, u32[]{:S(2)}, u32[]{:S(2)}) collective-permute-start(bf16[768,1536]{1,0:T(8,128)(2,1)S(1)} %code.3.refs_2_.refs_4_.refs_3_), channel_id=1, source_target_pairs={{0,1},{1,0},{2,3},{3,2},{4,5},{5,4},{6,7},{7,6},{8,9},{9,8},{10,11... | collective-permute-start | bytes 7077896 | tf_op jit(solution)/shard_map/ppermute | solution.py:325
  11.1 7.5 %collective-permute-start.3 = (bf16[64,1664]{1,0:T(8,128)(2,1)S(1)}, bf16[64,1664]{1,0:T(8,128)(2,1)S(1)}, u32[]{:S(2)}, u32[]{:S(2)}) collective-permute-start(bf16[64,1664]{1,0:T(8,128)(2,1)S(1)} %collective-permute-done.refs_0_), channel_id=1, source_target_pairs={{0,4},{4,8},{8,12},{12,14},{14,10},{10,6},{6,2},{2,0},{1,3},{5,1},... | collective-permute-start | bytes 638984 | tf_op jit(solution)/shard_map/ppermute | solution.py:32
  13.0 7.5 %collective-permute-start.7 = (bf16[64,1664]{1,0:T(8,128)(2,1)S(1)}, bf16[64,1664]{1,0:T(8,128)(2,1)S(1)}, u32[]{:S(2)}, u32[]{:S(2)}) collective-permute-start(bf16[64,1664]{1,0:T(8,128)(2,1)S(1)} %collective-permute-done.1.refs_1_), channel_id=1, source_target_pairs={{0,2},{4,0},{8,4},{12,8},{14,12},{10,14},{6,10},{2,6},{1,5},{5,9},... | collective-permute-start | bytes 638984 | tf_op jit(solution)/shard_map/ppermute | solution.py:32
  18.7 8.0 %collective-permute-start.6 = (bf16[64,1792]{1,0:T(8,128)(2,1)S(1)}, bf16[64,1792]{1,0:T(8,128)(2,1)S(1)}, u32[]{:S(2)}, u32[]{:S(2)}) collective-permute-start(bf16[64,1792]{1,0:T(8,128)(2,1)S(1)} %attach.2), channel_id=1, source_target_pairs={{0,4},{4,8},{8,12},{12,14},{14,10},{10,6},{6,2},{2,0},{1,3},{5,1},... | collective-permute-start | bytes 688136 | tf_op jit(solution)/shard_map/ppermute | solution.py:32
  20.6 7.4 %collective-permute-start.8 = (bf16[64,1792]{1,0:T(8,128)(2,1)S(1)}, bf16[64,1792]{1,0:T(8,128)(2,1)S(1)}, u32[]{:S(2)}, u32[]{:S(2)}) collective-permute-start(bf16[64,1792]{1,0:T(8,128)(2,1)S(1)} %attach.3), channel_id=1, source_target_pairs={{0,2},{4,0},{8,4},{12,8},{14,12},{10,14},{6,10},{2,6},{1,5},{5,9},... | collective-permute-start | bytes 688136 | tf_op jit(solution)/shard_map/ppermute | solution.py:32
  22.5 10.9 %collective-permute-start.11 = (bf16[64,192]{1,0:T(8,128)(2,1)S(1)}, bf16[64,192]{1,0:T(8,128)(2,1)S(1)}, u32[]{:S(2)}, u32[]{:S(2)}) collective-permute-start(bf16[64,192]{1,0:T(8,128)(2,1)S(1)} %get-tuple-element.33), channel_id=1, source_target_pairs={{0,6},{4,2},{8,0},{12,4},{14,8},{10,12},{6,14},{2,10},{1,9},{5,13}... | collective-permute-start | bytes 73736 | tf_op jit(solution)/shard_map/ppermute | solution.py:32
  25.6 7.8 %collective-permute-start.12 = (bf16[64,192]{1,0:T(8,128)(2,1)S(1)}, bf16[64,192]{1,0:T(8,128)(2,1)S(1)}, u32[]{:S(2)}, u32[]{:S(2)}) collective-permute-start(bf16[64,192]{1,0:T(8,128)(2,1)S(1)} %get-tuple-element.36), channel_id=1, source_target_pairs={{0,8},{4,12},{8,14},{12,10},{14,6},{10,2},{6,0},{2,4},{1,7},{5,3},... | collective-permute-start | bytes 73736 | tf_op jit(solution)/shard_map/ppermute | solution.py:32
  26.8 6.6 %collective-permute-start.10 = (bf16[64,1792]{1,0:T(8,128)(2,1)S(1)}, bf16[64,1792]{1,0:T(8,128)(2,1)S(1)}, u32[]{:S(2)}, u32[]{:S(2)}) collective-permute-start(bf16[64,1792]{1,0:T(8,128)(2,1)S(1)} %collective-permute-done.6.refs_0_.refs_2_), channel_id=1, source_target_pairs={{0,4},{4,8},{8,12},{12,14},{14,10},{10,6},{6,2},{2,0},{1,3},{5,1},... | collective-permute-start | bytes 688136 | tf_op jit(solution)/shard_map/ppermute | solution.py:32
  29.5 11.7 %collective-permute-start.9 = (bf16[64,192]{1,0:T(8,128)(2,1)S(1)}, bf16[64,192]{1,0:T(8,128)(2,1)S(1)}, u32[]{:S(2)}, u32[]{:S(2)}) collective-permute-start(bf16[64,192]{1,0:T(8,128)(2,1)S(1)} %get-tuple-element.38), channel_id=1, source_target_pairs={{0,12},{4,14},{8,10},{12,6},{14,2},{10,0},{6,4},{2,8},{1,11},{5,7}... | collective-permute-start | bytes 73736 | tf_op jit(solution)/shard_map/ppermute | solution.py:32
  33.4 7.9 %collective-permute-start.13 = (bf16[64,192]{1,0:T(8,128)(2,1)S(1)}, bf16[64,192]{1,0:T(8,128)(2,1)S(1)}, u32[]{:S(2)}, u32[]{:S(2)}) collective-permute-start(bf16[64,192]{1,0:T(8,128)(2,1)S(1)} %get-tuple-element.39), channel_id=1, source_target_pairs={{0,10},{4,6},{8,2},{12,0},{14,4},{10,8},{6,12},{2,14},{1,13},{5,15... | collective-permute-start | bytes 73736 | tf_op jit(solution)/shard_map/ppermute | solution.py:32
  34.9 6.7 %collective-permute-start.14 = (bf16[64,192]{1,0:T(8,128)(2,1)S(1)}, bf16[64,192]{1,0:T(8,128)(2,1)S(1)}, u32[]{:S(2)}, u32[]{:S(2)}) collective-permute-start(bf16[64,192]{1,0:T(8,128)(2,1)S(1)} %hidden.9), channel_id=1, source_target_pairs={{0,14},{4,10},{8,6},{12,2},{14,0},{10,4},{6,8},{2,12},{1,15},{5,11... | collective-permute-start | bytes 73736 | tf_op jit(solution)/shard_map/ppermute | solution.py:32

commit v5 on v4

--- a/solution.py
+++ b/solution.py
@@ -24,12 +24,7 @@
 
 def ring_send(value, owners, steps):
     order = list(range(0, owners, 2)) + list(range(1, owners, 2))[::-1]
-    pairs = [
-        (2 * order[p] + core, 2 * order[(p + sign * steps) % owners] + core)
-        for core, sign in ((0, 1), (1, -1))
-        for p in range(owners)
-    ]
-    return lax.ppermute(value, ("ep", "tp"), pairs)
+    return lax.ppermute(value, "ep", [(order[p], order[(p + steps) % owners]) for p in range(owners)])
 
 
 def code_columns(entries):
@@ -252,10 +247,9 @@
     blocks, out_ref, held = refs[: len(steps)], refs[len(steps)], refs[len(steps) + 1]
     owners = lax.axis_size("ep")
     place = ring_place(lax.axis_index("ep"), owners)
-    sign = 1 - 2 * lax.axis_index("tp")
     units = held.shape[2]
     for block, step in zip(blocks, steps):
-        source = ring_owner((place + sign * step + owners) % owners, owners)
+        source = ring_owner((place + step + owners) % owners, owners)
         width = block.shape[1]
         if width == units:
             held[source] = block[...]

time: 42.6 us -> 42.3 us (level)
  starting transfers between devices: 21.1 us -> 20.2 us
  waiting for transfers between devices: 5.61 us -> 6.25 us
    ppermute x12, waiting for transfers between devices: 3.51 us -> 5.6 us  [ring_send(): lax.ppermute(value, 'ep', [(order[p], order[(p + steps) % owners]) for p...]
    ppermute x3, waiting for transfers between devices: 2.1 us -> 0.64 us  [swap(): return lax.ppermute(part, 'tp', [(0, 1), (1, 0)])]
    ppermute x12, starting transfers between devices: 20 us -> 19 us  [ring_send(): lax.ppermute(value, 'ep', [(order[p], order[(p + steps) % owners]) for p...]
where the time goes in v5:
time: 42.3 us; the launch traced here: 42.2 us
  starting transfers between devices  20.2 us (48%)
  Pallas kernels  15.7 us (37%)
  waiting for transfers between devices  6.25 us (15%)
    ppermute x12, starting transfers between devices, ring_send(): lax.ppermute(value, 'ep', [(order[p], order[(p + steps) % owners]) for p...  19 us
    pallas_call x5, Pallas kernels, hidden_units(): pl.pallas_call(functools.partial(hidden_kernel, count=len(chunks), pieces...  7.53 us
    ppermute x12, waiting for transfers between devices, ring_send(): lax.ppermute(value, 'ep', [(order[p], order[(p + steps) % owners]) for p...  5.6 us
    pallas_call x2, Pallas kernels, code_weights(): pl.pallas_call(functools.partial(code_kernel, following=following), out_s...  4.96 us
    pallas_call x1, Pallas kernels, begin(): pl.pallas_call(functools.partial(begin_kernel, tiles=tiles, following=fol...  2.16 us
    ppermute x3, starting transfers between devices, swap(): return lax.ppermute(part, 'tp', [(0, 1), (1, 0)])  1.16 us
    pallas_call x1, Pallas kernels, join_units(): pl.pallas_call(functools.partial(join_kernel, steps=steps), out_shape=jax...  0.87 us
  transfers between devices with their start and end apart: 15, of which 5 were waited for; matrix products, arithmetic and copies ran while one was open for 0% of the time, Pallas kernels for 30%

profile of v5, /device:TPU:0, one launch (start us, length us, event | category | flops | bytes accessed | tf_op | source)
XLA Modules:
  0.0 42.2 jit_solution(7012185083651167832)
XLA Ops:
  0.0 2.2 %begin.1 = (bf16[64,1664]{1,0:T(8,128)(2,1)S(1)}, bf16[768,256]{1,0:T(8,128)(2,1)S(1)}, bf16[5,256,768]{2,1,0:T(8,128)(2,1)S(1)}) custom-call(bf16[64,1536]{1,0:T(8,128)(2,1)} %tokens_ref.1, s32[4,64]{1,0:T(4,128)} %bitcast.2, f32[4,64]{1,0:T(4,128)} %bitcast.3, bf16[8,192,768]{2,1,0:T(8,128)(2,1)} %refs_0_.1, bf16[8,192,768]{2,1,0:T(8,128)(2,1)} %refs_1_.1), custom_call_target="tpu_custom_call" | custom-call | flops 1024 | bytes 1024 | tf_op jit(solution)/shard_map/begin/pallas_call | solution.py:159
  2.2 0.5 %collective-permute-start.2 = (bf16[768,256]{1,0:T(8,128)(2,1)S(1)}, bf16[768,256]{1,0:T(8,128)(2,1)S(1)}, u32[]{:S(2)}, u32[]{:S(2)}) collective-permute-start(bf16[768,256]{1,0:T(8,128)(2,1)S(1)} %get-tuple-element.26.refs_2_.refs_1_), channel_id=1, source_target_pairs={{0,1},{1,0},{2,3},{3,2},{4,5},{5,4},{6,7},{7,6},{8,9},{9,8},{10,11... | collective-permute-start | bytes 1179656 | tf_op jit(solution)/shard_map/ppermute | solution.py:319
  2.7 2.6 %collective-permute-start.1 = (bf16[64,1664]{1,0:T(8,128)(2,1)S(1)}, bf16[64,1664]{1,0:T(8,128)(2,1)S(1)}, u32[]{:S(2)}, u32[]{:S(2)}) collective-permute-start(bf16[64,1664]{1,0:T(8,128)(2,1)S(1)} %get-tuple-element.24.refs_0_), channel_id=1, source_target_pairs={{0,2},{4,0},{8,4},{12,8},{14,12},{10,14},{6,10},{2,6},{1,3},{5,1},... | collective-permute-start | bytes 638984 | tf_op jit(solution)/shard_map/ppermute | solution.py:27
  5.4 2.4 %code.2 = (bf16[768,1280]{1,0:T(8,128)(2,1)S(1)}, bf16[6,256,768]{2,1,0:T(8,128)(2,1)S(1)}) custom-call(bf16[8,192,768]{2,1,0:T(8,128)(2,1)} %refs_0_.1, bf16[8,192,768]{2,1,0:T(8,128)(2,1)} %refs_1_.1, bf16[5,256,768]{2,1,0:T(8,128)(2,1)S(1)} %get-tuple-element.25.refs_2_, bf16[768,256]{1,0:T(8,128)(2,1)S(1)} %collective-permute-done.2.refs_3_.refs_5_.refs_4_), custom_call_target="tpu_custom_call" | custom-call | flops 1024 | bytes 1024 | tf_op jit(solution)/shard_map/code/pallas_call | solution.py:102
  8.0 2.6 %code.3.refs_2_.refs_4_.refs_3_ = bf16[768,1536]{1,0:T(8,128)(2,1)S(1)} custom-call(bf16[6,256,768]{2,1,0:T(8,128)(2,1)S(1)} %get-tuple-element.27.refs_0_, bf16[768,1280]{1,0:T(8,128)(2,1)S(1)} %get-tuple-element.28.refs_1_.refs_3_.refs_2_), custom_call_target="tpu_custom_call" | custom-call | flops 1024 | bytes 1024 | tf_op jit(solution)/shard_map/code/pallas_call | solution.py:102
  10.5 0.5 %collective-permute-start.5 = (bf16[768,1536]{1,0:T(8,128)(2,1)S(1)}, bf16[768,1536]{1,0:T(8,128)(2,1)S(1)}, u32[]{:S(2)}, u32[]{:S(2)}) collective-permute-start(bf16[768,1536]{1,0:T(8,128)(2,1)S(1)} %code.3.refs_2_.refs_4_.refs_3_), channel_id=1, source_target_pairs={{0,1},{1,0},{2,3},{3,2},{4,5},{5,4},{6,7},{7,6},{8,9},{9,8},{10,11... | collective-permute-start | bytes 7077896 | tf_op jit(solution)/shard_map/ppermute | solution.py:319
  11.2 1.4 %collective-permute-done.refs_0_ = bf16[64,1664]{1,0:T(8,128)(2,1)S(1)} collective-permute-done((bf16[64,1664]{1,0:T(8,128)(2,1)S(1)}, bf16[64,1664]{1,0:T(8,128)(2,1)S(1)}, u32[]{:S(2)}, u32[]{:S(2)}) %collective-permute-start) | collective-permute-done | bytes 213024 | tf_op jit(solution)/shard_map/ppermute | solution.py:27
  13.0 1.6 %collective-permute-start.7 = (bf16[64,1664]{1,0:T(8,128)(2,1)S(1)}, bf16[64,1664]{1,0:T(8,128)(2,1)S(1)}, u32[]{:S(2)}, u32[]{:S(2)}) collective-permute-start(bf16[64,1664]{1,0:T(8,128)(2,1)S(1)} %collective-permute-done.1.refs_1_), channel_id=1, source_target_pairs={{0,2},{4,0},{8,4},{12,8},{14,12},{10,14},{6,10},{2,6},{1,3},{5,1},... | collective-permute-start | bytes 638984 | tf_op jit(solution)/shard_map/ppermute | solution.py:27
  14.6 0.6 %collective-permute-done.5.refs_7_.refs_6_ = bf16[768,1536]{1,0:T(8,128)(2,1)S(1)} collective-permute-done((bf16[768,1536]{1,0:T(8,128)(2,1)S(1)}, bf16[768,1536]{1,0:T(8,128)(2,1)S(1)}, u32[]{:S(2)}, u32[]{:S(2)}) %collective-permute-start.5) | collective-permute-done | bytes 2359328 | tf_op jit(solution)/shard_map/ppermute | solution.py:319
  15.2 1.5 %hidden.5 = (bf16[64,192]{1,0:T(8,128)(2,1)S(1)}, bf16[64,192]{1,0:T(8,128)(2,1)S(1)}) custom-call(bf16[64,1664]{1,0:T(8,128)(2,1)S(1)} %collective-permute-done.refs_0_, bf16[64,1664]{1,0:T(8,128)(2,1)S(1)} %collective-permute-done.1.refs_1_, bf16[768,256]{1,0:T(8,128)(2,1)S(1)} %get-tuple-element.26.refs_2_.refs_1_, ...), custom_call_target="tpu_custom_call" | custom-call | flops 12000000000 | bytes 1024 | tf_op jit(solution)/shard_map/hidden/pallas_call | solution.py:233
  16.8 2.3 %collective-permute-done.3.chunk_ref.refs_0_ = bf16[64,1664]{1,0:T(8,128)(2,1)S(1)} collective-permute-done((bf16[64,1664]{1,0:T(8,128)(2,1)S(1)}, bf16[64,1664]{1,0:T(8,128)(2,1)S(1)}, u32[]{:S(2)}, u32[]{:S(2)}) %collective-permute-start.3) | collective-permute-done | bytes 213024 | tf_op jit(solution)/shard_map/ppermute | solution.py:27
  19.1 1.2 %collective-permute-start.6 = (bf16[64,1792]{1,0:T(8,128)(2,1)S(1)}, bf16[64,1792]{1,0:T(8,128)(2,1)S(1)}, u32[]{:S(2)}, u32[]{:S(2)}) collective-permute-start(bf16[64,1792]{1,0:T(8,128)(2,1)S(1)} %attach.2), channel_id=1, source_target_pairs={{0,4},{4,8},{8,12},{12,14},{14,10},{10,6},{6,2},{2,0},{1,5},{5,9},... | collective-permute-start | bytes 688136 | tf_op jit(solution)/shard_map/ppermute | solution.py:27
  20.4 0.9 %collective-permute-start.8 = (bf16[64,1792]{1,0:T(8,128)(2,1)S(1)}, bf16[64,1792]{1,0:T(8,128)(2,1)S(1)}, u32[]{:S(2)}, u32[]{:S(2)}) collective-permute-start(bf16[64,1792]{1,0:T(8,128)(2,1)S(1)} %attach.3), channel_id=1, source_target_pairs={{0,2},{4,0},{8,4},{12,8},{14,12},{10,14},{6,10},{2,6},{1,3},{5,1},... | collective-permute-start | bytes 688136 | tf_op jit(solution)/shard_map/ppermute | solution.py:27
  21.2 1.5 %hidden.6 = (bf16[64,192]{1,0:T(8,128)(2,1)S(1)}, bf16[64,192]{1,0:T(8,128)(2,1)S(1)}) custom-call(bf16[64,1664]{1,0:T(8,128)(2,1)S(1)} %collective-permute-done.3.chunk_ref.refs_0_, bf16[64,1664]{1,0:T(8,128)(2,1)S(1)} %collective-permute-done.7.refs_1_.chunk_ref, bf16[768,256]{1,0:T(8,128)(2,1)S(1)} %get-tuple-element.26.refs_2_.refs_1_, ...), custom_call_target="tpu_custom_call" | custom-call | flops 12000000000 | bytes 1024 | tf_op jit(solution)/shard_map/hidden/pallas_call | solution.py:233
  22.8 2.6 %collective-permute-start.11 = (bf16[64,192]{1,0:T(8,128)(2,1)S(1)}, bf16[64,192]{1,0:T(8,128)(2,1)S(1)}, u32[]{:S(2)}, u32[]{:S(2)}) collective-permute-start(bf16[64,192]{1,0:T(8,128)(2,1)S(1)} %get-tuple-element.33), channel_id=1, source_target_pairs={{0,6},{4,2},{8,0},{12,4},{14,8},{10,12},{6,14},{2,10},{1,7},{5,3},... | collective-permute-start | bytes 73736 | tf_op jit(solution)/shard_map/ppermute | solution.py:27
  25.7 2.0 %collective-permute-start.10 = (bf16[64,1792]{1,0:T(8,128)(2,1)S(1)}, bf16[64,1792]{1,0:T(8,128)(2,1)S(1)}, u32[]{:S(2)}, u32[]{:S(2)}) collective-permute-start(bf16[64,1792]{1,0:T(8,128)(2,1)S(1)} %collective-permute-done.6.refs_0_.refs_2_), channel_id=1, source_target_pairs={{0,4},{4,8},{8,12},{12,14},{14,10},{10,6},{6,2},{2,0},{1,5},{5,9},... | collective-permute-start | bytes 688136 | tf_op jit(solution)/shard_map/ppermute | solution.py:27
  27.7 1.5 %hidden.7 = (bf16[64,192]{1,0:T(8,128)(2,1)S(1)}, bf16[64,192]{1,0:T(8,128)(2,1)S(1)}) custom-call(bf16[64,1792]{1,0:T(8,128)(2,1)S(1)} %collective-permute-done.6.refs_0_.refs_2_, bf16[64,1792]{1,0:T(8,128)(2,1)S(1)} %collective-permute-done.8.refs_1_.refs_4_, bf16[768,256]{1,0:T(8,128)(2,1)S(1)} %get-tuple-element.26.refs_2_.refs_1_, ...), custom_call_target="tpu_custom_call" | custom-call | flops 12000000000 | bytes 1024 | tf_op jit(solution)/shard_map/hidden/pallas_call | solution.py:233
  29.2 3.0 %collective-permute-start.9 = (bf16[64,192]{1,0:T(8,128)(2,1)S(1)}, bf16[64,192]{1,0:T(8,128)(2,1)S(1)}, u32[]{:S(2)}, u32[]{:S(2)}) collective-permute-start(bf16[64,192]{1,0:T(8,128)(2,1)S(1)} %get-tuple-element.38), channel_id=1, source_target_pairs={{0,12},{4,14},{8,10},{12,6},{14,2},{10,0},{6,4},{2,8},{1,13},{5,15... | collective-permute-start | bytes 73736 | tf_op jit(solution)/shard_map/ppermute | solution.py:27
  32.2 0.9 %collective-permute-start.13 = (bf16[64,192]{1,0:T(8,128)(2,1)S(1)}, bf16[64,192]{1,0:T(8,128)(2,1)S(1)}, u32[]{:S(2)}, u32[]{:S(2)}) collective-permute-start(bf16[64,192]{1,0:T(8,128)(2,1)S(1)} %get-tuple-element.39), channel_id=1, source_target_pairs={{0,10},{4,6},{8,2},{12,0},{14,4},{10,8},{6,12},{2,14},{1,11},{5,7}... | collective-permute-start | bytes 73736 | tf_op jit(solution)/shard_map/ppermute | solution.py:27
  33.1 1.5 %hidden.9 = bf16[64,192]{1,0:T(8,128)(2,1)S(1)} custom-call(bf16[64,1792]{1,0:T(8,128)(2,1)S(1)} %collective-permute-done.10.refs_0_, bf16[768,256]{1,0:T(8,128)(2,1)S(1)} %get-tuple-element.26.refs_2_.refs_1_, bf16[768,1280]{1,0:T(8,128)(2,1)S(1)} %get-tuple-element.28.refs_1_.refs_3_.refs_2_, bf16[768,1536]{1,0:T(8,128)(2,1)S(1)} %code.3.refs_2_.refs_4_.refs_3_, ...), custom_call_target="tpu_custom_call" | custom-call | flops 12000000000 | bytes 1024 | tf_op jit(solution)/shard_map/hidden/pallas_call | solution.py:233
  34.6 3.4 %collective-permute-start.14 = (bf16[64,192]{1,0:T(8,128)(2,1)S(1)}, bf16[64,192]{1,0:T(8,128)(2,1)S(1)}, u32[]{:S(2)}, u32[]{:S(2)}) collective-permute-start(bf16[64,192]{1,0:T(8,128)(2,1)S(1)} %hidden.9), channel_id=1, source_target_pairs={{0,14},{4,10},{8,6},{12,2},{14,0},{10,4},{6,8},{2,12},{1,15},{5,11... | collective-permute-start | bytes 73736 | tf_op jit(solution)/shard_map/ppermute | solution.py:27
  38.0 1.5 %hidden.8.refs_3_ = bf16[64,192]{1,0:T(8,128)(2,1)S(1)} custom-call(bf16[64,1664]{1,0:T(8,128)(2,1)S(1)} %get-tuple-element.24.refs_0_, bf16[768,256]{1,0:T(8,128)(2,1)S(1)} %get-tuple-element.26.refs_2_.refs_1_, bf16[768,1280]{1,0:T(8,128)(2,1)S(1)} %get-tuple-element.28.refs_1_.refs_3_.refs_2_, bf16[768,1536]{1,0:T(8,128)(2,1)S(1)} %code.3.refs_2_.refs_4_.refs_3_, ...), custom_call_target="tpu_custom_call" | custom-call | flops 12000000000 | bytes 1024 | tf_op jit(solution)/shard_map/hidden/pallas_call | solution.py:233
  39.5 1.7 %collective-permute-done.14.refs_7_ = bf16[64,192]{1,0:T(8,128)(2,1)S(1)} collective-permute-done((bf16[64,192]{1,0:T(8,128)(2,1)S(1)}, bf16[64,192]{1,0:T(8,128)(2,1)S(1)}, u32[]{:S(2)}, u32[]{:S(2)}) %collective-permute-start.14) | collective-permute-done | bytes 24608 | tf_op jit(solution)/shard_map/ppermute | solution.py:27
  41.3 0.9 %join.1 = bf16[64,1536]{1,0:T(8,128)(2,1)} custom-call(bf16[64,192]{1,0:T(8,128)(2,1)S(1)} %collective-permute-done.9.refs_0_, bf16[64,192]{1,0:T(8,128)(2,1)S(1)} %collective-permute-done.12.refs_1_, bf16[64,1792]{1,0:T(8,128)(2,1)S(1)} %collective-permute-done.6.refs_0_.refs_2_, bf16[64,192]{1,0:T(8,128)(2,1)S(1)} %hidden.8.refs_3_, ...), custom_call_target="tpu_custom_call" | custom-call | tf_op jit(solution)/shard_map/join/pallas_call | solution.py:265
  (18 shorter events, 1.5 us)
Async XLA Ops:
  2.2 3.2 %collective-permute-start.2 = (bf16[768,256]{1,0:T(8,128)(2,1)S(1)}, bf16[768,256]{1,0:T(8,128)(2,1)S(1)}, u32[]{:S(2)}, u32[]{:S(2)}) collective-permute-start(bf16[768,256]{1,0:T(8,128)(2,1)S(1)} %get-tuple-element.26.refs_2_.refs_1_), channel_id=1, source_target_pairs={{0,1},{1,0},{2,3},{3,2},{4,5},{5,4},{6,7},{7,6},{8,9},{9,8},{10,11... | collective-permute-start | bytes 1179656 | tf_op jit(solution)/shard_map/ppermute | solution.py:319
  2.7 8.5 %collective-permute-start.1 = (bf16[64,1664]{1,0:T(8,128)(2,1)S(1)}, bf16[64,1664]{1,0:T(8,128)(2,1)S(1)}, u32[]{:S(2)}, u32[]{:S(2)}) collective-permute-start(bf16[64,1664]{1,0:T(8,128)(2,1)S(1)} %get-tuple-element.24.refs_0_), channel_id=1, source_target_pairs={{0,2},{4,0},{8,4},{12,8},{14,12},{10,14},{6,10},{2,6},{1,3},{5,1},... | collective-permute-start | bytes 638984 | tf_op jit(solution)/shard_map/ppermute | solution.py:27
  5.2 7.3 %collective-permute-start = (bf16[64,1664]{1,0:T(8,128)(2,1)S(1)}, bf16[64,1664]{1,0:T(8,128)(2,1)S(1)}, u32[]{:S(2)}, u32[]{:S(2)}) collective-permute-start(bf16[64,1664]{1,0:T(8,128)(2,1)S(1)} %get-tuple-element.24.refs_0_), channel_id=1, source_target_pairs={{0,4},{4,8},{8,12},{12,14},{14,10},{10,6},{6,2},{2,0},{1,5},{5,9},... | collective-permute-start | bytes 638984 | tf_op jit(solution)/shard_map/ppermute | solution.py:27
  7.8 6.8 %collective-permute-start.4 = (bf16[768,1280]{1,0:T(8,128)(2,1)S(1)}, bf16[768,1280]{1,0:T(8,128)(2,1)S(1)}, u32[]{:S(2)}, u32[]{:S(2)}) collective-permute-start(bf16[768,1280]{1,0:T(8,128)(2,1)S(1)} %get-tuple-element.28.refs_1_.refs_3_.refs_2_), channel_id=1, source_target_pairs={{0,1},{1,0},{2,3},{3,2},{4,5},{5,4},{6,7},{7,6},{8,9},{9,8},{10,11... | collective-permute-start | bytes 5898248 | tf_op jit(solution)/shard_map/ppermute | solution.py:319
  10.5 4.7 %collective-permute-start.5 = (bf16[768,1536]{1,0:T(8,128)(2,1)S(1)}, bf16[768,1536]{1,0:T(8,128)(2,1)S(1)}, u32[]{:S(2)}, u32[]{:S(2)}) collective-permute-start(bf16[768,1536]{1,0:T(8,128)(2,1)S(1)} %code.3.refs_2_.refs_4_.refs_3_), channel_id=1, source_target_pairs={{0,1},{1,0},{2,3},{3,2},{4,5},{5,4},{6,7},{7,6},{8,9},{9,8},{10,11... | collective-permute-start | bytes 7077896 | tf_op jit(solution)/shard_map/ppermute | solution.py:319
  12.6 6.5 %collective-permute-start.3 = (bf16[64,1664]{1,0:T(8,128)(2,1)S(1)}, bf16[64,1664]{1,0:T(8,128)(2,1)S(1)}, u32[]{:S(2)}, u32[]{:S(2)}) collective-permute-start(bf16[64,1664]{1,0:T(8,128)(2,1)S(1)} %collective-permute-done.refs_0_), channel_id=1, source_target_pairs={{0,4},{4,8},{8,12},{12,14},{14,10},{10,6},{6,2},{2,0},{1,5},{5,9},... | collective-permute-start | bytes 638984 | tf_op jit(solution)/shard_map/ppermute | solution.py:27
  13.0 7.3 %collective-permute-start.7 = (bf16[64,1664]{1,0:T(8,128)(2,1)S(1)}, bf16[64,1664]{1,0:T(8,128)(2,1)S(1)}, u32[]{:S(2)}, u32[]{:S(2)}) collective-permute-start(bf16[64,1664]{1,0:T(8,128)(2,1)S(1)} %collective-permute-done.1.refs_1_), channel_id=1, source_target_pairs={{0,2},{4,0},{8,4},{12,8},{14,12},{10,14},{6,10},{2,6},{1,3},{5,1},... | collective-permute-start | bytes 638984 | tf_op jit(solution)/shard_map/ppermute | solution.py:27
  19.1 6.6 %collective-permute-start.6 = (bf16[64,1792]{1,0:T(8,128)(2,1)S(1)}, bf16[64,1792]{1,0:T(8,128)(2,1)S(1)}, u32[]{:S(2)}, u32[]{:S(2)}) collective-permute-start(bf16[64,1792]{1,0:T(8,128)(2,1)S(1)} %attach.2), channel_id=1, source_target_pairs={{0,4},{4,8},{8,12},{12,14},{14,10},{10,6},{6,2},{2,0},{1,5},{5,9},... | collective-permute-start | bytes 688136 | tf_op jit(solution)/shard_map/ppermute | solution.py:27
  20.4 7.3 %collective-permute-start.8 = (bf16[64,1792]{1,0:T(8,128)(2,1)S(1)}, bf16[64,1792]{1,0:T(8,128)(2,1)S(1)}, u32[]{:S(2)}, u32[]{:S(2)}) collective-permute-start(bf16[64,1792]{1,0:T(8,128)(2,1)S(1)} %attach.3), channel_id=1, source_target_pairs={{0,2},{4,0},{8,4},{12,8},{14,12},{10,14},{6,10},{2,6},{1,3},{5,1},... | collective-permute-start | bytes 688136 | tf_op jit(solution)/shard_map/ppermute | solution.py:27
  22.8 10.3 %collective-permute-start.11 = (bf16[64,192]{1,0:T(8,128)(2,1)S(1)}, bf16[64,192]{1,0:T(8,128)(2,1)S(1)}, u32[]{:S(2)}, u32[]{:S(2)}) collective-permute-start(bf16[64,192]{1,0:T(8,128)(2,1)S(1)} %get-tuple-element.33), channel_id=1, source_target_pairs={{0,6},{4,2},{8,0},{12,4},{14,8},{10,12},{6,14},{2,10},{1,7},{5,3},... | collective-permute-start | bytes 73736 | tf_op jit(solution)/shard_map/ppermute | solution.py:27
  25.4 7.7 %collective-permute-start.12 = (bf16[64,192]{1,0:T(8,128)(2,1)S(1)}, bf16[64,192]{1,0:T(8,128)(2,1)S(1)}, u32[]{:S(2)}, u32[]{:S(2)}) collective-permute-start(bf16[64,192]{1,0:T(8,128)(2,1)S(1)} %get-tuple-element.36), channel_id=1, source_target_pairs={{0,8},{4,12},{8,14},{12,10},{14,6},{10,2},{6,0},{2,4},{1,9},{5,13}... | collective-permute-start | bytes 73736 | tf_op jit(solution)/shard_map/ppermute | solution.py:27
  25.7 7.4 %collective-permute-start.10 = (bf16[64,1792]{1,0:T(8,128)(2,1)S(1)}, bf16[64,1792]{1,0:T(8,128)(2,1)S(1)}, u32[]{:S(2)}, u32[]{:S(2)}) collective-permute-start(bf16[64,1792]{1,0:T(8,128)(2,1)S(1)} %collective-permute-done.6.refs_0_.refs_2_), channel_id=1, source_target_pairs={{0,4},{4,8},{8,12},{12,14},{14,10},{10,6},{6,2},{2,0},{1,5},{5,9},... | collective-permute-start | bytes 688136 | tf_op jit(solution)/shard_map/ppermute | solution.py:27
  29.2 10.3 %collective-permute-start.9 = (bf16[64,192]{1,0:T(8,128)(2,1)S(1)}, bf16[64,192]{1,0:T(8,128)(2,1)S(1)}, u32[]{:S(2)}, u32[]{:S(2)}) collective-permute-start(bf16[64,192]{1,0:T(8,128)(2,1)S(1)} %get-tuple-element.38), channel_id=1, source_target_pairs={{0,12},{4,14},{8,10},{12,6},{14,2},{10,0},{6,4},{2,8},{1,13},{5,15... | collective-permute-start | bytes 73736 | tf_op jit(solution)/shard_map/ppermute | solution.py:27
  32.2 7.3 %collective-permute-start.13 = (bf16[64,192]{1,0:T(8,128)(2,1)S(1)}, bf16[64,192]{1,0:T(8,128)(2,1)S(1)}, u32[]{:S(2)}, u32[]{:S(2)}) collective-permute-start(bf16[64,192]{1,0:T(8,128)(2,1)S(1)} %get-tuple-element.39), channel_id=1, source_target_pairs={{0,10},{4,6},{8,2},{12,0},{14,4},{10,8},{6,12},{2,14},{1,11},{5,7}... | collective-permute-start | bytes 73736 | tf_op jit(solution)/shard_map/ppermute | solution.py:27
  34.6 6.7 %collective-permute-start.14 = (bf16[64,192]{1,0:T(8,128)(2,1)S(1)}, bf16[64,192]{1,0:T(8,128)(2,1)S(1)}, u32[]{:S(2)}, u32[]{:S(2)}) collective-permute-start(bf16[64,192]{1,0:T(8,128)(2,1)S(1)} %hidden.9), channel_id=1, source_target_pairs={{0,14},{4,10},{8,6},{12,2},{14,0},{10,4},{6,8},{2,12},{1,15},{5,11... | collective-permute-start | bytes 73736 | tf_op jit(solution)/shard_map/ppermute | solution.py:27

commit v6 on v5

--- a/solution.py
+++ b/solution.py
@@ -30,16 +30,17 @@
 def code_columns(entries):
     depth, count = entries.shape
     blocks = entries.reshape(depth // BLOCK, BLOCK, count)
-    largest = jnp.max(jnp.abs(blocks), axis=1, keepdims=True)
-    largest = jnp.maximum(largest, 2.0**-40)
+    sizes = jnp.abs(blocks)
+    sizes = jnp.maximum(sizes[:, : BLOCK // 2], sizes[:, BLOCK // 2 :]).astype(jnp.float32)
+    largest = jnp.maximum(jnp.max(sizes, axis=1, keepdims=True), 2.0**-40)
     lifted = largest * 2.0**23
     power = jnp.minimum((largest * 0.7 + lifted) - lifted, 2.0**8)
-    lowered = blocks * (1.0 - 2.0**-12)
-    top = power * 1.5
-    lowered = jnp.minimum(jnp.maximum(lowered, -top), top)
+    top = (power * 1.5).astype(jnp.bfloat16)
+    blocks = jnp.minimum(jnp.maximum(blocks, -top), top)
+    lowered = blocks.astype(jnp.float32) * (1.0 - 2.0**-12)
     least = power * (0.25 * (1.0 + 2.0**-10))
     anchor = jnp.maximum(jnp.abs(lowered), least) * 2.0**22
-    return ((lowered + anchor) - anchor).reshape(depth, count)
+    return ((lowered + anchor) - anchor).reshape(depth, count).astype(jnp.bfloat16)
 
 
 def tile_rows(tile, experts):
@@ -51,9 +52,8 @@
 
 def code_tile(rows_ref, out_ref, first):
     depth = rows_ref.shape[1]
-    for low in range(0, depth, 256):
-        turned = rows_ref[:, low : low + 256].T.astype(jnp.float32)
-        out_ref[low : low + 256, pl.ds(first, 256)] = code_columns(turned).astype(jnp.bfloat16)
+    for low in range(0, depth, LANES):
+        out_ref[low : low + LANES, pl.ds(first, 256)] = code_columns(rows_ref[:, low : low + LANES].T)
 
 
 def fetch_rows(gate_ref, up_ref, tiles, target, arrived):

time: 42.3 us -> 42.1 us (level)
  no operation moved by 1% of the time
where the time goes in v6:
time: 42.1 us; the launch traced here: 42 us
  starting transfers between devices  20.1 us (48%)
  Pallas kernels  15.6 us (37%)
  waiting for transfers between devices  6.3 us (15%)
    ppermute x12, starting transfers between devices, ring_send(): lax.ppermute(value, 'ep', [(order[p], order[(p + steps) % owners]) for p...  18.9 us
    pallas_call x5, Pallas kernels, hidden_units(): pl.pallas_call(functools.partial(hidden_kernel, count=len(chunks), pieces...  7.55 us
    ppermute x12, waiting for transfers between devices, ring_send(): lax.ppermute(value, 'ep', [(order[p], order[(p + steps) % owners]) for p...  5.71 us
    pallas_call x2, Pallas kernels, code_weights(): pl.pallas_call(functools.partial(code_kernel, following=following), out_s...  4.84 us
    pallas_call x1, Pallas kernels, begin(): pl.pallas_call(functools.partial(begin_kernel, tiles=tiles, following=fol...  2.15 us
    ppermute x3, starting transfers between devices, swap(): return lax.ppermute(part, 'tp', [(0, 1), (1, 0)])  1.16 us
    pallas_call x1, Pallas kernels, join_units(): pl.pallas_call(functools.partial(join_kernel, steps=steps), out_shape=jax...  0.87 us
  transfers between devices with their start and end apart: 15, of which 5 were waited for; matrix products, arithmetic and copies ran while one was open for 0% of the time, Pallas kernels for 30%

profile of v6, /device:TPU:0, one launch (start us, length us, event | category | flops | bytes accessed | tf_op | source)
XLA Modules:
  0.0 42.0 jit_solution(13781928878154661880)
XLA Ops:
  0.0 2.1 %begin.1 = (bf16[64,1664]{1,0:T(8,128)(2,1)S(1)}, bf16[768,256]{1,0:T(8,128)(2,1)S(1)}, bf16[5,256,768]{2,1,0:T(8,128)(2,1)S(1)}) custom-call(bf16[64,1536]{1,0:T(8,128)(2,1)} %tokens_ref.1, s32[4,64]{1,0:T(4,128)} %bitcast.2, f32[4,64]{1,0:T(4,128)} %bitcast.3, bf16[8,192,768]{2,1,0:T(8,128)(2,1)} %refs_0_.1, bf16[8,192,768]{2,1,0:T(8,128)(2,1)} %refs_1_.1), custom_call_target="tpu_custom_call" | custom-call | flops 1024 | bytes 1024 | tf_op jit(solution)/shard_map/begin/pallas_call | solution.py:159
  2.2 0.5 %collective-permute-start.2 = (bf16[768,256]{1,0:T(8,128)(2,1)S(1)}, bf16[768,256]{1,0:T(8,128)(2,1)S(1)}, u32[]{:S(2)}, u32[]{:S(2)}) collective-permute-start(bf16[768,256]{1,0:T(8,128)(2,1)S(1)} %get-tuple-element.26.refs_2_.refs_1_), channel_id=1, source_target_pairs={{0,1},{1,0},{2,3},{3,2},{4,5},{5,4},{6,7},{7,6},{8,9},{9,8},{10,11... | collective-permute-start | bytes 1179656 | tf_op jit(solution)/shard_map/ppermute | solution.py:319
  2.7 2.6 %collective-permute-start.1 = (bf16[64,1664]{1,0:T(8,128)(2,1)S(1)}, bf16[64,1664]{1,0:T(8,128)(2,1)S(1)}, u32[]{:S(2)}, u32[]{:S(2)}) collective-permute-start(bf16[64,1664]{1,0:T(8,128)(2,1)S(1)} %get-tuple-element.24.refs_0_), channel_id=1, source_target_pairs={{0,2},{4,0},{8,4},{12,8},{14,12},{10,14},{6,10},{2,6},{1,3},{5,1},... | collective-permute-start | bytes 638984 | tf_op jit(solution)/shard_map/ppermute | solution.py:27
  5.4 2.3 %code.2 = (bf16[768,1280]{1,0:T(8,128)(2,1)S(1)}, bf16[6,256,768]{2,1,0:T(8,128)(2,1)S(1)}) custom-call(bf16[8,192,768]{2,1,0:T(8,128)(2,1)} %refs_0_.1, bf16[8,192,768]{2,1,0:T(8,128)(2,1)} %refs_1_.1, bf16[5,256,768]{2,1,0:T(8,128)(2,1)S(1)} %get-tuple-element.25.refs_2_, bf16[768,256]{1,0:T(8,128)(2,1)S(1)} %collective-permute-done.2.refs_3_.refs_5_.refs_4_), custom_call_target="tpu_custom_call" | custom-call | flops 1024 | bytes 1024 | tf_op jit(solution)/shard_map/code/pallas_call | solution.py:102
  7.9 2.5 %code.3.refs_2_.refs_4_.refs_3_ = bf16[768,1536]{1,0:T(8,128)(2,1)S(1)} custom-call(bf16[6,256,768]{2,1,0:T(8,128)(2,1)S(1)} %get-tuple-element.27.refs_0_, bf16[768,1280]{1,0:T(8,128)(2,1)S(1)} %get-tuple-element.28.refs_1_.refs_3_.refs_2_), custom_call_target="tpu_custom_call" | custom-call | flops 1024 | bytes 1024 | tf_op jit(solution)/shard_map/code/pallas_call | solution.py:102
  10.4 0.5 %collective-permute-start.5 = (bf16[768,1536]{1,0:T(8,128)(2,1)S(1)}, bf16[768,1536]{1,0:T(8,128)(2,1)S(1)}, u32[]{:S(2)}, u32[]{:S(2)}) collective-permute-start(bf16[768,1536]{1,0:T(8,128)(2,1)S(1)} %code.3.refs_2_.refs_4_.refs_3_), channel_id=1, source_target_pairs={{0,1},{1,0},{2,3},{3,2},{4,5},{5,4},{6,7},{7,6},{8,9},{9,8},{10,11... | collective-permute-start | bytes 7077896 | tf_op jit(solution)/shard_map/ppermute | solution.py:319
  11.2 1.4 %collective-permute-done.refs_0_ = bf16[64,1664]{1,0:T(8,128)(2,1)S(1)} collective-permute-done((bf16[64,1664]{1,0:T(8,128)(2,1)S(1)}, bf16[64,1664]{1,0:T(8,128)(2,1)S(1)}, u32[]{:S(2)}, u32[]{:S(2)}) %collective-permute-start) | collective-permute-done | bytes 213024 | tf_op jit(solution)/shard_map/ppermute | solution.py:27
  12.9 1.7 %collective-permute-start.7 = (bf16[64,1664]{1,0:T(8,128)(2,1)S(1)}, bf16[64,1664]{1,0:T(8,128)(2,1)S(1)}, u32[]{:S(2)}, u32[]{:S(2)}) collective-permute-start(bf16[64,1664]{1,0:T(8,128)(2,1)S(1)} %collective-permute-done.1.refs_1_), channel_id=1, source_target_pairs={{0,2},{4,0},{8,4},{12,8},{14,12},{10,14},{6,10},{2,6},{1,3},{5,1},... | collective-permute-start | bytes 638984 | tf_op jit(solution)/shard_map/ppermute | solution.py:27
  14.6 0.6 %collective-permute-done.5.refs_7_.refs_6_ = bf16[768,1536]{1,0:T(8,128)(2,1)S(1)} collective-permute-done((bf16[768,1536]{1,0:T(8,128)(2,1)S(1)}, bf16[768,1536]{1,0:T(8,128)(2,1)S(1)}, u32[]{:S(2)}, u32[]{:S(2)}) %collective-permute-start.5) | collective-permute-done | bytes 2359328 | tf_op jit(solution)/shard_map/ppermute | solution.py:319
  15.2 1.5 %hidden.5 = (bf16[64,192]{1,0:T(8,128)(2,1)S(1)}, bf16[64,192]{1,0:T(8,128)(2,1)S(1)}) custom-call(bf16[64,1664]{1,0:T(8,128)(2,1)S(1)} %collective-permute-done.refs_0_, bf16[64,1664]{1,0:T(8,128)(2,1)S(1)} %collective-permute-done.1.refs_1_, bf16[768,256]{1,0:T(8,128)(2,1)S(1)} %get-tuple-element.26.refs_2_.refs_1_, ...), custom_call_target="tpu_custom_call" | custom-call | flops 12000000000 | bytes 1024 | tf_op jit(solution)/shard_map/hidden/pallas_call | solution.py:233
  16.7 2.4 %collective-permute-done.3.chunk_ref.refs_0_ = bf16[64,1664]{1,0:T(8,128)(2,1)S(1)} collective-permute-done((bf16[64,1664]{1,0:T(8,128)(2,1)S(1)}, bf16[64,1664]{1,0:T(8,128)(2,1)S(1)}, u32[]{:S(2)}, u32[]{:S(2)}) %collective-permute-start.3) | collective-permute-done | bytes 213024 | tf_op jit(solution)/shard_map/ppermute | solution.py:27
  19.1 1.0 %collective-permute-start.6 = (bf16[64,1792]{1,0:T(8,128)(2,1)S(1)}, bf16[64,1792]{1,0:T(8,128)(2,1)S(1)}, u32[]{:S(2)}, u32[]{:S(2)}) collective-permute-start(bf16[64,1792]{1,0:T(8,128)(2,1)S(1)} %attach.2), channel_id=1, source_target_pairs={{0,4},{4,8},{8,12},{12,14},{14,10},{10,6},{6,2},{2,0},{1,5},{5,9},... | collective-permute-start | bytes 688136 | tf_op jit(solution)/shard_map/ppermute | solution.py:27
  20.3 1.0 %collective-permute-start.8 = (bf16[64,1792]{1,0:T(8,128)(2,1)S(1)}, bf16[64,1792]{1,0:T(8,128)(2,1)S(1)}, u32[]{:S(2)}, u32[]{:S(2)}) collective-permute-start(bf16[64,1792]{1,0:T(8,128)(2,1)S(1)} %attach.3), channel_id=1, source_target_pairs={{0,2},{4,0},{8,4},{12,8},{14,12},{10,14},{6,10},{2,6},{1,3},{5,1},... | collective-permute-start | bytes 688136 | tf_op jit(solution)/shard_map/ppermute | solution.py:27
  21.2 1.5 %hidden.6 = (bf16[64,192]{1,0:T(8,128)(2,1)S(1)}, bf16[64,192]{1,0:T(8,128)(2,1)S(1)}) custom-call(bf16[64,1664]{1,0:T(8,128)(2,1)S(1)} %collective-permute-done.3.chunk_ref.refs_0_, bf16[64,1664]{1,0:T(8,128)(2,1)S(1)} %collective-permute-done.7.refs_1_.chunk_ref, bf16[768,256]{1,0:T(8,128)(2,1)S(1)} %get-tuple-element.26.refs_2_.refs_1_, ...), custom_call_target="tpu_custom_call" | custom-call | flops 12000000000 | bytes 1024 | tf_op jit(solution)/shard_map/hidden/pallas_call | solution.py:233
  22.8 2.6 %collective-permute-start.11 = (bf16[64,192]{1,0:T(8,128)(2,1)S(1)}, bf16[64,192]{1,0:T(8,128)(2,1)S(1)}, u32[]{:S(2)}, u32[]{:S(2)}) collective-permute-start(bf16[64,192]{1,0:T(8,128)(2,1)S(1)} %get-tuple-element.33), channel_id=1, source_target_pairs={{0,6},{4,2},{8,0},{12,4},{14,8},{10,12},{6,14},{2,10},{1,7},{5,3},... | collective-permute-start | bytes 73736 | tf_op jit(solution)/shard_map/ppermute | solution.py:27
  25.7 1.8 %collective-permute-start.10 = (bf16[64,1792]{1,0:T(8,128)(2,1)S(1)}, bf16[64,1792]{1,0:T(8,128)(2,1)S(1)}, u32[]{:S(2)}, u32[]{:S(2)}) collective-permute-start(bf16[64,1792]{1,0:T(8,128)(2,1)S(1)} %collective-permute-done.6.refs_0_.refs_2_), channel_id=1, source_target_pairs={{0,4},{4,8},{8,12},{12,14},{14,10},{10,6},{6,2},{2,0},{1,5},{5,9},... | collective-permute-start | bytes 688136 | tf_op jit(solution)/shard_map/ppermute | solution.py:27
  27.6 1.5 %hidden.7 = (bf16[64,192]{1,0:T(8,128)(2,1)S(1)}, bf16[64,192]{1,0:T(8,128)(2,1)S(1)}) custom-call(bf16[64,1792]{1,0:T(8,128)(2,1)S(1)} %collective-permute-done.6.refs_0_.refs_2_, bf16[64,1792]{1,0:T(8,128)(2,1)S(1)} %collective-permute-done.8.refs_1_.refs_4_, bf16[768,256]{1,0:T(8,128)(2,1)S(1)} %get-tuple-element.26.refs_2_.refs_1_, ...), custom_call_target="tpu_custom_call" | custom-call | flops 12000000000 | bytes 1024 | tf_op jit(solution)/shard_map/hidden/pallas_call | solution.py:233
  29.1 2.9 %collective-permute-start.9 = (bf16[64,192]{1,0:T(8,128)(2,1)S(1)}, bf16[64,192]{1,0:T(8,128)(2,1)S(1)}, u32[]{:S(2)}, u32[]{:S(2)}) collective-permute-start(bf16[64,192]{1,0:T(8,128)(2,1)S(1)} %get-tuple-element.38), channel_id=1, source_target_pairs={{0,12},{4,14},{8,10},{12,6},{14,2},{10,0},{6,4},{2,8},{1,13},{5,15... | collective-permute-start | bytes 73736 | tf_op jit(solution)/shard_map/ppermute | solution.py:27
  31.9 1.0 %collective-permute-start.13 = (bf16[64,192]{1,0:T(8,128)(2,1)S(1)}, bf16[64,192]{1,0:T(8,128)(2,1)S(1)}, u32[]{:S(2)}, u32[]{:S(2)}) collective-permute-start(bf16[64,192]{1,0:T(8,128)(2,1)S(1)} %get-tuple-element.39), channel_id=1, source_target_pairs={{0,10},{4,6},{8,2},{12,0},{14,4},{10,8},{6,12},{2,14},{1,11},{5,7}... | collective-permute-start | bytes 73736 | tf_op jit(solution)/shard_map/ppermute | solution.py:27
  33.0 1.5 %hidden.9 = bf16[64,192]{1,0:T(8,128)(2,1)S(1)} custom-call(bf16[64,1792]{1,0:T(8,128)(2,1)S(1)} %collective-permute-done.10.refs_0_, bf16[768,256]{1,0:T(8,128)(2,1)S(1)} %get-tuple-element.26.refs_2_.refs_1_, bf16[768,1280]{1,0:T(8,128)(2,1)S(1)} %get-tuple-element.28.refs_1_.refs_3_.refs_2_, bf16[768,1536]{1,0:T(8,128)(2,1)S(1)} %code.3.refs_2_.refs_4_.refs_3_, ...), custom_call_target="tpu_custom_call" | custom-call | flops 12000000000 | bytes 1024 | tf_op jit(solution)/shard_map/hidden/pallas_call | solution.py:233
  34.5 3.5 %collective-permute-start.14 = (bf16[64,192]{1,0:T(8,128)(2,1)S(1)}, bf16[64,192]{1,0:T(8,128)(2,1)S(1)}, u32[]{:S(2)}, u32[]{:S(2)}) collective-permute-start(bf16[64,192]{1,0:T(8,128)(2,1)S(1)} %hidden.9), channel_id=1, source_target_pairs={{0,14},{4,10},{8,6},{12,2},{14,0},{10,4},{6,8},{2,12},{1,15},{5,11... | collective-permute-start | bytes 73736 | tf_op jit(solution)/shard_map/ppermute | solution.py:27
  37.9 1.5 %hidden.8.refs_3_ = bf16[64,192]{1,0:T(8,128)(2,1)S(1)} custom-call(bf16[64,1664]{1,0:T(8,128)(2,1)S(1)} %get-tuple-element.24.refs_0_, bf16[768,256]{1,0:T(8,128)(2,1)S(1)} %get-tuple-element.26.refs_2_.refs_1_, bf16[768,1280]{1,0:T(8,128)(2,1)S(1)} %get-tuple-element.28.refs_1_.refs_3_.refs_2_, bf16[768,1536]{1,0:T(8,128)(2,1)S(1)} %code.3.refs_2_.refs_4_.refs_3_, ...), custom_call_target="tpu_custom_call" | custom-call | flops 12000000000 | bytes 1024 | tf_op jit(solution)/shard_map/hidden/pallas_call | solution.py:233
  39.5 1.7 %collective-permute-done.14.refs_7_ = bf16[64,192]{1,0:T(8,128)(2,1)S(1)} collective-permute-done((bf16[64,192]{1,0:T(8,128)(2,1)S(1)}, bf16[64,192]{1,0:T(8,128)(2,1)S(1)}, u32[]{:S(2)}, u32[]{:S(2)}) %collective-permute-start.14) | collective-permute-done | bytes 24608 | tf_op jit(solution)/shard_map/ppermute | solution.py:27
  41.1 0.9 %join.1 = bf16[64,1536]{1,0:T(8,128)(2,1)} custom-call(bf16[64,192]{1,0:T(8,128)(2,1)S(1)} %collective-permute-done.9.refs_0_, bf16[64,192]{1,0:T(8,128)(2,1)S(1)} %collective-permute-done.12.refs_1_, bf16[64,1792]{1,0:T(8,128)(2,1)S(1)} %collective-permute-done.6.refs_0_.refs_2_, bf16[64,192]{1,0:T(8,128)(2,1)S(1)} %hidden.8.refs_3_, ...), custom_call_target="tpu_custom_call" | custom-call | tf_op jit(solution)/shard_map/join/pallas_call | solution.py:265
  (18 shorter events, 1.5 us)
Async XLA Ops:
  2.2 3.2 %collective-permute-start.2 = (bf16[768,256]{1,0:T(8,128)(2,1)S(1)}, bf16[768,256]{1,0:T(8,128)(2,1)S(1)}, u32[]{:S(2)}, u32[]{:S(2)}) collective-permute-start(bf16[768,256]{1,0:T(8,128)(2,1)S(1)} %get-tuple-element.26.refs_2_.refs_1_), channel_id=1, source_target_pairs={{0,1},{1,0},{2,3},{3,2},{4,5},{5,4},{6,7},{7,6},{8,9},{9,8},{10,11... | collective-permute-start | bytes 1179656 | tf_op jit(solution)/shard_map/ppermute | solution.py:319
  2.7 8.5 %collective-permute-start.1 = (bf16[64,1664]{1,0:T(8,128)(2,1)S(1)}, bf16[64,1664]{1,0:T(8,128)(2,1)S(1)}, u32[]{:S(2)}, u32[]{:S(2)}) collective-permute-start(bf16[64,1664]{1,0:T(8,128)(2,1)S(1)} %get-tuple-element.24.refs_0_), channel_id=1, source_target_pairs={{0,2},{4,0},{8,4},{12,8},{14,12},{10,14},{6,10},{2,6},{1,3},{5,1},... | collective-permute-start | bytes 638984 | tf_op jit(solution)/shard_map/ppermute | solution.py:27
  5.2 7.3 %collective-permute-start = (bf16[64,1664]{1,0:T(8,128)(2,1)S(1)}, bf16[64,1664]{1,0:T(8,128)(2,1)S(1)}, u32[]{:S(2)}, u32[]{:S(2)}) collective-permute-start(bf16[64,1664]{1,0:T(8,128)(2,1)S(1)} %get-tuple-element.24.refs_0_), channel_id=1, source_target_pairs={{0,4},{4,8},{8,12},{12,14},{14,10},{10,6},{6,2},{2,0},{1,5},{5,9},... | collective-permute-start | bytes 638984 | tf_op jit(solution)/shard_map/ppermute | solution.py:27
  7.8 6.8 %collective-permute-start.4 = (bf16[768,1280]{1,0:T(8,128)(2,1)S(1)}, bf16[768,1280]{1,0:T(8,128)(2,1)S(1)}, u32[]{:S(2)}, u32[]{:S(2)}) collective-permute-start(bf16[768,1280]{1,0:T(8,128)(2,1)S(1)} %get-tuple-element.28.refs_1_.refs_3_.refs_2_), channel_id=1, source_target_pairs={{0,1},{1,0},{2,3},{3,2},{4,5},{5,4},{6,7},{7,6},{8,9},{9,8},{10,11... | collective-permute-start | bytes 5898248 | tf_op jit(solution)/shard_map/ppermute | solution.py:319
  10.4 4.8 %collective-permute-start.5 = (bf16[768,1536]{1,0:T(8,128)(2,1)S(1)}, bf16[768,1536]{1,0:T(8,128)(2,1)S(1)}, u32[]{:S(2)}, u32[]{:S(2)}) collective-permute-start(bf16[768,1536]{1,0:T(8,128)(2,1)S(1)} %code.3.refs_2_.refs_4_.refs_3_), channel_id=1, source_target_pairs={{0,1},{1,0},{2,3},{3,2},{4,5},{5,4},{6,7},{7,6},{8,9},{9,8},{10,11... | collective-permute-start | bytes 7077896 | tf_op jit(solution)/shard_map/ppermute | solution.py:319
  12.6 6.5 %collective-permute-start.3 = (bf16[64,1664]{1,0:T(8,128)(2,1)S(1)}, bf16[64,1664]{1,0:T(8,128)(2,1)S(1)}, u32[]{:S(2)}, u32[]{:S(2)}) collective-permute-start(bf16[64,1664]{1,0:T(8,128)(2,1)S(1)} %collective-permute-done.refs_0_), channel_id=1, source_target_pairs={{0,4},{4,8},{8,12},{12,14},{14,10},{10,6},{6,2},{2,0},{1,5},{5,9},... | collective-permute-start | bytes 638984 | tf_op jit(solution)/shard_map/ppermute | solution.py:27
  12.9 7.3 %collective-permute-start.7 = (bf16[64,1664]{1,0:T(8,128)(2,1)S(1)}, bf16[64,1664]{1,0:T(8,128)(2,1)S(1)}, u32[]{:S(2)}, u32[]{:S(2)}) collective-permute-start(bf16[64,1664]{1,0:T(8,128)(2,1)S(1)} %collective-permute-done.1.refs_1_), channel_id=1, source_target_pairs={{0,2},{4,0},{8,4},{12,8},{14,12},{10,14},{6,10},{2,6},{1,3},{5,1},... | collective-permute-start | bytes 638984 | tf_op jit(solution)/shard_map/ppermute | solution.py:27
  19.1 6.6 %collective-permute-start.6 = (bf16[64,1792]{1,0:T(8,128)(2,1)S(1)}, bf16[64,1792]{1,0:T(8,128)(2,1)S(1)}, u32[]{:S(2)}, u32[]{:S(2)}) collective-permute-start(bf16[64,1792]{1,0:T(8,128)(2,1)S(1)} %attach.2), channel_id=1, source_target_pairs={{0,4},{4,8},{8,12},{12,14},{14,10},{10,6},{6,2},{2,0},{1,5},{5,9},... | collective-permute-start | bytes 688136 | tf_op jit(solution)/shard_map/ppermute | solution.py:27
  20.3 7.3 %collective-permute-start.8 = (bf16[64,1792]{1,0:T(8,128)(2,1)S(1)}, bf16[64,1792]{1,0:T(8,128)(2,1)S(1)}, u32[]{:S(2)}, u32[]{:S(2)}) collective-permute-start(bf16[64,1792]{1,0:T(8,128)(2,1)S(1)} %attach.3), channel_id=1, source_target_pairs={{0,2},{4,0},{8,4},{12,8},{14,12},{10,14},{6,10},{2,6},{1,3},{5,1},... | collective-permute-start | bytes 688136 | tf_op jit(solution)/shard_map/ppermute | solution.py:27
  22.8 10.2 %collective-permute-start.11 = (bf16[64,192]{1,0:T(8,128)(2,1)S(1)}, bf16[64,192]{1,0:T(8,128)(2,1)S(1)}, u32[]{:S(2)}, u32[]{:S(2)}) collective-permute-start(bf16[64,192]{1,0:T(8,128)(2,1)S(1)} %get-tuple-element.33), channel_id=1, source_target_pairs={{0,6},{4,2},{8,0},{12,4},{14,8},{10,12},{6,14},{2,10},{1,7},{5,3},... | collective-permute-start | bytes 73736 | tf_op jit(solution)/shard_map/ppermute | solution.py:27
  25.4 7.6 %collective-permute-start.12 = (bf16[64,192]{1,0:T(8,128)(2,1)S(1)}, bf16[64,192]{1,0:T(8,128)(2,1)S(1)}, u32[]{:S(2)}, u32[]{:S(2)}) collective-permute-start(bf16[64,192]{1,0:T(8,128)(2,1)S(1)} %get-tuple-element.36), channel_id=1, source_target_pairs={{0,8},{4,12},{8,14},{12,10},{14,6},{10,2},{6,0},{2,4},{1,9},{5,13}... | collective-permute-start | bytes 73736 | tf_op jit(solution)/shard_map/ppermute | solution.py:27
  25.7 7.2 %collective-permute-start.10 = (bf16[64,1792]{1,0:T(8,128)(2,1)S(1)}, bf16[64,1792]{1,0:T(8,128)(2,1)S(1)}, u32[]{:S(2)}, u32[]{:S(2)}) collective-permute-start(bf16[64,1792]{1,0:T(8,128)(2,1)S(1)} %collective-permute-done.6.refs_0_.refs_2_), channel_id=1, source_target_pairs={{0,4},{4,8},{8,12},{12,14},{14,10},{10,6},{6,2},{2,0},{1,5},{5,9},... | collective-permute-start | bytes 688136 | tf_op jit(solution)/shard_map/ppermute | solution.py:27
  29.1 10.4 %collective-permute-start.9 = (bf16[64,192]{1,0:T(8,128)(2,1)S(1)}, bf16[64,192]{1,0:T(8,128)(2,1)S(1)}, u32[]{:S(2)}, u32[]{:S(2)}) collective-permute-start(bf16[64,192]{1,0:T(8,128)(2,1)S(1)} %get-tuple-element.38), channel_id=1, source_target_pairs={{0,12},{4,14},{8,10},{12,6},{14,2},{10,0},{6,4},{2,8},{1,13},{5,15... | collective-permute-start | bytes 73736 | tf_op jit(solution)/shard_map/ppermute | solution.py:27
  31.9 7.5 %collective-permute-start.13 = (bf16[64,192]{1,0:T(8,128)(2,1)S(1)}, bf16[64,192]{1,0:T(8,128)(2,1)S(1)}, u32[]{:S(2)}, u32[]{:S(2)}) collective-permute-start(bf16[64,192]{1,0:T(8,128)(2,1)S(1)} %get-tuple-element.39), channel_id=1, source_target_pairs={{0,10},{4,6},{8,2},{12,0},{14,4},{10,8},{6,12},{2,14},{1,11},{5,7}... | collective-permute-start | bytes 73736 | tf_op jit(solution)/shard_map/ppermute | solution.py:27
  34.5 6.7 %collective-permute-start.14 = (bf16[64,192]{1,0:T(8,128)(2,1)S(1)}, bf16[64,192]{1,0:T(8,128)(2,1)S(1)}, u32[]{:S(2)}, u32[]{:S(2)}) collective-permute-start(bf16[64,192]{1,0:T(8,128)(2,1)S(1)} %hidden.9), channel_id=1, source_target_pairs={{0,14},{4,10},{8,6},{12,2},{14,0},{10,4},{6,8},{2,12},{1,15},{5,11... | collective-permute-start | bytes 73736 | tf_op jit(solution)/shard_map/ppermute | solution.py:27
